TPU v7x, 32 devices: a whole 2x2x4 slice. The times are simulated.
32 devices in a mesh: space: 2 (over y), vel: 16 (over z, x, core).
Axes of the slice: x: 2, y: 2, z: 4, core: 2. Of those that a mesh axis runs over, the one named last changes fastest.
Arguments:
- dist: float32 [256, 32768], P('space', 'vel'), as said below
- wall_temp: float32 [256], P('space'), may hold values from 0.6 to 1.5
- neighbours: int32 [6, 256], P(None, 'space'), may hold values from 0 to 255, as said below
- wall_mask: int32 [6, 256], P(None, 'space'), may hold values from 0 to 1, as said below
- face_rows: int32 [2, 2, 64], P('space'), may hold values from 0 to 127, as said below
Outputs:
- dist_out: float32 [256, 32768], P('space', 'vel')
Inputs may be any that keep to these rules, and one draw needn't show every extreme that they name: `dist`: strictly positive. Each block b holds the 2 x-planes b * 2 to (b + 1) * 2 - 1 of a periodic grid of 4 x 8 x 8 cells, its cells in some order; neighbours[k, c] is the cell across face k, periodic along x, and the cell itself across the channel's four side walls. `wall_mask`: all faces on the channel's four sides are walls, and x faces of solid screen elements, on both cells that share them. face_rows[b, 0, j] and face_rows[b, 1, j] are rows within block b, counted from 0, of its cells on its lowest and highest x-plane at the same position j across the channel, so the cell at face_rows[b, 1, j] has as +x neighbour the cell at face_rows[(b + 1) mod 2, 0, j] of the next block.
All inputs are finite; a program needn't handle non-finite values.
Results may differ from a plain program's by a relative error of at most 0.0003.
Values sent between devices are 32-bit elements; how exact they have to be, the bound alone decides.
No kernel may reach another device: no remote copies, remote signals or barrier semaphores. Data moves between devices by JAX's collectives and lax.ppermute only.
A program may use at most 64 MiB of HBM per device.

v0:
```python
import math

import jax
import jax.numpy as jnp
from jax import lax
from jax.sharding import PartitionSpec as P

NV = 32


LIMIT = 4.5
TIME_STEP = 0.05
BASELINE_SHEAR = 0.1
SHEAR_EXPONENT = 0.66
MOMENTUM_RATIO = 2.0 / 3.0


def padded(block, sides, width):
    for axis, dim in sides:
        count = lax.axis_size(axis)
        forward = [(i, i + 1) for i in range(count - 1)]
        forward.append((count - 1, 0))
        backward = [(target, source) for source, target in forward]
        low = lax.ppermute(
            lax.slice_in_dim(block, block.shape[dim] - width, None, axis=dim), axis, forward
        )
        high = lax.ppermute(lax.slice_in_dim(block, 0, width, axis=dim), axis, backward)
        block = jnp.concatenate([low, block, high], axis=dim)
    return block


def velocity_table(first_vel, vel_count):
    vel_index = first_vel + jnp.arange(vel_count, dtype=jnp.int32)
    spacing = 2.0 * LIMIT / NV

    def coordinate(slot):
        return -LIMIT + (slot.astype(jnp.float32) + 0.5) * spacing

    vel_x = coordinate(vel_index // NV % NV)
    vel_y = coordinate(vel_index // (NV * NV))
    vel_z = coordinate(vel_index % NV)
    return (vel_x, vel_y, vel_z)


def quad_weight():
    spacing = 2.0 * LIMIT / NV
    return spacing**3 * (2.0 * math.pi) ** (-1.5)


def normal_speeds(vel_x, vel_y, vel_z):
    return [-vel_x, vel_x, -vel_y, vel_y, -vel_z, vel_z]


def moment_table(vel_x, vel_y, vel_z, weight):
    speed_sq = vel_x * vel_x + vel_y * vel_y + vel_z * vel_z
    columns = [
        jnp.ones_like(vel_x),
        vel_x,
        vel_y,
        vel_z,
        vel_x * vel_x,
        vel_y * vel_y,
        vel_z * vel_z,
        vel_x * vel_y,
        vel_x * vel_z,
        vel_y * vel_z,
        vel_x * speed_sq,
        vel_y * speed_sq,
        vel_z * speed_sq,
    ]
    return weight * jnp.stack(columns, axis=1)


def reflect_table(speeds, weight):
    return weight * jnp.stack([jnp.maximum(normal_speed, 0.0) for normal_speed in speeds], axis=1)


def collide(current, moment_sums, vel_x, vel_y, vel_z):
    particle_count_per_volume = moment_sums[:, 0]
    flow_x = moment_sums[:, 1] / particle_count_per_volume
    flow_y = moment_sums[:, 2] / particle_count_per_volume
    flow_z = moment_sums[:, 3] / particle_count_per_volume
    press_xx = moment_sums[:, 4]
    press_yy = moment_sums[:, 5]
    press_zz = moment_sums[:, 6]
    press_xy = moment_sums[:, 7]
    press_xz = moment_sums[:, 8]
    press_yz = moment_sums[:, 9]
    internal_agitation = press_xx + press_yy + press_zz
    bulk_motion_norm = flow_x * flow_x + flow_y * flow_y + flow_z * flow_z
    site_kelvin = (internal_agitation / particle_count_per_volume - bulk_motion_norm) / 3.0
    heat_x = 0.5 * (
        moment_sums[:, 10]
        - 2.0 * (press_xx * flow_x + press_xy * flow_y + press_xz * flow_z)
        - flow_x * internal_agitation
        + 2.0 * particle_count_per_volume * flow_x * bulk_motion_norm
    )
    heat_y = 0.5 * (
        moment_sums[:, 11]
        - 2.0 * (press_xy * flow_x + press_yy * flow_y + press_yz * flow_z)
        - flow_y * internal_agitation
        + 2.0 * particle_count_per_volume * flow_y * bulk_motion_norm
    )
    heat_z = 0.5 * (
        moment_sums[:, 12]
        - 2.0 * (press_xz * flow_x + press_yz * flow_y + press_zz * flow_z)
        - flow_z * internal_agitation
        + 2.0 * particle_count_per_volume * flow_z * bulk_motion_norm
    )
    rel_x = vel_x[None, :] - flow_x[:, None]
    rel_y = vel_y[None, :] - flow_y[:, None]
    rel_z = vel_z[None, :] - flow_z[:, None]
    peculiar_motion_norm = rel_x * rel_x + rel_y * rel_y + rel_z * rel_z
    kelvin_vertical_array = site_kelvin[:, None]
    maxwellian_target = (particle_count_per_volume * site_kelvin ** (-1.5))[:, None] * jnp.exp(
        -peculiar_motion_norm / (2.0 * kelvin_vertical_array)
    )
    peculiar_conduction = (
        rel_x * heat_x[:, None] + rel_y * heat_y[:, None] + rel_z * heat_z[:, None]
    )
    conduction_scale = (1.0 - MOMENTUM_RATIO) / (5.0 * particle_count_per_volume * site_kelvin**2)
    kinetic_bgk_variant = maxwellian_target * (
        1.0
        + conduction_scale[:, None]
        * peculiar_conduction
        * (peculiar_motion_norm / kelvin_vertical_array - 5.0)
    )
    collision_rate_inverse_time = (
        particle_count_per_volume * site_kelvin ** (1.0 - SHEAR_EXPONENT) / BASELINE_SHEAR
    )
    return (kinetic_bgk_variant - current) * collision_rate_inverse_time[:, None]


def stream_term(own_rows, extended, index_list, wall_mask, wall_scale, wall_shape, speeds):
    stream_sum = jnp.zeros_like(own_rows)
    for direction in range(6):
        normal_speed = speeds[direction][None, :]
        beside = jnp.take(extended, index_list[direction], axis=0)
        wall_value = wall_scale[:, direction : direction + 1] * wall_shape
        inflow = jnp.where(wall_mask[direction][:, None] == 1, wall_value, beside)
        stream_sum = stream_sum - normal_speed * jnp.where(normal_speed > 0, own_rows, inflow)
    return stream_sum


def on_device(dist, wall_temp, neighbours, wall_mask, face_rows):
    cell_count, vel_count = dist.shape
    face_count = face_rows.shape[2]
    cell_start = lax.axis_index("space") * cell_count
    vel_x, vel_y, vel_z = velocity_table(lax.axis_index("vel") * vel_count, vel_count)
    weight = quad_weight()
    speeds = normal_speeds(vel_x, vel_y, vel_z)
    moments_tab = moment_table(vel_x, vel_y, vel_z, weight)
    reflect_tab = reflect_table(speeds, weight)
    low_rows = face_rows[0, 0]
    high_rows = face_rows[0, 1]
    counting = jnp.arange(face_count, dtype=jnp.int32)
    local_index = neighbours - cell_start
    index_list = [local_index[direction] for direction in range(6)]
    index_list[0] = index_list[0].at[low_rows].set(cell_count + counting)
    index_list[1] = index_list[1].at[high_rows].set(cell_count + face_count + counting)
    speed_sq = vel_x * vel_x + vel_y * vel_y + vel_z * vel_z
    wall_shape = jnp.exp(-speed_sq[None, :] / (2.0 * wall_temp[:, None]))
    spacing = 2.0 * LIMIT / NV
    axis_points = -LIMIT + (jnp.arange(NV, dtype=jnp.int32).astype(jnp.float32) + 0.5) * spacing
    profile = jnp.exp(-(axis_points * axis_points)[None, :] / (2.0 * wall_temp[:, None]))
    along_flux = jnp.sum(jnp.maximum(axis_points, 0.0)[None, :] * profile, axis=1)
    along_mass = jnp.sum(profile, axis=1)
    wall_norm = weight * along_flux * along_mass * along_mass

    def rate(current):
        low_face = jnp.take(current, low_rows, axis=0)
        high_face = jnp.take(current, high_rows, axis=0)
        padded_faces = padded(
            jnp.concatenate([low_face, high_face], axis=0), (("space", 0),), face_count
        )
        from_lower = padded_faces[:face_count]
        from_upper = padded_faces[3 * face_count :]
        extended = jnp.concatenate([current, from_lower, from_upper], axis=0)
        moment_sums = lax.psum(
            jnp.dot(current, moments_tab, precision=lax.Precision.HIGHEST), "vel"
        )
        outflow = lax.psum(jnp.dot(current, reflect_tab, precision=lax.Precision.HIGHEST), "vel")
        wall_scale = outflow / wall_norm[:, None]
        running = stream_term(
            current, extended, index_list, wall_mask, wall_scale, wall_shape, speeds
        )
        return running + collide(current, moment_sums, vel_x, vel_y, vel_z)

    current = dist
    slope_one = rate(current)
    middle = current + TIME_STEP * slope_one
    slope_two = rate(middle)
    current = current + 0.5 * TIME_STEP * (slope_one + slope_two)
    return current


def solution(mesh):
    return jax.shard_map(
        on_device,
        mesh=mesh,
        in_specs=(
            P("space", "vel"),
            P("space"),
            P(None, "space"),
            P(None, "space"),
            P("space", None, None),
        ),
        out_specs=P("space", "vel"),
        check_vma=False,
    )
```

profile of v0, /device:TPU:0, one launch (start us, length us, event | category | flops | bytes accessed | tf_op | source)
XLA Modules:
  0.0 199.2 jit_solution(7391289644962711111)
XLA Ops:
  0.0 0.8 compare_and_fusion.6
  0.8 0.0 copy-start
  0.8 2.3 %gather_fusion.1 = f32[64,2048]{1,0:T(8,128)S(1)} fusion(f32[128,2048]{1,0:T(8,128)} %param.9, s32[1024]{0:T(1024)S(1)} %pad_clamp_fusion.6), kind=kCustom, calls=%fused_computation.2.clone | custom fusion | bytes 1048832 | tf_op jit(solution)/shard_map/jit(_take)/gather | solution.py:171
  3.1 0.9 broadcast_select_fusion.2
  4.0 3.0 %collective-permute-start.1 = (f32[64,2048]{1,0:T(8,128)}, f32[64,2048]{1,0:T(8,128)}, u32[]{:S(2)}, u32[]{:S(2)}) collective-permute-start(f32[64,2048]{1,0:T(8,128)} %broadcast_select_fusion.2), channel_id=1, source_target_pairs={{16,0},{0,16},{17,1},{1,17},{18,2},{2,18},{19,3},{3,19},{20,4},{4,... | collective-permute-start | bytes 1572872 | tf_op jit(solution)/shard_map/ppermute | solution.py:27
  7.0 0.0 copy-start.3
  7.0 0.0 copy-start.4
  7.0 0.8 gather_fusion
  7.8 0.0 copy-start.8
  7.8 0.0 copy-start.5
  7.8 0.9 broadcast_select_fusion.3
  8.7 0.0 collective-permute-start
  8.8 0.8 scatter_fusion
  9.6 0.8 scatter_fusion.1
  10.4 0.2 fusion.140
  10.6 0.1 broadcast_maximum_fusion
  10.7 0.1 negate_maximum_fusion
  10.8 0.1 fusion.138
  11.0 0.1 fusion.142
  11.1 0.2 broadcast_maximum_fusion.2
  11.3 0.2 fusion.144
  11.5 0.1 multiply_add_fusion.1
  11.6 0.1 fusion.101
  11.8 0.2 stack.5
  12.0 0.9 convolution_bitcast_fusion
  12.9 0.1 stack.4
  13.0 0.9 convolution_bitcast_fusion.1
  13.9 0.1 multiply_reduce_fusion
  14.0 0.0 copy-start.6
  14.0 61.4 %all-reduce.1 = (f32[128,13]{0,1:T(8,128)S(1)}, f32[128,6]{0,1:T(8,128)S(1)}) all-reduce(f32[128,13]{0,1:T(8,128)S(1)} %convolution_bitcast_fusion, f32[128,6]{0,1:T(8,128)S(1)} %convolution_bitcast_fusion.1), channel_id=1, replica_groups=mesh['space'=2,'vel'=16] {'vel'}, use_global_device_ids=true, to_apply=%region_5.8 | all-reduce | flops 2432 | bytes 19456 | tf_op jit(solution)/shard_map/psum | solution.py:179
  75.4 0.6 multiply_bitcast_fusion.11
  76.1 0.6 multiply_bitcast_fusion.10
  76.7 0.6 multiply_bitcast_fusion.9
  77.3 0.1 constant_dynamic-update-slice_fusion.2
  77.4 0.0 collective-permute-done
  77.4 1.1 constant_dynamic-update-slice_fusion.1
  78.5 0.0 collective-permute-done.1
  78.5 1.1 constant_dynamic-update-slice_fusion
  79.6 1.9 gather_fusion.7
  81.5 1.9 gather_fusion.6
  83.4 1.9 gather_fusion.5
  85.3 1.9 gather_fusion.4
  87.3 1.9 gather_fusion.3
  89.2 2.0 gather_fusion.2
  91.2 6.9 %multiply_add_fusion = (f32[128,2048]{1,0:T(8,128)S(1)}, f32[128,2048]{1,0:T(8,128)}) fusion(f32[128,2048]{1,0:T(8,128)S(1)} %copy-done, f32[128]{0:T(128)} %get-tuple-element.85, f32[128]{0:T(128)} %get-tuple-element.84, f32[128]{0:T(128)} %get-tuple-element.43, f32[128]{0:T(128)} %get-tuple-element.44, f32[128]{0:T(128)} %get-tuple-element.42, ...), kind=kLoop, calls=%fused_computation.119 | loop fusion | flops 16777216 | bytes 9517568 | tf_op jit(solution)/shard_map/add | solution.py:191
  98.1 0.9 fusion.73
  99.1 0.9 fusion.78
  100.0 0.8 gather_fusion.9
  100.8 0.8 gather_fusion.8
  101.5 57.8 %all-reduce = (f32[128,13]{0,1:T(8,128)S(1)}, f32[128,6]{0,1:T(8,128)S(1)}) all-reduce(f32[128,13]{0,1:T(8,128)S(1)} %fusion.73, f32[128,6]{0,1:T(8,128)S(1)} %fusion.78), channel_id=1, replica_groups=mesh['space'=2,'vel'=16] {'vel'}, use_global_device_ids=true, to_apply=%region_7.10 | all-reduce | flops 2432 | bytes 19456 | tf_op jit(solution)/shard_map/psum | solution.py:179
  159.4 0.1 broadcast_select_fusion
  159.5 0.1 broadcast_select_fusion.1
  159.6 1.6 collective-permute-start.2
  161.2 0.5 collective-permute-start.3
  161.8 12.8 %collective-permute-done.2 = f32[64,2048]{1,0:T(8,128)S(1)} collective-permute-done((f32[64,2048]{1,0:T(8,128)S(1)}, f32[64,2048]{1,0:T(8,128)S(1)}, u32[]{:S(2)}, u32[]{:S(2)}) %collective-permute-start.2) | collective-permute-done | bytes 524320 | tf_op jit(solution)/shard_map/ppermute | solution.py:24
  174.5 5.7 %collective-permute-done.3 = f32[64,2048]{1,0:T(8,128)S(1)} collective-permute-done((f32[64,2048]{1,0:T(8,128)S(1)}, f32[64,2048]{1,0:T(8,128)S(1)}, u32[]{:S(2)}, u32[]{:S(2)}) %collective-permute-start.3) | collective-permute-done | bytes 524320 | tf_op jit(solution)/shard_map/ppermute | solution.py:27
  180.3 0.2 pad_maximum_fusion
  180.5 1.9 gather_fusion.15
  182.4 1.9 gather_fusion.14
  184.4 1.9 gather_fusion.13
  186.3 2.0 gather_fusion.12
  188.3 1.9 gather_fusion.11
  190.2 1.9 gather_fusion.10
  192.1 7.1 %fusion.30 = f32[128,2048]{1,0:T(8,128)} fusion(f32[128,2048]{1,0:T(8,128)S(1)} %copy-done, f32[128,2048]{1,0:T(8,128)} %get-tuple-element.20, f32[128,2048]{1,0:T(8,128)} %copy-done.1, f32[128,2048]{1,0:T(8,128)} %gather_fusion.15, f32[128,2048]{1,0:T(8,128)} %gather_fusion.14, f32[128,2048]{1,0:T(8,128)} %gather_fusion.13, f32[128,2048]{1,0:T(8,128)} %gather_fusion.12, ...), kind=kLoop, calls=%fused_computation.64 | loop fusion | flops 17039360 | bytes 10566144 | tf_op jit(solution)/shard_map/add | solution.py:193
  (45 shorter events, 0.4 us)
Async XLA Ops:
  0.8 6.2 %copy-start = (f32[128,2048]{1,0:T(8,128)S(1)}, f32[128,2048]{1,0:T(8,128)}, u32[]{:S(2)}) copy-start(f32[128,2048]{1,0:T(8,128)} %param.9) | copy-start | bytes 3145732
  4.0 74.5 %collective-permute-start.1 = (f32[64,2048]{1,0:T(8,128)}, f32[64,2048]{1,0:T(8,128)}, u32[]{:S(2)}, u32[]{:S(2)}) collective-permute-start(f32[64,2048]{1,0:T(8,128)} %broadcast_select_fusion.2), channel_id=1, source_target_pairs={{16,0},{0,16},{17,1},{1,17},{18,2},{2,18},{19,3},{3,19},{20,4},{4,... | collective-permute-start | bytes 1572872 | tf_op jit(solution)/shard_map/ppermute | solution.py:27
  7.0 1.7 copy-start.3
  7.0 1.7 copy-start.4
  7.8 4.0 %copy-start.8 = (f32[128]{0:T(128)S(1)}, f32[128]{0:T(128)}, u32[]{:S(2)}) copy-start(f32[128]{0:T(128)} %param.10) | copy-start | bytes 1540
  7.8 4.0 %copy-start.5 = (s32[6,128]{1,0:T(8,128)S(1)}, s32[6,128]{1,0:T(8,128)}, u32[]{:S(2)}) copy-start(s32[6,128]{1,0:T(8,128)} %param.12) | copy-start | bytes 9220
  8.7 68.7 %collective-permute-start = (f32[64,2048]{1,0:T(8,128)}, f32[64,2048]{1,0:T(8,128)}, u32[]{:S(2)}, u32[]{:S(2)}) collective-permute-start(f32[64,2048]{1,0:T(8,128)} %broadcast_select_fusion.3), channel_id=1, source_target_pairs={{0,16},{16,0},{1,17},{17,1},{2,18},{18,2},{3,19},{19,3},{4,20},{20... | collective-permute-start | bytes 1572872 | tf_op jit(solution)/shard_map/ppermute | solution.py:24
  14.0 61.4 %copy-start.6 = (f32[128]{0:T(128)}, f32[128]{0:T(128)S(1)}, u32[]{:S(2)}) copy-start(f32[128]{0:T(128)S(1)} %multiply_multiply_fusion) | copy-start | bytes 1540
  98.1 2.6 %copy-start.1 = (f32[128,2048]{1,0:T(8,128)}, f32[128,2048]{1,0:T(8,128)S(1)}, u32[]{:S(2)}) copy-start(f32[128,2048]{1,0:T(8,128)S(1)} %get-tuple-element.19) | copy-start | bytes 3145732
  100.8 58.6 %copy-start.7 = (f32[128]{0:T(128)S(1)}, f32[128]{0:T(128)}, u32[]{:S(2)}) copy-start(f32[128]{0:T(128)} %copy-done.6) | copy-start | bytes 1540
  159.4 20.9 %copy-start.2 = (f32[128,2048]{1,0:T(8,128)S(1)}, f32[128,2048]{1,0:T(8,128)}, u32[]{:S(2)}) copy-start(f32[128,2048]{1,0:T(8,128)} %copy-done.1) | copy-start | bytes 3145732
  159.6 14.9 %collective-permute-start.2 = (f32[64,2048]{1,0:T(8,128)S(1)}, f32[64,2048]{1,0:T(8,128)S(1)}, u32[]{:S(2)}, u32[]{:S(2)}) collective-permute-start(f32[64,2048]{1,0:T(8,128)S(1)} %broadcast_select_fusion.1), channel_id=1, source_target_pairs={{0,16},{16,0},{1,17},{17,1},{2,18},{18,2},{3,19},{19,3},{4,20},{20... | collective-permute-start | bytes 1572872 | tf_op jit(solution)/shard_map/ppermute | solution.py:24
  161.2 19.1 %collective-permute-start.3 = (f32[64,2048]{1,0:T(8,128)S(1)}, f32[64,2048]{1,0:T(8,128)S(1)}, u32[]{:S(2)}, u32[]{:S(2)}) collective-permute-start(f32[64,2048]{1,0:T(8,128)S(1)} %broadcast_select_fusion), channel_id=1, source_target_pairs={{16,0},{0,16},{17,1},{1,17},{18,2},{2,18},{19,3},{3,19},{20,4},{4,... | collective-permute-start | bytes 1572872 | tf_op jit(solution)/shard_map/ppermute | solution.py:27
where the time goes:
time: 199 us
  blocking collectives  119 us (60%)
  local copies, waits for them, and re-layouts  31.9 us (16%)
  other arithmetic  20.4 us (10%)
  waiting for transfers between devices  18.5 us (9%)
  starting transfers between devices  5.07 us (3%)
  matrix products  3.67 us (2%)
    psum x2, blocking collectives, rate(): lax.psum(jnp.dot(current, moments_tab, precision=lax.Precision.HIGHEST),...  119 us
    gather x12, local copies, waits for them, and re-layouts, stream_term(): beside = jnp.take(extended, index_list[direction], axis=0)  23.2 us
    ppermute x2, waiting for transfers between devices, padded(): lax.ppermute(lax.slice_in_dim(block, block.shape[dim] - width, None, axis...  12.8 us
    add x1, other arithmetic, on_device(): current = current + 0.5 * TIME_STEP * (slope_one + slope_two)  7.1 us
    add x1, other arithmetic, on_device(): middle = current + TIME_STEP * slope_one  6.93 us
    ppermute x2, waiting for transfers between devices, padded(): lax.ppermute(lax.slice_in_dim(block, 0, width, axis=dim), axis, backward)  5.72 us
  transfers between devices with their start and end apart: 4, of which 2 were waited for; matrix products, arithmetic and copies ran while one was open for 5% of the time, Pallas kernels for 0%

commit v1 on v0

v1 whole, which is shorter than its diff:
```python
import functools
import math

import jax
import jax.numpy as jnp
from jax import lax
from jax.experimental import pallas as pl
from jax.experimental.pallas import tpu as pltpu
from jax.sharding import PartitionSpec as P

NV = 32
LIMIT = 4.5
SPACING = 2.0 * LIMIT / NV
WEIGHT = SPACING**3 * (2.0 * math.pi) ** (-1.5)
TIME_STEP = 0.05
BASELINE_SHEAR = 0.1
SHEAR_EXPONENT = 0.66
MOMENTUM_RATIO = 2.0 / 3.0
PLANE = NV * NV
HALF = PLANE // 2
ROWS = 8
COLUMN_TILE = 256
SUMS = 16
F32 = jnp.float32
BF16 = jnp.bfloat16


def point(slot):
    return -LIMIT + (slot.astype(F32) + 0.5) * SPACING


def lane_table(first, start, width):
    lane = lax.broadcasted_iota(jnp.int32, (1, width), 1) + start
    vel = first + lane
    vel_x = point((lane >> 5) & (NV - 1))
    vel_y = point(vel >> 10)
    vel_z = point(lane & (NV - 1))
    return vel_x, vel_y, vel_z


def first_vel(width):
    return lax.axis_index("vel") * width


def split(value, count):
    pieces = []
    for _ in range(count - 1):
        piece = value.astype(BF16)
        pieces.append(piece)
        value = value - piece.astype(F32)
    pieces.append(value.astype(BF16))
    return pieces


def dot(left, right, dims=((1,), (0,))):
    return lax.dot_general(left, right, (dims, ((), ())), preferred_element_type=F32)


def sums_of(values, vel_x, vel_y, vel_z):
    speed_sq = vel_x * vel_x + vel_y * vel_y + vel_z * vel_z
    table = WEIGHT * jnp.concatenate(
        [
            jnp.ones_like(vel_x),
            vel_x * vel_x,
            vel_y * vel_y,
            vel_z * vel_z,
            vel_x * vel_y,
            vel_x * vel_z,
            vel_y * vel_z,
            vel_x * speed_sq,
            vel_y * speed_sq,
            vel_z * speed_sq,
            jnp.maximum(-vel_x, 0.0),
            jnp.maximum(vel_x, 0.0),
            jnp.maximum(-vel_y, 0.0),
            jnp.maximum(vel_y, 0.0),
            jnp.maximum(-vel_z, 0.0),
            jnp.maximum(vel_z, 0.0),
        ],
        axis=0,
    )
    tables = split(table, 3)
    pieces = split(values, 3)
    stacked = jnp.concatenate(tables, axis=0)
    total = None
    for order, piece in enumerate(pieces):
        part = dot(stacked[: (3 - order) * SUMS], piece, ((1,), (1,)))
        for at in range(3 - order):
            term = part[at * SUMS : (at + 1) * SUMS]
            total = term if total is None else total + term
    return total


def half_slices(width):
    low, high = [], []
    for plane in range(width // PLANE):
        low.append((plane * PLANE, plane * HALF))
        high.append((plane * PLANE + HALF, plane * HALF))
    return low, high


def start_kernel(rows_ref, dist_ref, send_ref, sums_ref):
    cells, width = dist_ref.shape
    count = cells // 2
    low, high = half_slices(width)

    def move(at, _):
        low_row = rows_ref[0, 0, at]
        high_row = rows_ref[0, 1, at]
        for source, target in high:
            send_ref[pl.ds(at, 1), target : target + HALF] = dist_ref[
                pl.ds(high_row, 1), source : source + HALF
            ]
        for source, target in low:
            send_ref[pl.ds(count + at, 1), target : target + HALF] = dist_ref[
                pl.ds(low_row, 1), source : source + HALF
            ]
        return 0

    lax.fori_loop(0, count, move, 0, unroll=4)
    vel_x, vel_y, vel_z = lane_table(first_vel(width), 0, width)
    sums_ref[...] = sums_of(dist_ref[...], vel_x, vel_y, vel_z)


def picks(near_ref, mask_ref, face, cell_start, cells):
    index = near_ref[face : face + 1, :] - cell_start
    hit = lax.broadcasted_iota(jnp.int32, (cells, cells), 0) == index
    open_face = mask_ref[face : face + 1, :] != 1
    return jnp.where(hit & open_face, 1.0, 0.0).astype(F32)


def stream_kernel(near_ref, mask_ref, dist_ref, out_ref):
    stream_body(near_ref, mask_ref, dist_ref, None, out_ref)


def stream_last_kernel(near_ref, mask_ref, dist_ref, middle_ref, out_ref):
    stream_body(near_ref, mask_ref, middle_ref, dist_ref, out_ref)


def stream_body(near_ref, mask_ref, value_ref, dist_ref, out_ref):
    cells, width = value_ref.shape
    first = first_vel(width)
    cell_start = lax.axis_index("space") * cells
    upward = first >= (NV // 2) * PLANE
    faces = [picks(near_ref, mask_ref, face, cell_start, cells) for face in range(6)]
    along_y = jnp.where(upward, faces[2], faces[3])
    chosen = []
    for face in (faces[0], faces[1], along_y, faces[4], faces[5]):
        flipped = face.T.astype(BF16)
        chosen.append(jnp.concatenate([flipped, flipped], axis=1))
    rest = jnp.concatenate(chosen[2:], axis=0)
    for start in range(0, width, COLUMN_TILE):
        side = chosen[0] if start % PLANE >= HALF else chosen[1]
        vel_x, vel_y, vel_z = lane_table(first, start, COLUMN_TILE)
        values = value_ref[:, start : start + COLUMN_TILE]
        pieces = jnp.concatenate(split(values, 2), axis=0)
        moved = dot(jnp.concatenate([side, rest], axis=0), pieces)
        speed_x, speed_y, speed_z = jnp.abs(vel_x), jnp.abs(vel_y), jnp.abs(vel_z)
        from_z = jnp.where(vel_z > 0, moved[2 * cells : 3 * cells], moved[3 * cells :])
        stream = (
            speed_x * moved[:cells]
            + speed_y * moved[cells : 2 * cells]
            + speed_z * from_z
            - (speed_x + speed_y + speed_z) * values
        )
        if dist_ref is None:
            out_ref[:, start : start + COLUMN_TILE] = stream
        else:
            out_ref[:, start : start + COLUMN_TILE] = (
                0.5 * (dist_ref[:, start : start + COLUMN_TILE] + values)
                + (0.5 * TIME_STEP) * stream
            )


def columns_of(sums, wall_temp, mask, upward):
    count = sums[0:1]
    inv_count = 1.0 / count
    flow_x = (sums[11:12] - sums[10:11]) * inv_count
    flow_y = (sums[13:14] - sums[12:13]) * inv_count
    flow_z = (sums[15:16] - sums[14:15]) * inv_count
    p_xx, p_yy, p_zz, p_xy, p_xz, p_yz = (sums[at : at + 1] for at in range(1, 7))
    energy = p_xx + p_yy + p_zz
    flow_sq = flow_x * flow_x + flow_y * flow_y + flow_z * flow_z
    temp = (energy * inv_count - flow_sq) / 3.0
    inv_temp = 1.0 / temp

    def heat(third, flow, press):
        return 0.5 * (
            third
            - 2.0 * (press[0] * flow_x + press[1] * flow_y + press[2] * flow_z)
            - flow * energy
            + 2.0 * count * flow * flow_sq
        )

    scale = ((1.0 - MOMENTUM_RATIO) / 5.0) * inv_count * inv_temp * inv_temp
    heat_x = scale * heat(sums[7:8], flow_x, (p_xx, p_xy, p_xz))
    heat_y = scale * heat(sums[8:9], flow_y, (p_xy, p_yy, p_yz))
    heat_z = scale * heat(sums[9:10], flow_z, (p_xz, p_yz, p_zz))
    peak = count * inv_temp * lax.rsqrt(temp)
    rate = count * jnp.exp((1.0 - SHEAR_EXPONENT) * jnp.log(temp)) * (1.0 / BASELINE_SHEAR)
    axis_point = point(lax.broadcasted_iota(jnp.int32, (NV, 1), 0))
    cooling = -0.5 / wall_temp
    profile = jnp.exp(axis_point * axis_point * cooling)
    mass = jnp.sum(profile, axis=0, keepdims=True)
    flux = jnp.sum(jnp.maximum(axis_point, 0.0) * profile, axis=0, keepdims=True)
    inv_norm = 1.0 / (WEIGHT * flux * mass * mass)
    back = [
        jnp.where(mask[face : face + 1] == 1, sums[10 + face : 11 + face] * inv_norm, 0.0)
        for face in range(6)
    ]
    rows = [
        flow_x,
        flow_y,
        flow_z,
        inv_temp,
        heat_x,
        heat_y,
        heat_z,
        peak,
        rate,
        cooling,
        back[0],
        back[1],
        jnp.where(upward, back[2], back[3]),
        back[4],
        back[5],
    ]
    cells = count.shape[1]
    rows.append(jnp.zeros((128 - len(rows), cells), F32))
    return jnp.concatenate(rows, axis=0).T


def local_rate(columns, values, vel_x, vel_y, vel_z):
    def column(at):
        return columns[:, at : at + 1]

    rel_x = vel_x - column(0)
    rel_y = vel_y - column(1)
    rel_z = vel_z - column(2)
    ratio = (rel_x * rel_x + rel_y * rel_y + rel_z * rel_z) * column(3)
    conduction = rel_x * column(4) + rel_y * column(5) + rel_z * column(6)
    target = column(7) * jnp.exp(-0.5 * ratio) * (1.0 + conduction * (ratio - 5.0))
    speed_sq = vel_x * vel_x + vel_y * vel_y + vel_z * vel_z
    shape = jnp.exp(speed_sq * column(9))
    back = (
        jnp.maximum(vel_x, 0.0) * column(10)
        + jnp.maximum(-vel_x, 0.0) * column(11)
        + jnp.abs(vel_y) * column(12)
        + jnp.maximum(vel_z, 0.0) * column(13)
        + jnp.maximum(-vel_z, 0.0) * column(14)
    )
    return (target - values) * column(8) + shape * back


def middle_kernel(
    rows_ref, temp_ref, mask_ref, sums_ref, dist_ref, stream_ref, out_ref, send_ref, columns_ref
):
    cells, width = dist_ref.shape
    count = cells // 2
    first = first_vel(width)
    low, high = half_slices(width)
    upward = first >= (NV // 2) * PLANE
    columns_ref[...] = columns_of(sums_ref[...], temp_ref[...], mask_ref[...], upward)

    def group(at, _):
        rows = pl.ds(pl.multiple_of(at * ROWS, ROWS), ROWS)
        columns = columns_ref[rows, :]
        vel_x, vel_y, vel_z = lane_table(first, 0, width)
        values = dist_ref[rows, :]
        rate = stream_ref[rows, :] + local_rate(columns, values, vel_x, vel_y, vel_z)
        out_ref[rows, :] = values + TIME_STEP * rate
        return 0

    lax.fori_loop(0, cells // ROWS, group, 0)

    def move(at, _):
        low_row = rows_ref[0, 0, at]
        high_row = rows_ref[0, 1, at]
        for source, target in high:
            send_ref[pl.ds(at, 1), target : target + HALF] = out_ref[
                pl.ds(high_row, 1), source : source + HALF
            ]
        for source, target in low:
            send_ref[pl.ds(count + at, 1), target : target + HALF] = out_ref[
                pl.ds(low_row, 1), source : source + HALF
            ]
        return 0

    lax.fori_loop(0, count, move, 0, unroll=4)


def halo_picks(face_ref, mask_ref, cells):
    count = cells // 2
    mask = jnp.concatenate(
        [mask_ref[...].astype(F32), jnp.zeros((128 - mask_ref.shape[0], cells), F32)], axis=0
    ).T
    row = lax.broadcasted_iota(jnp.int32, (cells, count), 0)
    sides = []
    for face in (1, 0):
        hit = (row == face_ref[0, face : face + 1, :]) & (mask[:, face : face + 1] != 1.0)
        side = jnp.where(hit, 1.0, 0.0).astype(BF16)
        sides.append(jnp.concatenate([side, side], axis=1))
    return sides


def halo_part(halo_refs, side, start, count):
    lanes = slice(start, start + COLUMN_TILE)
    if len(halo_refs) == 1:
        rows = halo_refs[0][(1 - side) * count : (2 - side) * count, lanes]
    else:
        rows = halo_refs[1 - side][:, lanes]
    return jnp.concatenate(split(rows, 2), axis=0)


def join_kernel(face_ref, mask_ref, part_ref, *refs):
    halo_refs, (out_ref, sums_ref) = refs[:-2], refs[-2:]
    cells, width = part_ref.shape
    count = cells // 2
    sides = halo_picks(face_ref, mask_ref, cells)
    first = first_vel(width)
    for side, ranges in enumerate(half_slices(width)):
        for source, target in ranges:
            for step in range(0, HALF, COLUMN_TILE):
                lanes = slice(source + step, source + step + COLUMN_TILE)
                vel_x, _, _ = lane_table(first, source + step, COLUMN_TILE)
                halo = dot(sides[side], halo_part(halo_refs, side, target + step, count))
                out_ref[:, lanes] = part_ref[:, lanes] + (TIME_STEP * jnp.abs(vel_x)) * halo
    vel_x, vel_y, vel_z = lane_table(first, 0, width)
    sums_ref[...] = sums_of(out_ref[...], vel_x, vel_y, vel_z)


def last_kernel(face_ref, temp_ref, mask_ref, sums_ref, middle_ref, part_ref, *refs):
    halo_refs, (out_ref, columns_ref) = refs[:-2], refs[-2:]
    cells, width = part_ref.shape
    count = cells // 2
    first = first_vel(width)
    upward = first >= (NV // 2) * PLANE
    columns_ref[...] = columns_of(sums_ref[...], temp_ref[...], mask_ref[...], upward)

    def group(at, _):
        rows = pl.ds(pl.multiple_of(at * ROWS, ROWS), ROWS)
        columns = columns_ref[rows, :]
        vel_x, vel_y, vel_z = lane_table(first, 0, width)
        rate = local_rate(columns, middle_ref[rows, :], vel_x, vel_y, vel_z)
        out_ref[rows, :] = part_ref[rows, :] + (0.5 * TIME_STEP) * rate
        return 0

    lax.fori_loop(0, cells // ROWS, group, 0)
    sides = halo_picks(face_ref, mask_ref, cells)
    for side, ranges in enumerate(half_slices(width)):
        for source, target in ranges:
            for step in range(0, HALF, COLUMN_TILE):
                lanes = slice(source + step, source + step + COLUMN_TILE)
                vel_x, _, _ = lane_table(first, source + step, COLUMN_TILE)
                halo = dot(sides[side], halo_part(halo_refs, side, target + step, count))
                out_ref[:, lanes] = out_ref[:, lanes] + (0.5 * TIME_STEP * jnp.abs(vel_x)) * halo


def call(kernel, outs, scalars, arrays, scratch=(), flops=0):
    specs = [pl.BlockSpec(memory_space=pltpu.SMEM)] * len(scalars)
    specs += [pl.BlockSpec(memory_space=pltpu.VMEM)] * len(arrays)
    size = sum(math.prod(array.shape) * 4 for array in arrays)
    return pl.pallas_call(
        kernel,
        out_shape=[jax.ShapeDtypeStruct(shape, F32) for shape in outs],
        in_specs=specs,
        out_specs=[pl.BlockSpec(memory_space=pltpu.VMEM)] * len(outs),
        scratch_shapes=list(scratch),
        compiler_params=pltpu.CompilerParams(vmem_limit_bytes=40 * 2**20),
        cost_estimate=pl.CostEstimate(flops=flops, bytes_accessed=size, transcendentals=0),
    )(*scalars, *arrays)


def total(value):
    count = lax.axis_size("vel")
    step = 1
    while step < count:
        value = value + lax.ppermute(value, "vel", [(i, i ^ step) for i in range(count)])
        step *= 2
    return value


def exchange(send):
    count = lax.axis_size("space")
    forward = [(i, (i + 1) % count) for i in range(count)]
    backward = [(target, source) for source, target in forward]
    if count == 2:
        return [lax.ppermute(send, "space", forward)]
    half = send.shape[0] // 2
    return [
        lax.ppermute(send[:half], "space", forward),
        lax.ppermute(send[half:], "space", backward),
    ]


def on_device(dist, wall_temp, neighbours, wall_mask, face_rows):
    cells, width = dist.shape
    temp = wall_temp[None, :]
    whole, sums, send = (cells, width), (SUMS, cells), (cells, width // 2)
    column_scratch = [pltpu.VMEM((cells, 128), F32)]

    sent, own_sums = call(start_kernel, [send, sums], [face_rows], [dist])
    halo = exchange(sent)
    (stream,) = call(stream_kernel, [whole], [], [neighbours, wall_mask, dist])
    sums_one = total(own_sums)
    part, sent = call(
        middle_kernel,
        [whole, send],
        [face_rows],
        [temp, wall_mask, sums_one, dist, stream],
        column_scratch,
    )
    halo_two = exchange(sent)
    middle, own_sums = call(join_kernel, [whole, sums], [], [face_rows, wall_mask, part, *halo])
    (part,) = call(stream_last_kernel, [whole], [], [neighbours, wall_mask, dist, middle])
    sums_two = total(own_sums)
    (result,) = call(
        last_kernel,
        [whole],
        [],
        [face_rows, temp, wall_mask, sums_two, middle, part, *halo_two],
        column_scratch,
    )
    return result


def solution(mesh):
    return jax.shard_map(
        on_device,
        mesh=mesh,
        in_specs=(
            P("space", "vel"),
            P("space"),
            P(None, "space"),
            P(None, "space"),
            P("space", None, None),
        ),
        out_specs=P("space", "vel"),
        check_vma=False,
    )
```

time: 199 us -> 43.6 us (0.22)
  blocking collectives: 119 us -> 0 us
  local copies, waits for them, and re-layouts: 31.9 us -> 2.57 us
  other arithmetic: 20.4 us -> 0.03 us
  Pallas kernels: 0 us -> 13.3 us
  starting transfers between devices: 5.07 us -> 15.6 us
  waiting for transfers between devices: 18.5 us -> 11.8 us
  matrix products: 3.67 us -> 0 us
    psum x2 -> x0, blocking collectives: 119 us -> none  [rate(): lax.psum(jnp.dot(current, moments_tab, precision=lax.Precision.HIGHEST),...]
    gather x16 -> x0, local copies, waits for them, and re-layouts: 27.8 us -> none  [the longest x12 23.2 us: stream_term(): beside = jnp.take(extended, index_list[direction], axis=0)]
    add x8, other arithmetic: 14.3 us -> 0.03 us  [total(): value + lax.ppermute(value, 'vel', [(i, i ^ step) for i in range(count)])]
    pallas_call x0 -> x6, Pallas kernels: none -> 13.3 us  [call(): pl.pallas_call(kernel, out_shape=[jax.ShapeDtypeStruct(shape, F32) for sh...]
    ppermute x4 -> x10, starting transfers between devices: 5.07 us -> 15.6 us  [the longest x8 11.8 us: total(): lax.ppermute(value, 'vel', [(i, i ^ step) for i in range(count)])]
    ppermute x4 -> x10, waiting for transfers between devices: 18.5 us -> 11.8 us  [the longest x8 11.8 us: total(): lax.ppermute(value, 'vel', [(i, i ^ step) for i in range(count)])]
    dot_general x4 -> x0, matrix products: 3.67 us -> none  [the longest x2 1.84 us: rate(): jnp.dot(current, reflect_tab, precision=lax.Precision.HIGHEST)]
    select_n x7 -> x0, other arithmetic: 2.02 us -> none  [the longest x2 1 us: rate(): low_face = jnp.take(current, low_rows, axis=0)]
  transfers between devices with their start and end apart: 4 -> 10, of which waited for: 2 -> 7; matrix products, arithmetic and copies ran while one was open for 5% -> 0% of each run, Pallas kernels for 0% -> 16%
where the time goes in v1:
time: 43.6 us; the launch traced here: 43.4 us
  starting transfers between devices  15.6 us (36%)
  Pallas kernels  13.3 us (31%)
  waiting for transfers between devices  11.8 us (27%)
  local copies, waits for them, and re-layouts  2.57 us (6%)
    pallas_call x6, Pallas kernels, call(): pl.pallas_call(kernel, out_shape=[jax.ShapeDtypeStruct(shape, F32) for sh...  13.3 us
    ppermute x8, starting transfers between devices, total(): lax.ppermute(value, 'vel', [(i, i ^ step) for i in range(count)])  11.8 us
    ppermute x8, waiting for transfers between devices, total(): lax.ppermute(value, 'vel', [(i, i ^ step) for i in range(count)])  11.8 us
    ppermute x2, starting transfers between devices, exchange(): return [lax.ppermute(send, 'space', forward)]  3.75 us
    unnamed x12, local copies, waits for them, and re-layouts  2.57 us
  transfers between devices with their start and end apart: 10, of which 7 were waited for; matrix products, arithmetic and copies ran while one was open for 0% of the time, Pallas kernels for 16%

profile of v1, /device:TPU:0, one launch (start us, length us, event | category | flops | bytes accessed | tf_op | source)
XLA Modules:
  0.0 43.4 jit_solution(10365460869409309462)
XLA Ops:
  0.0 0.0 copy-start
  0.0 1.2 %copy-done = f32[128,2048]{1,0:T(8,128)S(1)} copy-done((f32[128,2048]{1,0:T(8,128)S(1)}, f32[128,2048]{1,0:T(8,128)}, u32[]{:S(2)}) %copy-start) | copy-done | bytes 1048600
  1.2 0.0 copy-start.4
  1.2 0.7 %copy-done.4 = s32[1,2,64]{2,1,0:T(2,128)S(1)} copy-done((s32[1,2,64]{2,1,0:T(2,128)S(1)}, s32[1,2,64]{2,1,0:T(2,128)}, u32[]{:S(2)}) %copy-start.4) | copy-done | bytes 536
  1.9 0.0 copy-start.1
  1.9 1.7 %shard_map.55 = (f32[128,1024]{1,0:T(8,128)S(1)}, f32[16,128]{1,0:T(8,128)S(1)}) custom-call(s32[1,2,64]{2,1,0:T(2,128)S(1)} %copy-done.4, f32[128,2048]{1,0:T(8,128)S(1)} %copy-done), custom_call_target="tpu_custom_call" | custom-call | bytes 1048576 | tf_op jit(solution)/shard_map/pallas_call | solution.py:363
  3.6 0.5 %collective-permute-start = (f32[16,128]{1,0:T(8,128)S(1)}, f32[16,128]{1,0:T(8,128)S(1)}, u32[]{:S(2)}, u32[]{:S(2)}) collective-permute-start(f32[16,128]{1,0:T(8,128)S(1)} %get-tuple-element.11), channel_id=1, source_target_pairs={{0,1},{1,0},{2,3},{3,2},{4,5},{5,4},{6,7},{7,6},{8,9},{9,8},{10,11... | collective-permute-start | bytes 24584 | tf_op jit(solution)/shard_map/ppermute | solution.py:378
  4.1 2.6 %collective-permute-start.4 = (f32[128,1024]{1,0:T(8,128)S(1)}, f32[128,1024]{1,0:T(8,128)S(1)}, u32[]{:S(2)}, u32[]{:S(2)}) collective-permute-start(f32[128,1024]{1,0:T(8,128)S(1)} %get-tuple-element.13), channel_id=1, source_target_pairs={{0,16},{16,0},{1,17},{17,1},{2,18},{18,2},{3,19},{19,3},{4,20},{20... | collective-permute-start | bytes 1572872 | tf_op jit(solution)/shard_map/ppermute | solution.py:388
  6.7 0.0 collective-permute-done
  6.7 1.5 %collective-permute-start.1 = (f32[16,128]{1,0:T(8,128)S(1)}, f32[16,128]{1,0:T(8,128)S(1)}, u32[]{:S(2)}, u32[]{:S(2)}) collective-permute-start(f32[16,128]{1,0:T(8,128)S(1)} %add.24), channel_id=1, source_target_pairs={{0,2},{1,3},{2,0},{3,1},{4,6},{5,7},{6,4},{7,5},{8,10},{9,11},{10,... | collective-permute-start | bytes 24584 | tf_op jit(solution)/shard_map/ppermute | solution.py:378
  8.2 2.2 %collective-permute-done.1 = f32[16,128]{1,0:T(8,128)S(1)} collective-permute-done((f32[16,128]{1,0:T(8,128)S(1)}, f32[16,128]{1,0:T(8,128)S(1)}, u32[]{:S(2)}, u32[]{:S(2)}) %collective-permute-start.1) | collective-permute-done | bytes 8224 | tf_op jit(solution)/shard_map/ppermute | solution.py:378
  10.3 0.0 copy-start.2
  10.3 0.0 copy-start.3
  10.3 1.6 %collective-permute-start.2 = (f32[16,128]{1,0:T(8,128)S(1)}, f32[16,128]{1,0:T(8,128)S(1)}, u32[]{:S(2)}, u32[]{:S(2)}) collective-permute-start(f32[16,128]{1,0:T(8,128)S(1)} %add.25), channel_id=1, source_target_pairs={{0,4},{1,5},{2,6},{3,7},{4,0},{5,1},{6,2},{7,3},{8,12},{9,13},{10,... | collective-permute-start | bytes 24584 | tf_op jit(solution)/shard_map/ppermute | solution.py:378
  12.0 2.1 %collective-permute-done.2 = f32[16,128]{1,0:T(8,128)S(1)} collective-permute-done((f32[16,128]{1,0:T(8,128)S(1)}, f32[16,128]{1,0:T(8,128)S(1)}, u32[]{:S(2)}, u32[]{:S(2)}) %collective-permute-start.2) | collective-permute-done | bytes 8224 | tf_op jit(solution)/shard_map/ppermute | solution.py:378
  14.0 2.6 %collective-permute-start.3 = (f32[16,128]{1,0:T(8,128)S(1)}, f32[16,128]{1,0:T(8,128)S(1)}, u32[]{:S(2)}, u32[]{:S(2)}) collective-permute-start(f32[16,128]{1,0:T(8,128)S(1)} %add.26), channel_id=1, source_target_pairs={{0,8},{1,9},{2,10},{3,11},{4,12},{5,13},{6,14},{7,15},{8,0},{9,1},... | collective-permute-start | bytes 24584 | tf_op jit(solution)/shard_map/ppermute | solution.py:378
  16.6 0.0 copy-done.1
  16.6 0.0 copy-done.2
  16.6 0.0 copy-done.3
  16.6 0.8 %shard_map.56.stream_ref = f32[128,2048]{1,0:T(8,128)S(1)} custom-call(s32[6,128]{1,0:T(8,128)S(1)} %copy-done.3, s32[6,128]{1,0:T(8,128)S(1)} %copy-done.2, f32[128,2048]{1,0:T(8,128)S(1)} %copy-done.1), custom_call_target="tpu_custom_call" | custom-call | bytes 1054720 | tf_op jit(solution)/shard_map/pallas_call | solution.py:363
  17.5 1.1 %collective-permute-done.3 = f32[16,128]{1,0:T(8,128)S(1)} collective-permute-done((f32[16,128]{1,0:T(8,128)S(1)}, f32[16,128]{1,0:T(8,128)S(1)}, u32[]{:S(2)}, u32[]{:S(2)}) %collective-permute-start.3) | collective-permute-done | bytes 8224 | tf_op jit(solution)/shard_map/ppermute | solution.py:378
  18.6 0.0 copy-start.5
  18.6 0.7 %copy-done.5 = f32[128]{0:T(128)S(1)} copy-done((f32[128]{0:T(128)S(1)}, f32[128]{0:T(128)}, u32[]{:S(2)}) %copy-start.5) | copy-done | bytes 536
  19.3 4.3 %shard_map.57 = (f32[128,2048]{1,0:T(8,128)S(1)}, f32[128,1024]{1,0:T(8,128)S(1)}) custom-call(s32[1,2,64]{2,1,0:T(2,128)S(1)} %copy-done.4, f32[1,128]{1,0:T(1,128)S(1)} %bitcast.1, s32[6,128]{1,0:T(8,128)S(1)} %copy-done.2, f32[16,128]{1,0:T(8,128)S(1)} %add.27.sums_ref, f32[128,2048]{1,0:T(8,128)S(1)} %copy-done.1, f32[128,2048]{1,0:T(8,128)S(1)} %shard_map.56.stream_ref), custom_call_target="tpu_custom_call" | custom-call | bytes 2108928 | tf_op jit(solution)/shard_map/pallas_call | solution.py:363
  23.5 1.2 %collective-permute-start.9 = (f32[128,1024]{1,0:T(8,128)S(1)}, f32[128,1024]{1,0:T(8,128)S(1)}, u32[]{:S(2)}, u32[]{:S(2)}) collective-permute-start(f32[128,1024]{1,0:T(8,128)S(1)} %get-tuple-element.16), channel_id=1, source_target_pairs={{0,16},{16,0},{1,17},{17,1},{2,18},{18,2},{3,19},{19,3},{4,20},{20... | collective-permute-start | bytes 1572872 | tf_op jit(solution)/shard_map/ppermute | solution.py:388
  24.7 0.0 collective-permute-done.4.refs_0_
  24.7 1.0 %shard_map.58 = (f32[128,2048]{1,0:T(8,128)S(1)}, f32[16,128]{1,0:T(8,128)S(1)}) custom-call(s32[1,2,64]{2,1,0:T(2,128)S(1)} %copy-done.4, s32[6,128]{1,0:T(8,128)S(1)} %copy-done.2, f32[128,2048]{1,0:T(8,128)S(1)} %get-tuple-element.12.part_ref, f32[128,1024]{1,0:T(8,128)S(1)} %collective-permute-done.4.refs_0_), custom_call_target="tpu_custom_call" | custom-call | bytes 1576448 | tf_op jit(solution)/shard_map/pallas_call | solution.py:363
  25.8 0.0 collective-permute-start.5
  25.8 1.2 %collective-permute-done.5 = f32[16,128]{1,0:T(8,128)S(1)} collective-permute-done((f32[16,128]{1,0:T(8,128)S(1)}, f32[16,128]{1,0:T(8,128)S(1)}, u32[]{:S(2)}, u32[]{:S(2)}) %collective-permute-start.5) | collective-permute-done | bytes 8224 | tf_op jit(solution)/shard_map/ppermute | solution.py:378
  27.0 1.5 %collective-permute-start.6 = (f32[16,128]{1,0:T(8,128)S(1)}, f32[16,128]{1,0:T(8,128)S(1)}, u32[]{:S(2)}, u32[]{:S(2)}) collective-permute-start(f32[16,128]{1,0:T(8,128)S(1)} %add.28), channel_id=1, source_target_pairs={{0,2},{1,3},{2,0},{3,1},{4,6},{5,7},{6,4},{7,5},{8,10},{9,11},{10,... | collective-permute-start | bytes 24584 | tf_op jit(solution)/shard_map/ppermute | solution.py:378
  28.4 2.2 %collective-permute-done.6 = f32[16,128]{1,0:T(8,128)S(1)} collective-permute-done((f32[16,128]{1,0:T(8,128)S(1)}, f32[16,128]{1,0:T(8,128)S(1)}, u32[]{:S(2)}, u32[]{:S(2)}) %collective-permute-start.6) | collective-permute-done | bytes 8224 | tf_op jit(solution)/shard_map/ppermute | solution.py:378
  30.6 1.6 %collective-permute-start.7 = (f32[16,128]{1,0:T(8,128)S(1)}, f32[16,128]{1,0:T(8,128)S(1)}, u32[]{:S(2)}, u32[]{:S(2)}) collective-permute-start(f32[16,128]{1,0:T(8,128)S(1)} %add.29), channel_id=1, source_target_pairs={{0,4},{1,5},{2,6},{3,7},{4,0},{5,1},{6,2},{7,3},{8,12},{9,13},{10,... | collective-permute-start | bytes 24584 | tf_op jit(solution)/shard_map/ppermute | solution.py:378
  32.2 2.1 %collective-permute-done.7 = f32[16,128]{1,0:T(8,128)S(1)} collective-permute-done((f32[16,128]{1,0:T(8,128)S(1)}, f32[16,128]{1,0:T(8,128)S(1)}, u32[]{:S(2)}, u32[]{:S(2)}) %collective-permute-start.7) | collective-permute-done | bytes 8224 | tf_op jit(solution)/shard_map/ppermute | solution.py:378
  34.3 2.6 %collective-permute-start.8 = (f32[16,128]{1,0:T(8,128)S(1)}, f32[16,128]{1,0:T(8,128)S(1)}, u32[]{:S(2)}, u32[]{:S(2)}) collective-permute-start(f32[16,128]{1,0:T(8,128)S(1)} %add.30), channel_id=1, source_target_pairs={{0,8},{1,9},{2,10},{3,11},{4,12},{5,13},{6,14},{7,15},{8,0},{9,1},... | collective-permute-start | bytes 24584 | tf_op jit(solution)/shard_map/ppermute | solution.py:378
  36.9 0.9 %shard_map.59.part_ref = f32[128,2048]{1,0:T(8,128)S(1)} custom-call(s32[6,128]{1,0:T(8,128)S(1)} %copy-done.3, s32[6,128]{1,0:T(8,128)S(1)} %copy-done.2, f32[128,2048]{1,0:T(8,128)S(1)} %copy-done.1, f32[128,2048]{1,0:T(8,128)S(1)} %get-tuple-element.15.middle_ref), custom_call_target="tpu_custom_call" | custom-call | bytes 2103296 | tf_op jit(solution)/shard_map/pallas_call | solution.py:363
  37.8 1.0 %collective-permute-done.8 = f32[16,128]{1,0:T(8,128)S(1)} collective-permute-done((f32[16,128]{1,0:T(8,128)S(1)}, f32[16,128]{1,0:T(8,128)S(1)}, u32[]{:S(2)}, u32[]{:S(2)}) %collective-permute-start.8) | collective-permute-done | bytes 8224 | tf_op jit(solution)/shard_map/ppermute | solution.py:378
  38.8 0.0 collective-permute-done.9.refs_0_
  38.8 4.6 %shard_map.60 = f32[128,2048]{1,0:T(8,128)} custom-call(s32[1,2,64]{2,1,0:T(2,128)S(1)} %copy-done.4, f32[1,128]{1,0:T(1,128)S(1)} %bitcast.2, s32[6,128]{1,0:T(8,128)S(1)} %copy-done.2, f32[16,128]{1,0:T(8,128)S(1)} %add.31.sums_ref, f32[128,2048]{1,0:T(8,128)S(1)} %get-tuple-element.15.middle_ref, f32[128,2048]{1,0:T(8,128)S(1)} %shard_map.59.part_ref, ...), custom_call_target="tpu_custom_call" | custom-call | bytes 2633728 | tf_op jit(solution)/shard_map/pallas_call | solution.py:363
  (8 shorter events, 0.0 us)
Async XLA Ops:
  0.0 1.2 %copy-start = (f32[128,2048]{1,0:T(8,128)S(1)}, f32[128,2048]{1,0:T(8,128)}, u32[]{:S(2)}) copy-start(f32[128,2048]{1,0:T(8,128)} %dist_ref.7) | copy-start | bytes 3145732
  1.2 0.7 %copy-start.4 = (s32[1,2,64]{2,1,0:T(2,128)S(1)}, s32[1,2,64]{2,1,0:T(2,128)}, u32[]{:S(2)}) copy-start(s32[1,2,64]{2,1,0:T(2,128)} %face_ref.3) | copy-start | bytes 1540
  1.9 14.7 %copy-start.1 = (f32[128,2048]{1,0:T(8,128)S(1)}, f32[128,2048]{1,0:T(8,128)}, u32[]{:S(2)}) copy-start(f32[128,2048]{1,0:T(8,128)} %dist_ref.7) | copy-start | bytes 3145732
  3.6 3.0 %collective-permute-start = (f32[16,128]{1,0:T(8,128)S(1)}, f32[16,128]{1,0:T(8,128)S(1)}, u32[]{:S(2)}, u32[]{:S(2)}) collective-permute-start(f32[16,128]{1,0:T(8,128)S(1)} %get-tuple-element.11), channel_id=1, source_target_pairs={{0,1},{1,0},{2,3},{3,2},{4,5},{5,4},{6,7},{7,6},{8,9},{9,8},{10,11... | collective-permute-start | bytes 24584 | tf_op jit(solution)/shard_map/ppermute | solution.py:378
  4.1 20.6 %collective-permute-start.4 = (f32[128,1024]{1,0:T(8,128)S(1)}, f32[128,1024]{1,0:T(8,128)S(1)}, u32[]{:S(2)}, u32[]{:S(2)}) collective-permute-start(f32[128,1024]{1,0:T(8,128)S(1)} %get-tuple-element.13), channel_id=1, source_target_pairs={{0,16},{16,0},{1,17},{17,1},{2,18},{18,2},{3,19},{19,3},{4,20},{20... | collective-permute-start | bytes 1572872 | tf_op jit(solution)/shard_map/ppermute | solution.py:388
  6.7 3.7 %collective-permute-start.1 = (f32[16,128]{1,0:T(8,128)S(1)}, f32[16,128]{1,0:T(8,128)S(1)}, u32[]{:S(2)}, u32[]{:S(2)}) collective-permute-start(f32[16,128]{1,0:T(8,128)S(1)} %add.24), channel_id=1, source_target_pairs={{0,2},{1,3},{2,0},{3,1},{4,6},{5,7},{6,4},{7,5},{8,10},{9,11},{10,... | collective-permute-start | bytes 24584 | tf_op jit(solution)/shard_map/ppermute | solution.py:378
  10.3 6.3 %copy-start.2 = (s32[6,128]{1,0:T(8,128)S(1)}, s32[6,128]{1,0:T(8,128)}, u32[]{:S(2)}) copy-start(s32[6,128]{1,0:T(8,128)} %mask_ref.9) | copy-start | bytes 9220
  10.3 6.3 %copy-start.3 = (s32[6,128]{1,0:T(8,128)S(1)}, s32[6,128]{1,0:T(8,128)}, u32[]{:S(2)}) copy-start(s32[6,128]{1,0:T(8,128)} %near_ref.3) | copy-start | bytes 9220
  10.3 3.7 %collective-permute-start.2 = (f32[16,128]{1,0:T(8,128)S(1)}, f32[16,128]{1,0:T(8,128)S(1)}, u32[]{:S(2)}, u32[]{:S(2)}) collective-permute-start(f32[16,128]{1,0:T(8,128)S(1)} %add.25), channel_id=1, source_target_pairs={{0,4},{1,5},{2,6},{3,7},{4,0},{5,1},{6,2},{7,3},{8,12},{9,13},{10,... | collective-permute-start | bytes 24584 | tf_op jit(solution)/shard_map/ppermute | solution.py:378
  14.0 4.5 %collective-permute-start.3 = (f32[16,128]{1,0:T(8,128)S(1)}, f32[16,128]{1,0:T(8,128)S(1)}, u32[]{:S(2)}, u32[]{:S(2)}) collective-permute-start(f32[16,128]{1,0:T(8,128)S(1)} %add.26), channel_id=1, source_target_pairs={{0,8},{1,9},{2,10},{3,11},{4,12},{5,13},{6,14},{7,15},{8,0},{9,1},... | collective-permute-start | bytes 24584 | tf_op jit(solution)/shard_map/ppermute | solution.py:378
  18.6 0.7 %copy-start.5 = (f32[128]{0:T(128)S(1)}, f32[128]{0:T(128)}, u32[]{:S(2)}) copy-start(f32[128]{0:T(128)} %param.6) | copy-start | bytes 1540
  23.5 15.3 %collective-permute-start.9 = (f32[128,1024]{1,0:T(8,128)S(1)}, f32[128,1024]{1,0:T(8,128)S(1)}, u32[]{:S(2)}, u32[]{:S(2)}) collective-permute-start(f32[128,1024]{1,0:T(8,128)S(1)} %get-tuple-element.16), channel_id=1, source_target_pairs={{0,16},{16,0},{1,17},{17,1},{2,18},{18,2},{3,19},{19,3},{4,20},{20... | collective-permute-start | bytes 1572872 | tf_op jit(solution)/shard_map/ppermute | solution.py:388
  25.8 1.2 %collective-permute-start.5 = (f32[16,128]{1,0:T(8,128)S(1)}, f32[16,128]{1,0:T(8,128)S(1)}, u32[]{:S(2)}, u32[]{:S(2)}) collective-permute-start(f32[16,128]{1,0:T(8,128)S(1)} %get-tuple-element.14), channel_id=1, source_target_pairs={{0,1},{1,0},{2,3},{3,2},{4,5},{5,4},{6,7},{7,6},{8,9},{9,8},{10,11... | collective-permute-start | bytes 24584 | tf_op jit(solution)/shard_map/ppermute | solution.py:378
  27.0 3.7 %collective-permute-start.6 = (f32[16,128]{1,0:T(8,128)S(1)}, f32[16,128]{1,0:T(8,128)S(1)}, u32[]{:S(2)}, u32[]{:S(2)}) collective-permute-start(f32[16,128]{1,0:T(8,128)S(1)} %add.28), channel_id=1, source_target_pairs={{0,2},{1,3},{2,0},{3,1},{4,6},{5,7},{6,4},{7,5},{8,10},{9,11},{10,... | collective-permute-start | bytes 24584 | tf_op jit(solution)/shard_map/ppermute | solution.py:378
  30.6 3.7 %collective-permute-start.7 = (f32[16,128]{1,0:T(8,128)S(1)}, f32[16,128]{1,0:T(8,128)S(1)}, u32[]{:S(2)}, u32[]{:S(2)}) collective-permute-start(f32[16,128]{1,0:T(8,128)S(1)} %add.29), channel_id=1, source_target_pairs={{0,4},{1,5},{2,6},{3,7},{4,0},{5,1},{6,2},{7,3},{8,12},{9,13},{10,... | collective-permute-start | bytes 24584 | tf_op jit(solution)/shard_map/ppermute | solution.py:378
  34.3 4.5 %collective-permute-start.8 = (f32[16,128]{1,0:T(8,128)S(1)}, f32[16,128]{1,0:T(8,128)S(1)}, u32[]{:S(2)}, u32[]{:S(2)}) collective-permute-start(f32[16,128]{1,0:T(8,128)S(1)} %add.30), channel_id=1, source_target_pairs={{0,8},{1,9},{2,10},{3,11},{4,12},{5,13},{6,14},{7,15},{8,0},{9,1},... | collective-permute-start | bytes 24584 | tf_op jit(solution)/shard_map/ppermute | solution.py:378

commit v2 on v1

v2 whole, which is shorter than its diff:
```python
import math

import jax
import jax.numpy as jnp
from jax import lax
from jax.experimental import pallas as pl
from jax.experimental.pallas import tpu as pltpu
from jax.sharding import PartitionSpec as P

NV = 32
LIMIT = 4.5
SPACING = 2.0 * LIMIT / NV
WEIGHT = SPACING**3 * (2.0 * math.pi) ** (-1.5)
TIME_STEP = 0.05
BASELINE_SHEAR = 0.1
SHEAR_EXPONENT = 0.66
MOMENTUM_RATIO = 2.0 / 3.0
PLANE = NV * NV
HALF = PLANE // 2
ROWS = 8
LANES = 128
COLUMN_TILE = 256
SUMS = 16
LOG2E = math.log2(math.e)
F32 = jnp.float32
BF16 = jnp.bfloat16


def point(slot):
    return -LIMIT + (slot.astype(F32) + 0.5) * SPACING


def lane_points(start, width):
    lane = lax.broadcasted_iota(jnp.int32, (1, width), 1) + start
    return point((lane >> 5) & (NV - 1)), point(lane & (NV - 1))


def planes_y(width):
    planes = width // PLANE
    first = lax.axis_index("vel") * planes
    return [point(first + at) for at in range(planes)], first >= NV // 2


def split(value, count):
    pieces = []
    for _ in range(count - 1):
        piece = value.astype(BF16)
        pieces.append(piece)
        value = value - piece.astype(F32)
    pieces.append(value.astype(BF16))
    return pieces


def dot(left, right, dims=((1,), (0,))):
    return lax.dot_general(left, right, (dims, ((), ())), preferred_element_type=F32)


def sum_table():
    lane = lax.broadcasted_iota(jnp.int32, (1, PLANE), 1)
    at_x = (2 * ((lane >> 5) & (NV - 1)) - (NV - 1)).astype(F32)
    at_z = (2 * (lane & (NV - 1)) - (NV - 1)).astype(F32)
    square = at_x * at_x + at_z * at_z
    rows = [
        jnp.ones_like(at_x),
        jnp.maximum(at_x, 0.0),
        jnp.maximum(-at_x, 0.0),
        jnp.maximum(at_z, 0.0),
        jnp.maximum(-at_z, 0.0),
        at_x * at_x,
        at_z * at_z,
        at_x * at_z,
        at_x * square,
        at_z * square,
    ]
    rows.append(jnp.zeros((SUMS - len(rows), PLANE), F32))
    return jnp.concatenate(split(jnp.concatenate(rows, axis=0), 2), axis=0)


def plane_sums(table_ref, value_ref, start, stop):
    width = value_ref.shape[1]
    parts = [value_ref[:, plane + start : plane + stop] for plane in range(0, width, PLANE)]
    values = jnp.concatenate(parts, axis=0)
    table = table_ref[:, start:stop]
    total = None
    for piece in split(values, 3):
        part = dot(table, piece, ((1,), (1,)))
        total = part if total is None else total + part
    return total[:SUMS] + total[SUMS:]


def sums_of(found, width):
    planes, upward = planes_y(width)
    cells = found.shape[1] // len(planes)
    unit = SPACING / 2
    count = up = xx = yy = zz = xy = xz = yz = third_x = third_y = third_z = 0.0
    x_plus = x_minus = z_plus = z_minus = 0.0
    for at, vel_y in enumerate(planes):
        rows = [found[row : row + 1, at * cells : (at + 1) * cells] for row in range(10)]
        ones, plus_x, minus_x, plus_z, minus_z = rows[0], *(unit * row for row in rows[1:5])
        sq_x, sq_z, cross = (unit * unit * row for row in rows[5:8])
        cube_x, cube_z = (unit**3 * row for row in rows[8:10])
        sq_y = vel_y * vel_y
        along_x, along_z = plus_x - minus_x, plus_z - minus_z
        count += ones
        x_plus += plus_x
        x_minus += minus_x
        z_plus += plus_z
        z_minus += minus_z
        up += jnp.abs(vel_y) * ones
        xx += sq_x
        yy += sq_y * ones
        zz += sq_z
        xy += vel_y * along_x
        xz += cross
        yz += vel_y * along_z
        third_x += cube_x + sq_y * along_x
        third_y += vel_y * (sq_x + sq_z + sq_y * ones)
        third_z += cube_z + sq_y * along_z
    y_plus = jnp.where(upward, up, 0.0)
    y_minus = jnp.where(upward, 0.0, up)
    rows = [count, xx, yy, zz, xy, xz, yz, third_x, third_y, third_z]
    rows += [x_minus, x_plus, y_minus, y_plus, z_minus, z_plus]
    return WEIGHT * jnp.concatenate(rows, axis=0)


def half_slices(width):
    low, high = [], []
    for plane in range(width // PLANE):
        low.append((plane * PLANE, plane * HALF))
        high.append((plane * PLANE + HALF, plane * HALF))
    return low, high


def move_rows(rows_ref, value_ref, send_ref, side):
    cells, width = value_ref.shape
    count = cells // 2
    ranges = half_slices(width)[side]

    def move(at, _):
        row = rows_ref[0, side, at]
        for source, target in ranges:
            send_ref[pl.ds((1 - side) * count + at, 1), target : target + HALF] = value_ref[
                pl.ds(row, 1), source : source + HALF
            ]
        return 0

    lax.fori_loop(0, count, move, 0, unroll=8)


def start_kernel(face_ref, dist_ref, own_ref, send_ref, sums_ref, table_ref, rows_ref, row_sem, sems):
    width = dist_ref.shape[1]
    row_copy = pltpu.make_async_copy(face_ref, rows_ref, row_sem)
    row_copy.start()
    copies = []
    for side, ranges in enumerate(half_slices(width)):
        for at, (source, _) in enumerate(ranges):
            lanes = slice(source, source + HALF)
            copy = pltpu.make_async_copy(
                dist_ref.at[:, lanes], own_ref.at[:, lanes], sems.at[side, at]
            )
            copy.start()
            copies.append((side, copy))
    table_ref[...] = sum_table()
    row_copy.wait()
    found = 0.0
    for side in range(2):
        for owner, copy in copies:
            if owner == side:
                copy.wait()
        move_rows(rows_ref, own_ref, send_ref, side)
        found += plane_sums(table_ref, own_ref, side * HALF, (side + 1) * HALF)
    sums_ref[...] = sums_of(found, width)


def picks(near_ref, mask_ref, face, cell_start, cells):
    index = near_ref[face : face + 1, :] - cell_start
    hit = lax.broadcasted_iota(jnp.int32, (cells, cells), 0) == index
    open_face = mask_ref[face : face + 1, :] != 1
    return jnp.where(hit & open_face, 1.0, 0.0).astype(F32)


def along(near_ref, mask_ref, upward):
    cells = near_ref.shape[1]
    cell_start = lax.axis_index("space") * cells
    faces = [picks(near_ref, mask_ref, face, cell_start, cells) for face in range(6)]
    return [faces[0], faces[1], jnp.where(upward, faces[2], faces[3]), faces[4], faces[5]]


def stream_tiles(near_ref, mask_ref, value_ref, store):
    cells, width = value_ref.shape
    planes, upward = planes_y(width)
    chosen = []
    for face in along(near_ref, mask_ref, upward):
        flipped = face.T.astype(BF16)
        chosen.append(jnp.concatenate([flipped, flipped], axis=1))
    rest = jnp.concatenate(chosen[2:], axis=0)
    for start in range(0, width, COLUMN_TILE):
        side = chosen[0] if start % PLANE >= HALF else chosen[1]
        vel_x, vel_z = lane_points(start, COLUMN_TILE)
        values = value_ref[:, start : start + COLUMN_TILE]
        pieces = jnp.concatenate(split(values, 2), axis=0)
        moved = dot(jnp.concatenate([side, rest], axis=0), pieces)
        speed_x, speed_z = jnp.abs(vel_x), jnp.abs(vel_z)
        speed_y = jnp.abs(planes[start // PLANE])
        from_z = jnp.where(vel_z > 0, moved[2 * cells : 3 * cells], moved[3 * cells :])
        stream = (
            speed_x * moved[:cells]
            + speed_y * moved[cells : 2 * cells]
            + speed_z * from_z
            - (speed_x + speed_y + speed_z) * values
        )
        store(slice(start, start + COLUMN_TILE), values, stream)


def stream_kernel(near_ref, mask_ref, value_ref, out_ref):
    def store(lanes, values, stream):
        out_ref[:, lanes] = TIME_STEP * stream

    stream_tiles(near_ref, mask_ref, value_ref, store)


def stream_last_kernel(near_ref, mask_ref, dist_ref, middle_ref, out_ref):
    def store(lanes, values, stream):
        out_ref[:, lanes] = 0.5 * (dist_ref[:, lanes] + values) + (0.5 * TIME_STEP) * stream

    stream_tiles(near_ref, mask_ref, middle_ref, store)


def wall_kernel(face_ref, temp_ref, mask_ref, shape_ref, back_ref, side_ref):
    cells, width = shape_ref.shape
    count = cells // 2
    planes, _ = planes_y(width)
    cooling = (-0.5 * LOG2E) / temp_ref[...]
    axis_point = point(lax.broadcasted_iota(jnp.int32, (NV, 1), 0))
    profile = jnp.exp2(axis_point * axis_point * cooling)
    mass = jnp.sum(profile, axis=0, keepdims=True)
    flux = jnp.sum(jnp.maximum(axis_point, 0.0) * profile, axis=0, keepdims=True)
    inv_norm = 1.0 / (WEIGHT * flux * mass * mass)
    mask = mask_ref[...]
    back_ref[...] = jnp.concatenate(
        [jnp.where(mask == 1, inv_norm, 0.0), jnp.zeros((2, cells), F32)], axis=0
    )
    rows = [mask[:2].astype(F32), cooling, jnp.zeros((LANES - 3, cells), F32)]
    columns = jnp.concatenate(rows, axis=0).T
    row = lax.broadcasted_iota(jnp.int32, (cells, count), 0)
    for side, face in enumerate((1, 0)):
        hit = (row == face_ref[0, face : face + 1, :]) & (columns[:, face : face + 1] != 1.0)
        picked = jnp.where(hit, 1.0, 0.0).astype(BF16)
        side_ref[side * cells : (side + 1) * cells, :] = jnp.concatenate([picked, picked], axis=1)
    cooling = jnp.broadcast_to(columns[:, 2:3], (cells, LANES))
    for start in range(0, PLANE, LANES):
        vel_x, vel_z = lane_points(start, LANES)
        flat = vel_x * vel_x + vel_z * vel_z
        for at, vel_y in enumerate(planes):
            lanes = slice(at * PLANE + start, at * PLANE + start + LANES)
            shape_ref[:, lanes] = jnp.exp2((flat + vel_y * vel_y) * cooling)


def columns_of(sums, back, width, step, keep):
    _, upward = planes_y(width)
    count = sums[0:1]
    inv_count = 1.0 / count
    flow_x = (sums[11:12] - sums[10:11]) * inv_count
    flow_y = (sums[13:14] - sums[12:13]) * inv_count
    flow_z = (sums[15:16] - sums[14:15]) * inv_count
    p_xx, p_yy, p_zz, p_xy, p_xz, p_yz = (sums[at : at + 1] for at in range(1, 7))
    energy = p_xx + p_yy + p_zz
    flow_sq = flow_x * flow_x + flow_y * flow_y + flow_z * flow_z
    temp = (energy * inv_count - flow_sq) / 3.0
    inv_temp = 1.0 / temp

    def heat(third, flow, press):
        return 0.5 * (
            third
            - 2.0 * (press[0] * flow_x + press[1] * flow_y + press[2] * flow_z)
            - flow * energy
            + 2.0 * count * flow * flow_sq
        )

    scale = ((1.0 - MOMENTUM_RATIO) / 5.0) * inv_count * inv_temp * inv_temp * (-2.0 / LOG2E)
    rate = (count * jnp.exp((1.0 - SHEAR_EXPONENT) * jnp.log(temp))) * (step / BASELINE_SHEAR)
    returned = (back[0:6] * step) * sums[10:16]
    rows = [
        flow_x,
        flow_y,
        flow_z,
        (-0.5 * LOG2E) * inv_temp,
        scale * heat(sums[7:8], flow_x, (p_xx, p_xy, p_xz)),
        scale * heat(sums[8:9], flow_y, (p_xy, p_yy, p_yz)),
        scale * heat(sums[9:10], flow_z, (p_xz, p_yz, p_zz)),
        count * inv_temp * lax.rsqrt(temp) * rate,
        keep - rate,
        jnp.where(upward, returned[2:3], returned[3:4]),
        returned[0:2],
        returned[4:6],
    ]
    rows.append(jnp.zeros((LANES - 14, count.shape[1]), F32))
    return jnp.concatenate(rows, axis=0).T


def relax(columns_ref, base_ref, value_ref, shape_ref, out_ref, done=None):
    cells, width = value_ref.shape
    planes, _ = planes_y(width)
    lane = lax.broadcasted_iota(jnp.int32, (ROWS, LANES), 1)
    first_x, vel_z = point((lane >> 5) & (NV - 1)), point(lane & (NV - 1))
    z_plus, z_minus = jnp.maximum(vel_z, 0.0), jnp.maximum(-vel_z, 0.0)

    def group(at, _):
        rows = pl.ds(pl.multiple_of(at * ROWS, ROWS), ROWS)
        columns = columns_ref[rows, :]
        flow_x, flow_y, flow_z, cool, heat_x, heat_y, heat_z, gain, keep, back_y, *back = (
            jnp.broadcast_to(columns[:, column : column + 1], (ROWS, LANES)) for column in range(14)
        )
        rel_z = vel_z - flow_z
        square_z = rel_z * rel_z * cool
        heat_of_z = rel_z * heat_z
        back_z = z_plus * back[2] + z_minus * back[3]
        of_y = []
        for vel_y in planes:
            rel_y = vel_y - flow_y
            of_y.append((rel_y * rel_y * cool, rel_y * heat_y, jnp.abs(vel_y) * back_y))
        for tile in range(PLANE // LANES):
            vel_x = first_x + (tile * (LANES // NV)) * SPACING
            rel_x = vel_x - flow_x
            square_xz = rel_x * rel_x * cool + square_z
            heat_xz = rel_x * heat_x + heat_of_z
            upper = tile * LANES >= HALF
            back_xz = jnp.abs(vel_x) * (back[0] if upper else back[1]) + back_z
            for plane, (square_y, heat_of_y, back_of_y) in enumerate(of_y):
                start = plane * PLANE + tile * LANES
                lanes = slice(start, start + LANES)
                square = square_xz + square_y
                skew = (heat_xz + heat_of_y) * (square + 2.5 * LOG2E) + 1.0
                out_ref[rows, lanes] = (
                    base_ref[rows, lanes]
                    + keep * value_ref[rows, lanes]
                    + gain * jnp.exp2(square) * skew
                    + shape_ref[rows, lanes] * (back_xz + back_of_y)
                )
        return 0

    parts = cells // ROWS // 4
    for part in range(4):
        lax.fori_loop(part * parts, (part + 1) * parts, group, 0)
        if done is not None:
            done(part)


def halo_tile(halo_refs, side, start, count):
    lanes = slice(start, start + COLUMN_TILE)
    if len(halo_refs) == 1:
        rows = halo_refs[0][(1 - side) * count : (2 - side) * count, lanes]
    else:
        rows = halo_refs[1 - side][:, lanes]
    return jnp.concatenate(split(rows, 2), axis=0)


def add_halo(side_ref, halo_refs, base_ref, out_ref, step):
    cells, width = base_ref.shape
    for side, ranges in enumerate(half_slices(width)):
        pick = side_ref[side * cells : (side + 1) * cells, :]
        for source, target in ranges:
            for tile in range(0, HALF, COLUMN_TILE):
                lanes = slice(source + tile, source + tile + COLUMN_TILE)
                vel_x, _ = lane_points(source + tile, COLUMN_TILE)
                halo = dot(pick, halo_tile(halo_refs, side, target + tile, cells // 2))
                out_ref[:, lanes] = base_ref[:, lanes] + (step * jnp.abs(vel_x)) * halo


def middle_kernel(face_ref, sums_ref, table_ref, back_ref, side_ref, own_ref, stream_ref, shape_ref, *refs):
    halo_refs = refs[:-7]
    out_ref, send_ref, next_ref, columns_ref, base_ref, rows_ref, row_sem = refs[-7:]
    width = own_ref.shape[1]
    row_copy = pltpu.make_async_copy(face_ref, rows_ref, row_sem)
    row_copy.start()
    columns_ref[...] = columns_of(sums_ref[...], back_ref[...], width, TIME_STEP, 1.0)
    add_halo(side_ref, halo_refs, stream_ref, base_ref, TIME_STEP)
    relax(columns_ref, base_ref, own_ref, shape_ref, out_ref)
    row_copy.wait()
    for side in range(2):
        move_rows(rows_ref, out_ref, send_ref, side)
    next_ref[...] = sums_of(plane_sums(table_ref, out_ref, 0, PLANE), width)


def last_kernel(sums_ref, back_ref, side_ref, middle_ref, part_ref, shape_ref, *refs):
    halo_refs = refs[:-5]
    out_ref, columns_ref, base_ref, result_ref, sems = refs[-5:]
    cells, width = middle_ref.shape
    step = 0.5 * TIME_STEP
    columns_ref[...] = columns_of(sums_ref[...], back_ref[...], width, step, 0.0)
    add_halo(side_ref, halo_refs, part_ref, base_ref, step)
    copies = []

    def done(part):
        rows = slice(part * cells // 4, (part + 1) * cells // 4)
        copy = pltpu.make_async_copy(result_ref.at[rows], out_ref.at[rows], sems.at[part])
        copy.start()
        copies.append(copy)

    relax(columns_ref, base_ref, middle_ref, shape_ref, result_ref, done)
    for copy in copies:
        copy.wait()


def call(kernel, outs, arrays, scratch=(), far=(), far_outs=False, flops=0):
    specs = [
        pl.BlockSpec(memory_space=pltpu.HBM if at in far else pltpu.VMEM)
        for at in range(len(arrays))
    ]
    out_space = pltpu.HBM if far_outs else pltpu.VMEM
    size = sum(math.prod(array.shape) * 4 for array in arrays)
    return pl.pallas_call(
        kernel,
        out_shape=[jax.ShapeDtypeStruct(shape, dtype) for shape, dtype in outs],
        in_specs=specs,
        out_specs=[pl.BlockSpec(memory_space=out_space)] * len(outs),
        scratch_shapes=list(scratch),
        compiler_params=pltpu.CompilerParams(vmem_limit_bytes=40 * 2**20),
        cost_estimate=pl.CostEstimate(flops=flops, bytes_accessed=size, transcendentals=0),
    )(*arrays)


def total(value):
    count = lax.axis_size("vel")
    step = 1
    while step < count:
        value = value + lax.ppermute(value, "vel", [(i, i ^ step) for i in range(count)])
        step *= 2
    return value


def exchange(send):
    count = lax.axis_size("space")
    forward = [(i, (i + 1) % count) for i in range(count)]
    backward = [(target, source) for source, target in forward]
    if count == 2:
        return [lax.ppermute(send, "space", forward)]
    half = send.shape[0] // 2
    return [
        lax.ppermute(send[:half], "space", forward),
        lax.ppermute(send[half:], "space", backward),
    ]


def on_device(dist, wall_temp, neighbours, wall_mask, face_rows):
    cells, width = dist.shape
    planes = width // PLANE
    whole, sums, send = ((cells, width), F32), ((SUMS, cells), F32), ((cells, width // 2), F32)
    table, back, sides = ((2 * SUMS, PLANE), BF16), ((8, cells), F32), ((2 * cells, cells), BF16)
    rows_scratch = [pltpu.SMEM(face_rows.shape, jnp.int32), pltpu.SemaphoreType.DMA(())]
    work = [pltpu.VMEM((cells, LANES), F32), pltpu.VMEM((cells, width), F32)]

    own, sent, own_sums, tab = call(
        start_kernel,
        [whole, send, sums, table],
        [face_rows, dist],
        rows_scratch + [pltpu.SemaphoreType.DMA((2, planes))],
        far=(0, 1),
    )
    halo = exchange(sent)
    shape, back, side = call(wall_kernel, [whole, back, sides], [face_rows, wall_temp[None, :], wall_mask])
    (stream,) = call(stream_kernel, [whole], [neighbours, wall_mask, own])
    sums_one = total(own_sums)
    middle, sent, own_sums = call(
        middle_kernel,
        [whole, send, sums],
        [face_rows, sums_one, tab, back, side, own, stream, shape, *halo],
        work + rows_scratch,
        far=(0,),
    )
    halo = exchange(sent)
    (part,) = call(stream_last_kernel, [whole], [neighbours, wall_mask, own, middle])
    sums_two = total(own_sums)
    (result,) = call(
        last_kernel,
        [whole],
        [sums_two, back, side, middle, part, shape, *halo],
        work + [pltpu.VMEM((cells, width), F32), pltpu.SemaphoreType.DMA((4,))],
        far_outs=True,
    )
    return result


def solution(mesh):
    return jax.shard_map(
        on_device,
        mesh=mesh,
        in_specs=(
            P("space", "vel"),
            P("space"),
            P(None, "space"),
            P(None, "space"),
            P("space", None, None),
        ),
        out_specs=P("space", "vel"),
        check_vma=False,
    )
```

time: 43.6 us -> 40.4 us (0.927)
  Pallas kernels: 13.3 us -> 10.6 us
  starting transfers between devices: 15.6 us -> 15 us
  waiting for transfers between devices: 11.8 us -> 12.3 us
    pallas_call x6, Pallas kernels: 13.3 us -> 10.6 us  [call(): pl.pallas_call(kernel, out_shape=[jax.ShapeDtypeStruct(shape, dtype) for...]
    ppermute x8, starting transfers between devices: 11.8 us -> 11.4 us  [total(): lax.ppermute(value, 'vel', [(i, i ^ step) for i in range(count)])]
    unnamed x12 -> x10, local copies, waits for them, and re-layouts: 2.57 us -> 2.27 us
  transfers between devices with their start and end apart: 10 -> 10, of which waited for: 7 -> 8; matrix products, arithmetic and copies ran while one was open for 0% -> 0% of each run, Pallas kernels for 16% -> 5%
where the time goes in v2:
time: 40.4 us; the launch traced here: 40.2 us
  starting transfers between devices  15 us (37%)
  waiting for transfers between devices  12.3 us (30%)
  Pallas kernels  10.6 us (26%)
  local copies, waits for them, and re-layouts  2.27 us (6%)
    ppermute x8, waiting for transfers between devices, total(): lax.ppermute(value, 'vel', [(i, i ^ step) for i in range(count)])  12.3 us
    ppermute x8, starting transfers between devices, total(): lax.ppermute(value, 'vel', [(i, i ^ step) for i in range(count)])  11.4 us
    pallas_call x6, Pallas kernels, call(): pl.pallas_call(kernel, out_shape=[jax.ShapeDtypeStruct(shape, dtype) for...  10.6 us
    ppermute x2, starting transfers between devices, exchange(): return [lax.ppermute(send, 'space', forward)]  3.65 us
    unnamed x10, local copies, waits for them, and re-layouts  2.27 us
  transfers between devices with their start and end apart: 10, of which 8 were waited for; matrix products, arithmetic and copies ran while one was open for 0% of the time, Pallas kernels for 5%

profile of v2, /device:TPU:0, one launch (start us, length us, event | category | flops | bytes accessed | tf_op | source)
XLA Modules:
  0.0 40.2 jit_solution(8301895056849551187)
XLA Ops:
  0.0 0.0 copy-start
  0.0 1.2 %copy-done = f32[128,2048]{1,0:T(8,128)S(1)} copy-done((f32[128,2048]{1,0:T(8,128)S(1)}, f32[128,2048]{1,0:T(8,128)}, u32[]{:S(2)}) %copy-start) | copy-done | bytes 1048600
  1.2 0.0 copy-start.3
  1.2 0.7 %copy-done.3 = s32[1,2,64]{2,1,0:T(2,128)S(1)} copy-done((s32[1,2,64]{2,1,0:T(2,128)S(1)}, s32[1,2,64]{2,1,0:T(2,128)}, u32[]{:S(2)}) %copy-start.3) | copy-done | bytes 536
  1.9 2.3 %shard_map.55 = (f32[128,2048]{1,0:T(8,128)S(1)}, f32[128,1024]{1,0:T(8,128)S(1)}, f32[16,128]{1,0:T(8,128)S(1)}, bf16[32,1024]{1,0:T(8,128)(2,1)S(1)}) custom-call(s32[1,2,64]{2,1,0:T(2,128)S(1)} %copy-done.3, f32[128,2048]{1,0:T(8,128)S(1)} %copy-done), custom_call_target="tpu_custom_call" | custom-call | bytes 1049088 | tf_op jit(solution)/shard_map/pallas_call | solution.py:412
  4.2 3.0 %collective-permute-start.4 = (f32[128,1024]{1,0:T(8,128)S(1)}, f32[128,1024]{1,0:T(8,128)S(1)}, u32[]{:S(2)}, u32[]{:S(2)}) collective-permute-start(f32[128,1024]{1,0:T(8,128)S(1)} %get-tuple-element.21), channel_id=1, source_target_pairs={{0,16},{16,0},{1,17},{17,1},{2,18},{18,2},{3,19},{19,3},{4,20},{20... | collective-permute-start | bytes 1572872 | tf_op jit(solution)/shard_map/ppermute | solution.py:437
  7.2 0.0 collective-permute-start
  7.2 1.2 %collective-permute-done = f32[16,128]{1,0:T(8,128)S(1)} collective-permute-done((f32[16,128]{1,0:T(8,128)S(1)}, f32[16,128]{1,0:T(8,128)S(1)}, u32[]{:S(2)}, u32[]{:S(2)}) %collective-permute-start) | collective-permute-done | bytes 8224 | tf_op jit(solution)/shard_map/ppermute | solution.py:427
  8.4 1.5 %collective-permute-start.1 = (f32[16,128]{1,0:T(8,128)S(1)}, f32[16,128]{1,0:T(8,128)S(1)}, u32[]{:S(2)}, u32[]{:S(2)}) collective-permute-start(f32[16,128]{1,0:T(8,128)S(1)} %add.24), channel_id=1, source_target_pairs={{0,2},{1,3},{2,0},{3,1},{4,6},{5,7},{6,4},{7,5},{8,10},{9,11},{10,... | collective-permute-start | bytes 24584 | tf_op jit(solution)/shard_map/ppermute | solution.py:427
  9.9 2.2 %collective-permute-done.1 = f32[16,128]{1,0:T(8,128)S(1)} collective-permute-done((f32[16,128]{1,0:T(8,128)S(1)}, f32[16,128]{1,0:T(8,128)S(1)}, u32[]{:S(2)}, u32[]{:S(2)}) %collective-permute-start.1) | collective-permute-done | bytes 8224 | tf_op jit(solution)/shard_map/ppermute | solution.py:427
  12.0 1.6 %collective-permute-start.2 = (f32[16,128]{1,0:T(8,128)S(1)}, f32[16,128]{1,0:T(8,128)S(1)}, u32[]{:S(2)}, u32[]{:S(2)}) collective-permute-start(f32[16,128]{1,0:T(8,128)S(1)} %add.25), channel_id=1, source_target_pairs={{0,4},{1,5},{2,6},{3,7},{4,0},{5,1},{6,2},{7,3},{8,12},{9,13},{10,... | collective-permute-start | bytes 24584 | tf_op jit(solution)/shard_map/ppermute | solution.py:427
  13.6 2.1 %collective-permute-done.2 = f32[16,128]{1,0:T(8,128)S(1)} collective-permute-done((f32[16,128]{1,0:T(8,128)S(1)}, f32[16,128]{1,0:T(8,128)S(1)}, u32[]{:S(2)}, u32[]{:S(2)}) %collective-permute-start.2) | collective-permute-done | bytes 8224 | tf_op jit(solution)/shard_map/ppermute | solution.py:427
  15.7 0.0 copy-start.1
  15.7 0.0 copy-start.4
  15.7 2.6 %collective-permute-start.3 = (f32[16,128]{1,0:T(8,128)S(1)}, f32[16,128]{1,0:T(8,128)S(1)}, u32[]{:S(2)}, u32[]{:S(2)}) collective-permute-start(f32[16,128]{1,0:T(8,128)S(1)} %add.26), channel_id=1, source_target_pairs={{0,8},{1,9},{2,10},{3,11},{4,12},{5,13},{6,14},{7,15},{8,0},{9,1},... | collective-permute-start | bytes 24584 | tf_op jit(solution)/shard_map/ppermute | solution.py:427
  18.4 0.0 copy-done.1
  18.4 0.0 copy-done.4
  18.4 0.0 copy-start.2
  18.4 0.3 shard_map.56
  18.7 0.4 copy-done.2
  19.0 0.8 %shard_map.57.stream_ref = f32[128,2048]{1,0:T(8,128)S(1)} custom-call(s32[6,128]{1,0:T(8,128)S(1)} %copy-done.2, s32[6,128]{1,0:T(8,128)S(1)} %copy-done.1, f32[128,2048]{1,0:T(8,128)S(1)} %get-tuple-element.19.value_ref.own_ref.dist_ref), custom_call_target="tpu_custom_call" | custom-call | bytes 1054720 | tf_op jit(solution)/shard_map/pallas_call | solution.py:412
  19.9 0.4 %collective-permute-done.3 = f32[16,128]{1,0:T(8,128)S(1)} collective-permute-done((f32[16,128]{1,0:T(8,128)S(1)}, f32[16,128]{1,0:T(8,128)S(1)}, u32[]{:S(2)}, u32[]{:S(2)}) %collective-permute-start.3) | collective-permute-done | bytes 8224 | tf_op jit(solution)/shard_map/ppermute | solution.py:427
  20.3 0.0 collective-permute-done.4.refs_0_
  20.3 3.4 %shard_map.58 = (f32[128,2048]{1,0:T(8,128)S(1)}, f32[128,1024]{1,0:T(8,128)S(1)}, f32[16,128]{1,0:T(8,128)S(1)}) custom-call(s32[1,2,64]{2,1,0:T(2,128)S(1)} %copy-done.3, f32[16,128]{1,0:T(8,128)S(1)} %add.27.sums_ref, bf16[32,1024]{1,0:T(8,128)(2,1)S(1)} %get-tuple-element.16.table_ref, f32[8,128]{1,0:T(8,128)S(1)} %get-tuple-element.17.back_ref, ...), custom_call_target="tpu_custom_call" | custom-call | bytes 3944960 | tf_op jit(solution)/shard_map/pallas_call | solution.py:412
  23.7 0.6 %collective-permute-start.9 = (f32[128,1024]{1,0:T(8,128)S(1)}, f32[128,1024]{1,0:T(8,128)S(1)}, u32[]{:S(2)}, u32[]{:S(2)}) collective-permute-start(f32[128,1024]{1,0:T(8,128)S(1)} %get-tuple-element.24), channel_id=1, source_target_pairs={{0,16},{16,0},{1,17},{17,1},{2,18},{18,2},{3,19},{19,3},{4,20},{20... | collective-permute-start | bytes 1572872 | tf_op jit(solution)/shard_map/ppermute | solution.py:437
  24.3 0.0 collective-permute-start.5
  24.3 1.2 %collective-permute-done.5 = f32[16,128]{1,0:T(8,128)S(1)} collective-permute-done((f32[16,128]{1,0:T(8,128)S(1)}, f32[16,128]{1,0:T(8,128)S(1)}, u32[]{:S(2)}, u32[]{:S(2)}) %collective-permute-start.5) | collective-permute-done | bytes 8224 | tf_op jit(solution)/shard_map/ppermute | solution.py:427
  25.5 1.5 %collective-permute-start.6 = (f32[16,128]{1,0:T(8,128)S(1)}, f32[16,128]{1,0:T(8,128)S(1)}, u32[]{:S(2)}, u32[]{:S(2)}) collective-permute-start(f32[16,128]{1,0:T(8,128)S(1)} %add.28), channel_id=1, source_target_pairs={{0,2},{1,3},{2,0},{3,1},{4,6},{5,7},{6,4},{7,5},{8,10},{9,11},{10,... | collective-permute-start | bytes 24584 | tf_op jit(solution)/shard_map/ppermute | solution.py:427
  27.0 2.2 %collective-permute-done.6 = f32[16,128]{1,0:T(8,128)S(1)} collective-permute-done((f32[16,128]{1,0:T(8,128)S(1)}, f32[16,128]{1,0:T(8,128)S(1)}, u32[]{:S(2)}, u32[]{:S(2)}) %collective-permute-start.6) | collective-permute-done | bytes 8224 | tf_op jit(solution)/shard_map/ppermute | solution.py:427
  29.1 1.6 %collective-permute-start.7 = (f32[16,128]{1,0:T(8,128)S(1)}, f32[16,128]{1,0:T(8,128)S(1)}, u32[]{:S(2)}, u32[]{:S(2)}) collective-permute-start(f32[16,128]{1,0:T(8,128)S(1)} %add.29), channel_id=1, source_target_pairs={{0,4},{1,5},{2,6},{3,7},{4,0},{5,1},{6,2},{7,3},{8,12},{9,13},{10,... | collective-permute-start | bytes 24584 | tf_op jit(solution)/shard_map/ppermute | solution.py:427
  30.7 2.1 %collective-permute-done.7 = f32[16,128]{1,0:T(8,128)S(1)} collective-permute-done((f32[16,128]{1,0:T(8,128)S(1)}, f32[16,128]{1,0:T(8,128)S(1)}, u32[]{:S(2)}, u32[]{:S(2)}) %collective-permute-start.7) | collective-permute-done | bytes 8224 | tf_op jit(solution)/shard_map/ppermute | solution.py:427
  32.8 2.6 %collective-permute-start.8 = (f32[16,128]{1,0:T(8,128)S(1)}, f32[16,128]{1,0:T(8,128)S(1)}, u32[]{:S(2)}, u32[]{:S(2)}) collective-permute-start(f32[16,128]{1,0:T(8,128)S(1)} %add.30), channel_id=1, source_target_pairs={{0,8},{1,9},{2,10},{3,11},{4,12},{5,13},{6,14},{7,15},{8,0},{9,1},... | collective-permute-start | bytes 24584 | tf_op jit(solution)/shard_map/ppermute | solution.py:427
  35.4 0.9 %shard_map.59.part_ref = f32[128,2048]{1,0:T(8,128)S(1)} custom-call(s32[6,128]{1,0:T(8,128)S(1)} %copy-done.2, s32[6,128]{1,0:T(8,128)S(1)} %copy-done.1, f32[128,2048]{1,0:T(8,128)S(1)} %get-tuple-element.19.value_ref.own_ref.dist_ref, f32[128,2048]{1,0:T(8,128)S(1)} %get-tuple-element.23.middle_ref), custom_call_target="tpu_custom_call" | custom-call | bytes 2103296 | tf_op jit(solution)/shard_map/pallas_call | solution.py:412
  36.3 1.0 %collective-permute-done.8 = f32[16,128]{1,0:T(8,128)S(1)} collective-permute-done((f32[16,128]{1,0:T(8,128)S(1)}, f32[16,128]{1,0:T(8,128)S(1)}, u32[]{:S(2)}, u32[]{:S(2)}) %collective-permute-start.8) | collective-permute-done | bytes 8224 | tf_op jit(solution)/shard_map/ppermute | solution.py:427
  37.4 0.0 collective-permute-done.9.refs_0_
  37.4 2.9 %shard_map.60 = f32[128,2048]{1,0:T(8,128)} custom-call(f32[16,128]{1,0:T(8,128)S(1)} %add.31.sums_ref, f32[8,128]{1,0:T(8,128)S(1)} %get-tuple-element.17.back_ref, bf16[256,128]{1,0:T(8,128)(2,1)S(1)} %get-tuple-element.18.side_ref, f32[128,2048]{1,0:T(8,128)S(1)} %get-tuple-element.23.middle_ref, f32[128,2048]{1,0:T(8,128)S(1)} %shard_map.59.part_ref, ...), custom_call_target="tpu_custom_call" | custom-call | bytes 3813376 | tf_op jit(solution)/shard_map/pallas_call | solution.py:412
  (8 shorter events, 0.0 us)
Async XLA Ops:
  0.0 1.2 %copy-start = (f32[128,2048]{1,0:T(8,128)S(1)}, f32[128,2048]{1,0:T(8,128)}, u32[]{:S(2)}) copy-start(f32[128,2048]{1,0:T(8,128)} %dist_ref.1) | copy-start | bytes 3145732
  1.2 0.7 %copy-start.3 = (s32[1,2,64]{2,1,0:T(2,128)S(1)}, s32[1,2,64]{2,1,0:T(2,128)}, u32[]{:S(2)}) copy-start(s32[1,2,64]{2,1,0:T(2,128)} %face_ref.5) | copy-start | bytes 1540
  4.2 16.1 %collective-permute-start.4 = (f32[128,1024]{1,0:T(8,128)S(1)}, f32[128,1024]{1,0:T(8,128)S(1)}, u32[]{:S(2)}, u32[]{:S(2)}) collective-permute-start(f32[128,1024]{1,0:T(8,128)S(1)} %get-tuple-element.21), channel_id=1, source_target_pairs={{0,16},{16,0},{1,17},{17,1},{2,18},{18,2},{3,19},{19,3},{4,20},{20... | collective-permute-start | bytes 1572872 | tf_op jit(solution)/shard_map/ppermute | solution.py:437
  7.2 1.2 %collective-permute-start = (f32[16,128]{1,0:T(8,128)S(1)}, f32[16,128]{1,0:T(8,128)S(1)}, u32[]{:S(2)}, u32[]{:S(2)}) collective-permute-start(f32[16,128]{1,0:T(8,128)S(1)} %get-tuple-element.15), channel_id=1, source_target_pairs={{0,1},{1,0},{2,3},{3,2},{4,5},{5,4},{6,7},{7,6},{8,9},{9,8},{10,11... | collective-permute-start | bytes 24584 | tf_op jit(solution)/shard_map/ppermute | solution.py:427
  8.4 3.7 %collective-permute-start.1 = (f32[16,128]{1,0:T(8,128)S(1)}, f32[16,128]{1,0:T(8,128)S(1)}, u32[]{:S(2)}, u32[]{:S(2)}) collective-permute-start(f32[16,128]{1,0:T(8,128)S(1)} %add.24), channel_id=1, source_target_pairs={{0,2},{1,3},{2,0},{3,1},{4,6},{5,7},{6,4},{7,5},{8,10},{9,11},{10,... | collective-permute-start | bytes 24584 | tf_op jit(solution)/shard_map/ppermute | solution.py:427
  12.0 3.7 %collective-permute-start.2 = (f32[16,128]{1,0:T(8,128)S(1)}, f32[16,128]{1,0:T(8,128)S(1)}, u32[]{:S(2)}, u32[]{:S(2)}) collective-permute-start(f32[16,128]{1,0:T(8,128)S(1)} %add.25), channel_id=1, source_target_pairs={{0,4},{1,5},{2,6},{3,7},{4,0},{5,1},{6,2},{7,3},{8,12},{9,13},{10,... | collective-permute-start | bytes 24584 | tf_op jit(solution)/shard_map/ppermute | solution.py:427
  15.7 2.7 %copy-start.1 = (s32[6,128]{1,0:T(8,128)S(1)}, s32[6,128]{1,0:T(8,128)}, u32[]{:S(2)}) copy-start(s32[6,128]{1,0:T(8,128)} %mask_ref.5) | copy-start | bytes 9220
  15.7 2.7 %copy-start.4 = (f32[128]{0:T(128)S(1)}, f32[128]{0:T(128)}, u32[]{:S(2)}) copy-start(f32[128]{0:T(128)} %param.6) | copy-start | bytes 1540
  15.7 4.6 %collective-permute-start.3 = (f32[16,128]{1,0:T(8,128)S(1)}, f32[16,128]{1,0:T(8,128)S(1)}, u32[]{:S(2)}, u32[]{:S(2)}) collective-permute-start(f32[16,128]{1,0:T(8,128)S(1)} %add.26), channel_id=1, source_target_pairs={{0,8},{1,9},{2,10},{3,11},{4,12},{5,13},{6,14},{7,15},{8,0},{9,1},... | collective-permute-start | bytes 24584 | tf_op jit(solution)/shard_map/ppermute | solution.py:427
  18.4 0.7 %copy-start.2 = (s32[6,128]{1,0:T(8,128)S(1)}, s32[6,128]{1,0:T(8,128)}, u32[]{:S(2)}) copy-start(s32[6,128]{1,0:T(8,128)} %near_ref.3) | copy-start | bytes 9220
  23.7 13.7 %collective-permute-start.9 = (f32[128,1024]{1,0:T(8,128)S(1)}, f32[128,1024]{1,0:T(8,128)S(1)}, u32[]{:S(2)}, u32[]{:S(2)}) collective-permute-start(f32[128,1024]{1,0:T(8,128)S(1)} %get-tuple-element.24), channel_id=1, source_target_pairs={{0,16},{16,0},{1,17},{17,1},{2,18},{18,2},{3,19},{19,3},{4,20},{20... | collective-permute-start | bytes 1572872 | tf_op jit(solution)/shard_map/ppermute | solution.py:437
  24.3 1.2 %collective-permute-start.5 = (f32[16,128]{1,0:T(8,128)S(1)}, f32[16,128]{1,0:T(8,128)S(1)}, u32[]{:S(2)}, u32[]{:S(2)}) collective-permute-start(f32[16,128]{1,0:T(8,128)S(1)} %get-tuple-element.22), channel_id=1, source_target_pairs={{0,1},{1,0},{2,3},{3,2},{4,5},{5,4},{6,7},{7,6},{8,9},{9,8},{10,11... | collective-permute-start | bytes 24584 | tf_op jit(solution)/shard_map/ppermute | solution.py:427
  25.5 3.7 %collective-permute-start.6 = (f32[16,128]{1,0:T(8,128)S(1)}, f32[16,128]{1,0:T(8,128)S(1)}, u32[]{:S(2)}, u32[]{:S(2)}) collective-permute-start(f32[16,128]{1,0:T(8,128)S(1)} %add.28), channel_id=1, source_target_pairs={{0,2},{1,3},{2,0},{3,1},{4,6},{5,7},{6,4},{7,5},{8,10},{9,11},{10,... | collective-permute-start | bytes 24584 | tf_op jit(solution)/shard_map/ppermute | solution.py:427
  29.1 3.7 %collective-permute-start.7 = (f32[16,128]{1,0:T(8,128)S(1)}, f32[16,128]{1,0:T(8,128)S(1)}, u32[]{:S(2)}, u32[]{:S(2)}) collective-permute-start(f32[16,128]{1,0:T(8,128)S(1)} %add.29), channel_id=1, source_target_pairs={{0,4},{1,5},{2,6},{3,7},{4,0},{5,1},{6,2},{7,3},{8,12},{9,13},{10,... | collective-permute-start | bytes 24584 | tf_op jit(solution)/shard_map/ppermute | solution.py:427
  32.8 4.5 %collective-permute-start.8 = (f32[16,128]{1,0:T(8,128)S(1)}, f32[16,128]{1,0:T(8,128)S(1)}, u32[]{:S(2)}, u32[]{:S(2)}) collective-permute-start(f32[16,128]{1,0:T(8,128)S(1)} %add.30), channel_id=1, source_target_pairs={{0,8},{1,9},{2,10},{3,11},{4,12},{5,13},{6,14},{7,15},{8,0},{9,1},... | collective-permute-start | bytes 24584 | tf_op jit(solution)/shard_map/ppermute | solution.py:427

commit v3 on v2

v3 whole, which is shorter than its diff:
```python
import functools
import math

import jax
import jax.numpy as jnp
from jax import lax
from jax.experimental import pallas as pl
from jax.experimental.pallas import tpu as pltpu
from jax.sharding import PartitionSpec as P

NV = 32
LIMIT = 4.5
SPACING = 2.0 * LIMIT / NV
WEIGHT = SPACING**3 * (2.0 * math.pi) ** (-1.5)
TIME_STEP = 0.05
BASELINE_SHEAR = 0.1
SHEAR_EXPONENT = 0.66
MOMENTUM_RATIO = 2.0 / 3.0
PLANE = NV * NV
HALF = PLANE // 2
ROWS = 8
LANES = 128
COLUMN_TILE = 256
SUMS = 16
FACES = 6
NOTES = 8
BEND = 2.5 * math.log2(math.e)
LOG2E = math.log2(math.e)
F32 = jnp.float32
BF16 = jnp.bfloat16


def point(slot):
    return -LIMIT + (slot.astype(F32) + 0.5) * SPACING


def lane_points(start, width):
    lane = lax.broadcasted_iota(jnp.int32, (1, width), 1) + start
    return point((lane >> 5) & (NV - 1)), point(lane & (NV - 1))


def planes_y(width):
    planes = width // PLANE
    first = lax.axis_index("vel") * planes
    return [point(first + at) for at in range(planes)], first >= NV // 2


def split(value, count):
    pieces = []
    for _ in range(count - 1):
        piece = value.astype(BF16)
        pieces.append(piece)
        value = value - piece.astype(F32)
    pieces.append(value.astype(BF16))
    return pieces


def dot(left, right, dims=((1,), (0,))):
    return lax.dot_general(left, right, (dims, ((), ())), preferred_element_type=F32)


def exact(left, right, dims=((1,), (0,))):
    rows = left.shape[0]
    found = dot(jnp.concatenate(split(left, 3), axis=0), right, dims)
    return found[:rows] + found[rows : 2 * rows] + found[2 * rows :]


def inward(vel_x, vel_y, vel_z):
    return [
        jnp.maximum(sign * vel, 0.0) for vel in (vel_x, vel_y, vel_z) for sign in (1.0, -1.0)
    ]


def weights(vel_x, vel_y, vel_z):
    speed_sq = vel_x * vel_x + vel_y * vel_y + vel_z * vel_z
    into = inward(vel_x, vel_y, vel_z)
    rows = [
        jnp.ones_like(vel_x),
        vel_x * vel_x,
        vel_y * vel_y,
        vel_z * vel_z,
        vel_x * vel_y,
        vel_x * vel_z,
        vel_y * vel_z,
        vel_x * speed_sq,
        vel_y * speed_sq,
        vel_z * speed_sq,
        into[1],
        into[0],
        into[3],
        into[2],
        into[5],
        into[4],
    ]
    return WEIGHT * jnp.concatenate(rows, axis=0), into


def face_hits(face_ref, cells):
    row = lax.broadcasted_iota(jnp.int32, (cells, face_ref.shape[2]), 0)
    return [jnp.where(row == face_ref[0, side : side + 1, :], 1.0, 0.0) for side in range(2)]


def sums_kernel(face_ref, dist_ref, sums_ref, send_ref):
    cells, width = dist_ref.shape
    planes, _ = planes_y(width)
    total = None
    for start in range(0, width, HALF):
        lanes = slice(start, start + HALF)
        vel_x, vel_z = lane_points(start, HALF)
        vel_y = jnp.full((1, HALF), planes[start // PLANE])
        base, into = weights(vel_x, vel_y, vel_z)
        table = jnp.concatenate([base] + [base * speed for speed in into], axis=0)
        coarse, fine = split(table, 2)
        finest = split(base, 3)[2]
        pieces = split(dist_ref[:, lanes], 3)
        across = ((1,), (1,))
        one = dot(jnp.concatenate([coarse, fine, finest], axis=0), pieces[0], across)
        two = dot(jnp.concatenate([coarse, fine], axis=0), pieces[1], across)
        three = dot(coarse, pieces[2], across)
        rows = table.shape[0]
        part = one[:rows] + one[rows : 2 * rows] + two[:rows] + two[rows:] + three
        part = jnp.concatenate([part[:SUMS] + one[2 * rows :], part[SUMS:]], axis=0)
        total = part if total is None else total + part
    sums_ref[...] = total
    low, high = face_hits(face_ref, cells)
    base, from_low, from_high = total[:SUMS], total[SUMS : 2 * SUMS], total[2 * SUMS : 3 * SUMS]
    upward = exact(jnp.concatenate([base, from_low], axis=0), high.astype(BF16))
    downward = exact(jnp.concatenate([base, from_high], axis=0), low.astype(BF16))
    send_ref[...] = jnp.concatenate([upward, downward], axis=0)


def halo_rows(refs, side, rows=slice(None)):
    if len(refs) == 2:
        return refs[side][rows]
    half = refs[0].shape[0] // 2
    start, stop, _ = rows.indices(half)
    return refs[0][side * half + start : side * half + stop]


def gather_kernel(sums_ref, *refs):
    halo_refs, out_ref = refs[:-1], refs[-1]
    rows = sums_ref.shape[0]
    out_ref[:rows, :] = sums_ref[...]
    out_ref[rows:, :] = jnp.concatenate([halo_rows(halo_refs, 0), halo_rows(halo_refs, 1)], axis=1)

def half_slices(width):
    low, high = [], []
    for plane in range(width // PLANE):
        low.append((plane * PLANE, plane * HALF))
        high.append((plane * PLANE + HALF, plane * HALF))
    return low, high


def move_rows(rows_ref, plane, value_ref, send_ref, side, first):
    cells, width = value_ref.shape
    ranges = half_slices(width)[side]

    def move(at, _):
        row = rows_ref[0, plane, at]
        for source, target in ranges:
            send_ref[pl.ds(first + at, 1), target : target + HALF] = value_ref[
                pl.ds(row, 1), source : source + HALF
            ]
        return 0

    lax.fori_loop(0, cells // 2, move, 0, unroll=8)


def wall_rows(temp_ref):
    cooling = (-0.5 * LOG2E) / temp_ref[...]
    axis_point = point(lax.broadcasted_iota(jnp.int32, (NV, 1), 0))
    profile = jnp.exp2(axis_point * axis_point * cooling)
    mass = jnp.sum(profile, axis=0, keepdims=True)
    flux = jnp.sum(jnp.maximum(axis_point, 0.0) * profile, axis=0, keepdims=True)
    return 1.0 / (WEIGHT * flux * mass * mass), cooling


def near_plane_kernel(rows_ref, face_ref, temp_ref, mask_ref, dist_ref, send_ref):
    cells, _ = dist_ref.shape
    count = cells // 2
    inv_norm, cooling = wall_rows(temp_ref)
    notes = jnp.concatenate([mask_ref[...].astype(F32), inv_norm, cooling], axis=0)
    low, high = face_hits(face_ref, cells)
    for side, hits in ((1, high), (0, low)):
        first = (1 - side) * (count + NOTES)
        send_ref[first + count : first + count + NOTES, :count] = exact(notes, hits.astype(BF16))
        move_rows(rows_ref, side, dist_ref, send_ref, side, first)


def far_plane_kernel(rows_ref, dist_ref, send_ref):
    for side in (1, 0):
        first = (1 - side) * (dist_ref.shape[0] // 2)
        move_rows(rows_ref, 1 - side, dist_ref, send_ref, side, first)


def picks(near_ref, mask_ref, face, cell_start, cells):
    index = near_ref[face : face + 1, :] - cell_start
    hit = lax.broadcasted_iota(jnp.int32, (cells, cells), 0) == index
    open_face = mask_ref[face : face + 1, :] != 1
    return jnp.where(hit & open_face, 1.0, 0.0).astype(F32)


def along(near_ref, mask_ref, upward):
    cells = near_ref.shape[1]
    cell_start = lax.axis_index("space") * cells
    faces = [picks(near_ref, mask_ref, face, cell_start, cells) for face in range(6)]
    return [faces[0], faces[1], jnp.where(upward, faces[2], faces[3]), faces[4], faces[5]]


def stream_tiles(near_ref, mask_ref, value_ref, store):
    cells, width = value_ref.shape
    planes, upward = planes_y(width)
    chosen = []
    for face in along(near_ref, mask_ref, upward):
        flipped = face.T.astype(BF16)
        chosen.append(jnp.concatenate([flipped, flipped], axis=1))
    rest = jnp.concatenate(chosen[2:], axis=0)
    for start in range(0, width, COLUMN_TILE):
        side = chosen[0] if start % PLANE >= HALF else chosen[1]
        vel_x, vel_z = lane_points(start, COLUMN_TILE)
        values = value_ref[:, start : start + COLUMN_TILE]
        pieces = jnp.concatenate(split(values, 2), axis=0)
        moved = dot(jnp.concatenate([side, rest], axis=0), pieces)
        speed_x, speed_z = jnp.abs(vel_x), jnp.abs(vel_z)
        speed_y = jnp.abs(planes[start // PLANE])
        from_z = jnp.where(vel_z > 0, moved[2 * cells : 3 * cells], moved[3 * cells :])
        stream = (
            speed_x * moved[:cells]
            + speed_y * moved[cells : 2 * cells]
            + speed_z * from_z
            - (speed_x + speed_y + speed_z) * values
        )
        store(slice(start, start + COLUMN_TILE), values, stream)


def stream_kernel(near_ref, mask_ref, value_ref, out_ref):
    def store(lanes, values, stream):
        out_ref[:, lanes] = TIME_STEP * stream

    stream_tiles(near_ref, mask_ref, value_ref, store)


def stream_last_kernel(near_ref, mask_ref, dist_ref, middle_ref, out_ref):
    def store(lanes, values, stream):
        out_ref[:, lanes] = 0.5 * (dist_ref[:, lanes] + values) + (0.5 * TIME_STEP) * stream

    stream_tiles(near_ref, mask_ref, middle_ref, store)


def wall_kernel(face_ref, temp_ref, mask_ref, shape_ref, back_ref, side_ref):
    cells, width = shape_ref.shape
    count = cells // 2
    planes, _ = planes_y(width)
    inv_norm, cooling = wall_rows(temp_ref)
    mask = mask_ref[...]
    back_ref[...] = jnp.concatenate(
        [jnp.where(mask == 1, inv_norm, 0.0), cooling, jnp.zeros((1, cells), F32)],
        axis=0,
    )
    rows = [mask[:2].astype(F32), cooling, jnp.zeros((LANES - 3, cells), F32)]
    columns = jnp.concatenate(rows, axis=0).T
    row = lax.broadcasted_iota(jnp.int32, (cells, count), 0)
    for side, face in enumerate((1, 0)):
        hit = (row == face_ref[0, face : face + 1, :]) & (columns[:, face : face + 1] != 1.0)
        picked = jnp.where(hit, 1.0, 0.0).astype(BF16)
        side_ref[side * cells : (side + 1) * cells, :] = jnp.concatenate([picked, picked], axis=1)
    cooling = jnp.broadcast_to(columns[:, 2:3], (cells, LANES))
    for start in range(0, PLANE, LANES):
        vel_x, vel_z = lane_points(start, LANES)
        flat = vel_x * vel_x + vel_z * vel_z
        for at, vel_y in enumerate(planes):
            lanes = slice(at * PLANE + start, at * PLANE + start + LANES)
            shape_ref[:, lanes] = jnp.exp2((flat + vel_y * vel_y) * cooling)


def coefficients(sums, back, step, keep):
    count = sums[0:1]
    inv_count = 1.0 / count
    flow_x = (sums[11:12] - sums[10:11]) * inv_count
    flow_y = (sums[13:14] - sums[12:13]) * inv_count
    flow_z = (sums[15:16] - sums[14:15]) * inv_count
    p_xx, p_yy, p_zz, p_xy, p_xz, p_yz = (sums[at : at + 1] for at in range(1, 7))
    energy = p_xx + p_yy + p_zz
    flow_sq = flow_x * flow_x + flow_y * flow_y + flow_z * flow_z
    temp = (energy * inv_count - flow_sq) / 3.0
    inv_temp = 1.0 / temp

    def heat(third, flow, press):
        return 0.5 * (
            third
            - 2.0 * (press[0] * flow_x + press[1] * flow_y + press[2] * flow_z)
            - flow * energy
            + 2.0 * count * flow * flow_sq
        )

    scale = ((1.0 - MOMENTUM_RATIO) / 5.0) * inv_count * inv_temp * inv_temp * (-2.0 / LOG2E)
    rate = (count * jnp.exp((1.0 - SHEAR_EXPONENT) * jnp.log(temp))) * (step / BASELINE_SHEAR)
    returned = (back[0:6] * step) * sums[10:16]
    rows = [
        flow_x,
        flow_y,
        flow_z,
        (-0.5 * LOG2E) * inv_temp,
        scale * heat(sums[7:8], flow_x, (p_xx, p_xy, p_xz)),
        scale * heat(sums[8:9], flow_y, (p_xy, p_yy, p_yz)),
        scale * heat(sums[9:10], flow_z, (p_xz, p_yz, p_zz)),
        count * inv_temp * lax.rsqrt(temp) * rate,
        keep - rate,
    ]
    return rows, returned


def columns_of(sums, back, width, step, keep):
    _, upward = planes_y(width)
    rows, returned = coefficients(sums, back, step, keep)
    rows += [
        jnp.where(upward, returned[2:3], returned[3:4]),
        returned[0:2],
        returned[4:6],
        jnp.zeros((LANES - 14, sums.shape[1]), F32),
    ]
    return jnp.concatenate(rows, axis=0).T


def relax(columns_ref, base_ref, value_ref, shape_ref, out_ref, half=False):
    cells, width = value_ref.shape
    planes, _ = planes_y(2 * width if half else width)
    lane = lax.broadcasted_iota(jnp.int32, (ROWS, LANES), 1)
    first_x, vel_z = point((lane >> 5) & (NV - 1)), point(lane & (NV - 1))
    z_plus, z_minus = jnp.maximum(vel_z, 0.0), jnp.maximum(-vel_z, 0.0)

    def group(at, _, tiles=range(PLANE // LANES), stride=PLANE):
        rows = pl.ds(pl.multiple_of(at * ROWS, ROWS), ROWS)
        columns = columns_ref[rows, :]
        flow_x, flow_y, flow_z, cool, heat_x, heat_y, heat_z, gain, keep, back_y, *back = (
            jnp.broadcast_to(columns[:, column : column + 1], (ROWS, LANES)) for column in range(14)
        )
        rel_z = vel_z - flow_z
        square_z = rel_z * rel_z * cool
        heat_of_z = rel_z * heat_z
        back_z = z_plus * back[2] + z_minus * back[3]
        of_y = []
        for vel_y in planes:
            rel_y = vel_y - flow_y
            of_y.append((rel_y * rel_y * cool, rel_y * heat_y, jnp.abs(vel_y) * back_y))
        for tile in tiles:
            vel_x = first_x + (tile * (LANES // NV)) * SPACING
            rel_x = vel_x - flow_x
            square_xz = rel_x * rel_x * cool + square_z
            heat_xz = rel_x * heat_x + heat_of_z
            upper = tile * LANES >= HALF
            back_xz = jnp.abs(vel_x) * (back[0] if upper else back[1]) + back_z
            for plane, (square_y, heat_of_y, back_of_y) in enumerate(of_y):
                start = plane * stride + (tile - tiles[0]) * LANES
                lanes = slice(start, start + LANES)
                square = square_xz + square_y
                skew = (heat_xz + heat_of_y) * (square + 2.5 * LOG2E) + 1.0
                out_ref[rows, lanes] = (
                    base_ref[rows, lanes]
                    + keep * value_ref[rows, lanes]
                    + gain * jnp.exp2(square) * skew
                    + shape_ref[rows, lanes] * (back_xz + back_of_y)
                )
        return 0

    groups = cells // ROWS
    if half:
        low, high = range(HALF // LANES), range(HALF // LANES, PLANE // LANES)
        lax.fori_loop(0, groups // 2, functools.partial(group, tiles=high, stride=HALF), 0)
        lax.fori_loop(groups // 2, groups, functools.partial(group, tiles=low, stride=HALF), 0)
    else:
        lax.fori_loop(0, groups, group, 0)


def middle_kernel(sums_ref, back_ref, side_ref, own_ref, stream_ref, shape_ref, *refs):
    halo_refs, (out_ref, columns_ref, base_ref) = refs[:-3], refs[-3:]
    cells, width = own_ref.shape
    columns_ref[...] = columns_of(sums_ref[:SUMS], back_ref[...], width, TIME_STEP, 1.0)
    for side, ranges in enumerate(half_slices(width)):
        pick = side_ref[side * cells : (side + 1) * cells, :]
        for source, target in ranges:
            for tile in range(0, HALF, COLUMN_TILE):
                lanes = slice(source + tile, source + tile + COLUMN_TILE)
                vel_x, _ = lane_points(source + tile, COLUMN_TILE)
                rows = halo_rows(halo_refs, 1 - side, slice(0, cells // 2))
                rows = rows[:, target + tile : target + tile + COLUMN_TILE]
                halo = dot(pick, jnp.concatenate(split(rows, 2), axis=0))
                base_ref[:, lanes] = stream_ref[:, lanes] + (TIME_STEP * jnp.abs(vel_x)) * halo
    relax(columns_ref, base_ref, own_ref, shape_ref, out_ref)


def relax_kernel(sums_ref, back_ref, middle_ref, part_ref, shape_ref, out_ref, columns_ref):
    width = middle_ref.shape[1]
    step = 0.5 * TIME_STEP
    columns_ref[...] = columns_of(sums_ref[...], back_ref[...], width, step, 0.0)
    relax(columns_ref, part_ref, middle_ref, shape_ref, out_ref)


ORDERS = (
    [(0, 0, 0)],
    [(2, 0, 0)],
    [(0, 2, 0)],
    [(0, 0, 2)],
    [(1, 1, 0)],
    [(1, 0, 1)],
    [(0, 1, 1)],
    [(3, 0, 0), (1, 2, 0), (1, 0, 2)],
    [(0, 3, 0), (2, 1, 0), (0, 1, 2)],
    [(0, 0, 3), (2, 0, 1), (0, 2, 1)],
    [("-", 0, 0)],
    [("+", 0, 0)],
    [(0, "-", 0)],
    [(0, "+", 0)],
    [(0, 0, "-")],
    [(0, 0, "+")],
)


def power(value, order):
    if order == "+":
        return jnp.maximum(value, 0.0)
    if order == "-":
        return jnp.maximum(-value, 0.0)
    result = None
    for _ in range(order):
        result = value if result is None else result * value
    return result


def advance_kernel(face_ref, near_ref, mask_ref, sums_ref, back_ref, out_ref):
    cells = near_ref.shape[1]
    count = cells // 2
    cell_start = lax.axis_index("space") * cells
    sums = sums_ref[:SUMS]
    flux = [sums_ref[SUMS * (face + 1) : SUMS * (face + 2)] for face in range(FACES)]
    gas = 0.0
    for face in range(FACES):
        hits = picks(near_ref, mask_ref, face, cell_start, cells).astype(BF16)
        gas += exact(flux[face], hits) - flux[face]
    arrived = sums_ref[SUMS * (FACES + 2) :]
    for face, hits in enumerate(face_hits(face_ref, cells)):
        found = exact(
            arrived[:, face * count : (face + 1) * count], hits.astype(BF16), ((1,), (1,))
        )
        gas += jnp.where(mask_ref[face : face + 1, :] != 1, found, 0.0)

    rows, returned = coefficients(sums, back_ref[...], TIME_STEP, 1.0)
    flows, cool, heats, gain, keep = rows[0:3], rows[3], rows[4:7], rows[7], rows[8]
    points = jnp.broadcast_to(point(lax.broadcasted_iota(jnp.int32, (NV, cells), 0)), (NV, cells))
    axes = []
    for flow in flows:
        off = points - flow
        bell = jnp.exp2(off * off * cool)
        axes.append([bell, bell * off, bell * off * off, bell * off * off * off])
    known = {}

    def along_axis(axis, order):
        if (axis, order) not in known:
            factor = power(points, order)
            known[axis, order] = [
                jnp.sum(term if factor is None else factor * term, axis=0, keepdims=True)
                for term in axes[axis]
            ]
        return known[axis, order]

    wall_bell = jnp.exp2(points * points * back_ref[6:7])
    above = jnp.maximum(points, 0.0)
    wall_sums = [jnp.sum(jnp.where(points > 0, wall_bell, 0.0), axis=0, keepdims=True)]
    for _ in range(4):
        wall_bell = wall_bell * above
        wall_sums.append(jnp.sum(wall_bell, axis=0, keepdims=True))

    def wall_full(order):
        if order in ("+", "-"):
            return wall_sums[1]
        return None if order % 2 else 2.0 * wall_sums[order]

    def wall_half(order, sign):
        if order in ("+", "-"):
            return wall_sums[2] if order == sign else None
        found = wall_sums[order + 1]
        return -found if order % 2 and sign == "-" else found

    found_rows = []
    for orders in ORDERS:
        bells, walls = 0.0, 0.0
        for order in orders:
            (x0, x1, x2, x3), (y0, y1, y2, y3), (z0, z1, z2, z3) = (
                along_axis(axis, order[axis]) for axis in range(3)
            )
            xy, xz, yz = x0 * y0, x0 * z0, y0 * z0
            skew = heats[0] * (x1 * (BEND * yz + cool * (y2 * z0 + y0 * z2)) + cool * x3 * yz)
            skew += heats[1] * (y1 * (BEND * xz + cool * (x2 * z0 + x0 * z2)) + cool * y3 * xz)
            skew += heats[2] * (z1 * (BEND * xy + cool * (x2 * y0 + x0 * y2)) + cool * z3 * xy)
            bells += xy * z0 + skew
            for face in range(FACES):
                terms = [
                    wall_half(order[axis], "+-"[face % 2])
                    if axis == face // 2
                    else wall_full(order[axis])
                    for axis in range(3)
                ]
                if all(term is not None for term in terms):
                    walls += returned[face : face + 1] * terms[0] * terms[1] * terms[2]
        found_rows.append(gain * bells + walls)
    found = WEIGHT * jnp.concatenate(found_rows, axis=0)
    out_ref[...] = found + keep * sums + TIME_STEP * gas


def halo_stream_kernel(face_ref, near_ref, *refs):
    halo_refs, (base_ref, shape_ref, values_ref, notes_ref, open_ref) = refs[:-5], refs[-5:]
    rows, width = base_ref.shape
    count = rows // 2
    planes, upward = planes_y(2 * width)
    cell_start = lax.axis_index("space") * rows
    notes = jnp.concatenate(
        [halo_rows(halo_refs, side, slice(count, count + NOTES))[:, :count] for side in range(2)],
        axis=1,
    )
    notes_ref[...] = notes
    passing = jnp.where(notes[:FACES] != 1.0, 1.0, 0.0)
    lane = lax.broadcasted_iota(jnp.int32, (1, rows), 1)
    picked = [
        jnp.where(lane < count, passing[0:1], passing[1:2]),
        jnp.where(upward, passing[2:3], passing[3:4]),
        passing[4:6],
        notes[7:8],
        jnp.zeros((LANES - 5, rows), F32),
    ]
    columns = jnp.concatenate(picked, axis=0).T
    open_x, open_y, open_low, open_high, cooling = (
        jnp.broadcast_to(columns[:, at : at + 1], (rows, LANES)) for at in range(5)
    )
    open_ref[...] = TIME_STEP * open_x
    low = face_hits(face_ref, rows)[0]
    low_flipped, low = low.T.astype(BF16), low.astype(BF16)
    row = lax.broadcasted_iota(jnp.int32, (rows, rows), 0)
    steps = []
    for face in range(2, FACES):
        hits = jnp.where(row == near_ref[face : face + 1, :] - cell_start, 1.0, 0.0)
        from_rows = dot(low_flipped, hits.T.astype(BF16)).astype(BF16)
        steps.append(dot(from_rows, low))
    along_y = jnp.where(upward, steps[0], steps[1])
    picks_all = jnp.concatenate([along_y, steps[2], steps[3]], axis=0).astype(BF16)
    picks_all = jnp.concatenate([picks_all, picks_all], axis=1)
    for side in range(2):
        block = slice(side * count, (side + 1) * count)
        values_ref[block, :] = halo_rows(halo_refs, side, slice(0, count))

        def wide(column):
            return jnp.concatenate([column[block]] * (COLUMN_TILE // LANES), axis=1)

        for start in range(0, width, COLUMN_TILE):
            lanes = slice(start, start + COLUMN_TILE)
            vel_x, vel_z = lane_points((1 - side) * HALF + start % HALF, COLUMN_TILE)
            vel_y = planes[start // HALF]
            values = values_ref[block, lanes]
            moved = dot(picks_all, jnp.concatenate(split(values, 2), axis=0))
            speed_x, speed_y, speed_z = jnp.abs(vel_x), jnp.abs(vel_y), jnp.abs(vel_z)
            from_z = jnp.where(
                vel_z > 0,
                wide(open_low) * moved[count : 2 * count],
                wide(open_high) * moved[2 * count :],
            )
            base_ref[block, lanes] = TIME_STEP * (
                speed_y * (wide(open_y) * moved[:count])
                + speed_z * from_z
                - (speed_x + speed_y + speed_z) * values
            )
            speed_sq = vel_x * vel_x + vel_y * vel_y + vel_z * vel_z
            shape_ref[block, lanes] = jnp.exp2(speed_sq * wide(cooling))


def halo_relax_kernel(sums_ref, notes_ref, base_ref, shape_ref, values_ref, out_ref, columns_ref):
    width = values_ref.shape[1]
    sums = sums_ref[SUMS * (FACES + 1) : SUMS * (FACES + 2)]
    notes = notes_ref[...]
    back = jnp.where(notes[:FACES] == 1.0, notes[6:7], 0.0)
    columns_ref[...] = columns_of(sums, back, 2 * width, TIME_STEP, 1.0)
    relax(columns_ref, base_ref, values_ref, shape_ref, out_ref, half=True)


def last_kernel(side_ref, part_ref, plane_ref, open_ref, *refs):
    halo_refs, (out_ref, result_ref, sems) = refs[:-3], refs[-3:]
    cells, width = part_ref.shape
    count = cells // 2
    copies = []
    for side, ranges in enumerate(half_slices(width)):
        pick = side_ref[side * cells : (side + 1) * cells, :]
        block = slice((1 - side) * count, (2 - side) * count)
        gate = jnp.concatenate([open_ref[block]] * (COLUMN_TILE // LANES), axis=1)
        for source, target in ranges:
            for tile in range(0, HALF, COLUMN_TILE):
                lanes = slice(source + tile, source + tile + COLUMN_TILE)
                there = slice(target + tile, target + tile + COLUMN_TILE)
                speed_x = jnp.abs(lane_points(source + tile, COLUMN_TILE)[0])
                rows = halo_rows(halo_refs, 1 - side)[:, there]
                rows = plane_ref[block, there] + gate * speed_x * rows
                halo = dot(pick, jnp.concatenate(split(rows, 2), axis=0))
                result_ref[:, lanes] = part_ref[:, lanes] + (0.5 * TIME_STEP * speed_x) * halo
                copy = pltpu.make_async_copy(
                    result_ref.at[:, lanes], out_ref.at[:, lanes], sems.at[len(copies)]
                )
                copy.start()
                copies.append(copy)
    for copy in copies:
        copy.wait()


def call(kernel, outs, arrays, scratch=(), scalars=0, far_outs=False, flops=0):
    specs = [
        pl.BlockSpec(memory_space=pltpu.SMEM if at < scalars else pltpu.VMEM)
        for at in range(len(arrays))
    ]
    out_space = pltpu.HBM if far_outs else pltpu.VMEM
    size = sum(math.prod(array.shape) * 4 for array in arrays)
    return pl.pallas_call(
        kernel,
        out_shape=[jax.ShapeDtypeStruct(shape, dtype) for shape, dtype in outs],
        in_specs=specs,
        out_specs=[pl.BlockSpec(memory_space=out_space)] * len(outs),
        scratch_shapes=list(scratch),
        compiler_params=pltpu.CompilerParams(vmem_limit_bytes=40 * 2**20),
        cost_estimate=pl.CostEstimate(flops=flops, bytes_accessed=size, transcendentals=0),
    )(*arrays)


def total(value):
    count = lax.axis_size("vel")
    step = 1
    while step < count:
        value = value + lax.ppermute(value, "vel", [(i, i ^ step) for i in range(count)])
        step *= 2
    return value


def exchange(send):
    count = lax.axis_size("space")
    forward = [(i, (i + 1) % count) for i in range(count)]
    backward = [(target, source) for source, target in forward]
    if count == 2:
        return [lax.ppermute(send, "space", forward)]
    half = send.shape[0] // 2
    return [
        lax.ppermute(send[:half], "space", forward),
        lax.ppermute(send[half:], "space", backward),
    ]


def on_device(dist, wall_temp, neighbours, wall_mask, face_rows):
    cells, width = dist.shape
    count, half = cells // 2, width // 2
    temp = wall_temp[None, :]
    whole, plane = ((cells, width), F32), ((cells, half), F32)
    every = SUMS * (FACES + 1)
    columns = pltpu.VMEM((cells, LANES), F32)

    own_sums, sent = call(
        sums_kernel, [((every, cells), F32), ((4 * SUMS, count), F32)], [face_rows, dist]
    )
    halo_sums = exchange(sent)
    (sent,) = call(
        near_plane_kernel,
        [((2 * (count + NOTES), half), F32)],
        [face_rows, face_rows, temp, wall_mask, dist],
        scalars=1,
    )
    near = exchange(sent)
    (sent,) = call(far_plane_kernel, [plane], [face_rows, dist], scalars=1)
    far = exchange(sent)
    (sums,) = call(gather_kernel, [((every + 2 * SUMS, cells), F32)], [own_sums, *halo_sums])
    shape, back, side = call(
        wall_kernel,
        [whole, ((8, cells), F32), ((2 * cells, cells), BF16)],
        [face_rows, temp, wall_mask],
    )
    (stream,) = call(stream_kernel, [whole], [neighbours, wall_mask, dist])
    base, halo_shape, values, notes, gate = call(
        halo_stream_kernel,
        [plane, plane, plane, ((NOTES, cells), F32), ((cells, LANES), F32)],
        [face_rows, neighbours, *near],
    )
    sums = total(sums)
    (middle,) = call(
        middle_kernel,
        [whole],
        [sums, back, side, dist, stream, shape, *near],
        [columns, pltpu.VMEM((cells, width), F32)],
    )
    (sums_two,) = call(
        advance_kernel, [((SUMS, cells), F32)], [face_rows, neighbours, wall_mask, sums, back]
    )
    (part,) = call(stream_last_kernel, [whole], [neighbours, wall_mask, dist, middle])
    (part,) = call(relax_kernel, [whole], [sums_two, back, middle, part, shape], [columns])
    (plane_one,) = call(
        halo_relax_kernel, [plane], [sums, notes, base, halo_shape, values], [columns]
    )
    (result,) = call(
        last_kernel,
        [whole],
        [side, part, plane_one, gate, *far],
        [pltpu.VMEM((cells, width), F32), pltpu.SemaphoreType.DMA((width // COLUMN_TILE,))],
        far_outs=True,
    )
    return result


def solution(mesh):
    return jax.shard_map(
        on_device,
        mesh=mesh,
        in_specs=(
            P("space", "vel"),
            P("space"),
            P(None, "space"),
            P(None, "space"),
            P("space", None, None),
        ),
        out_specs=P("space", "vel"),
        check_vma=False,
    )
```

time: 40.4 us -> 57.6 us (1.43)
  waiting for transfers between devices: 12.3 us -> 28.7 us
  Pallas kernels: 10.6 us -> 14.2 us
  starting transfers between devices: 15 us -> 11.7 us
    ppermute x2 -> x3, waiting for transfers between devices: 0.01 us -> 21 us  [exchange(): return [lax.ppermute(send, 'space', forward)]]
    ppermute x8 -> x4, starting transfers between devices: 11.4 us -> 6.53 us  [total(): lax.ppermute(value, 'vel', [(i, i ^ step) for i in range(count)])]
    ppermute x8 -> x4, waiting for transfers between devices: 12.3 us -> 7.71 us  [total(): lax.ppermute(value, 'vel', [(i, i ^ step) for i in range(count)])]
    pallas_call x6 -> x13, Pallas kernels: 10.6 us -> 14.2 us  [call(): pl.pallas_call(kernel, out_shape=[jax.ShapeDtypeStruct(shape, dtype) for...]
    ppermute x2 -> x3, starting transfers between devices: 3.65 us -> 5.14 us  [exchange(): return [lax.ppermute(send, 'space', forward)]]
    unnamed x10 -> x14, local copies, waits for them, and re-layouts: 2.27 us -> 2.61 us
  transfers between devices with their start and end apart: 10 -> 7, of which waited for: 8 -> 5; matrix products, arithmetic and copies ran while one was open for 0% -> 0% of each run, Pallas kernels for 5% -> 20%
where the time goes in v3:
time: 57.6 us; the launch traced here: 57.4 us
  waiting for transfers between devices  28.7 us (50%)
  Pallas kernels  14.2 us (25%)
  starting transfers between devices  11.7 us (20%)
  local copies, waits for them, and re-layouts  2.61 us (5%)
    ppermute x3, waiting for transfers between devices, exchange(): return [lax.ppermute(send, 'space', forward)]  21 us
    pallas_call x13, Pallas kernels, call(): pl.pallas_call(kernel, out_shape=[jax.ShapeDtypeStruct(shape, dtype) for...  14.2 us
    ppermute x4, waiting for transfers between devices, total(): lax.ppermute(value, 'vel', [(i, i ^ step) for i in range(count)])  7.71 us
    ppermute x4, starting transfers between devices, total(): lax.ppermute(value, 'vel', [(i, i ^ step) for i in range(count)])  6.53 us
    ppermute x3, starting transfers between devices, exchange(): return [lax.ppermute(send, 'space', forward)]  5.14 us
    unnamed x14, local copies, waits for them, and re-layouts  2.61 us
  transfers between devices with their start and end apart: 7, of which 5 were waited for; matrix products, arithmetic and copies ran while one was open for 0% of the time, Pallas kernels for 20%

profile of v3, /device:TPU:0, one launch (start us, length us, event | category | flops | bytes accessed | tf_op | source)
XLA Modules:
  0.0 57.4 jit_solution(17834198881884987070)
XLA Ops:
  0.0 0.0 copy-start.5
  0.0 0.0 copy-start.6
  0.0 0.7 %copy-done.5 = s32[1,2,64]{2,1,0:T(2,128)S(1)} copy-done((s32[1,2,64]{2,1,0:T(2,128)S(1)}, s32[1,2,64]{2,1,0:T(2,128)}, u32[]{:S(2)}) %copy-start.5) | copy-done | bytes 536
  0.7 0.0 copy-done.6
  0.7 0.0 copy-start
  0.7 1.2 %copy-done = f32[128,2048]{1,0:T(8,128)S(1)} copy-done((f32[128,2048]{1,0:T(8,128)S(1)}, f32[128,2048]{1,0:T(8,128)}, u32[]{:S(2)}) %copy-start) | copy-done | bytes 1048600
  1.9 0.0 copy-start.2
  1.9 0.7 %copy-done.2 = s32[6,128]{1,0:T(8,128)S(1)} copy-done((s32[6,128]{1,0:T(8,128)S(1)}, s32[6,128]{1,0:T(8,128)}, u32[]{:S(2)}) %copy-start.2) | copy-done | bytes 3096
  2.6 0.0 copy-start.1
  2.6 1.4 %shard_map.60 = f32[144,1024]{1,0:T(8,128)S(1)} custom-call(s32[1,2,64]{2,1,0:T(2,128)S(1)} %copy-done.5, s32[1,2,64]{2,1,0:T(2,128)S(1)} %copy-done.5, f32[1,128]{1,0:T(1,128)S(1)} %bitcast.1, s32[6,128]{1,0:T(8,128)S(1)} %copy-done.2, f32[128,2048]{1,0:T(8,128)S(1)} %copy-done), custom_call_target="tpu_custom_call" | custom-call | bytes 1053184 | tf_op jit(solution)/shard_map/pallas_call | solution.py:617
  4.0 3.0 %collective-permute-start.5 = (f32[144,1024]{1,0:T(8,128)S(1)}, f32[144,1024]{1,0:T(8,128)S(1)}, u32[]{:S(2)}, u32[]{:S(2)}) collective-permute-start(f32[144,1024]{1,0:T(8,128)S(1)} %shard_map.60), channel_id=1, source_target_pairs={{0,16},{16,0},{1,17},{17,1},{2,18},{18,2},{3,19},{19,3},{4,20},{20... | collective-permute-start | bytes 1769480 | tf_op jit(solution)/shard_map/ppermute | solution.py:642
  7.1 0.0 copy-done.1
  7.1 1.2 %shard_map.66 = f32[128,1024]{1,0:T(8,128)S(1)} custom-call(s32[1,2,64]{2,1,0:T(2,128)S(1)} %copy-done.5, f32[128,2048]{1,0:T(8,128)S(1)} %copy-done.1), custom_call_target="tpu_custom_call" | custom-call | bytes 1049088 | tf_op jit(solution)/shard_map/pallas_call | solution.py:617
  8.3 0.1 collective-permute-start.6
  8.3 1.0 %shard_map.56 = (f32[112,128]{1,0:T(8,128)S(1)}, f32[64,64]{1,0:T(8,128)S(1)}) custom-call(s32[1,2,64]{2,1,0:T(2,128)S(1)} %copy-done.5, f32[128,2048]{1,0:T(8,128)S(1)} %copy-done.1), custom_call_target="tpu_custom_call" | custom-call | bytes 1049088 | tf_op jit(solution)/shard_map/pallas_call | solution.py:617
  9.3 2.0 %collective-permute-start = (f32[64,64]{1,0:T(8,128)S(1)}, f32[64,64]{1,0:T(8,128)S(1)}, u32[]{:S(2)}, u32[]{:S(2)}) collective-permute-start(f32[64,64]{1,0:T(8,128)S(1)} %get-tuple-element.17), channel_id=1, source_target_pairs={{0,16},{16,0},{1,17},{17,1},{2,18},{18,2},{3,19},{19,3},{4,20},{20... | collective-permute-start | bytes 49160 | tf_op jit(solution)/shard_map/ppermute | solution.py:642
  11.3 21.0 %collective-permute-done.refs_0_ = f32[64,64]{1,0:T(8,128)S(1)} collective-permute-done((f32[64,64]{1,0:T(8,128)S(1)}, f32[64,64]{1,0:T(8,128)S(1)}, u32[]{:S(2)}, u32[]{:S(2)}) %collective-permute-start) | collective-permute-done | bytes 16416 | tf_op jit(solution)/shard_map/ppermute | solution.py:642
  32.3 0.1 shard_map.57
  32.4 0.0 collective-permute-start.1
  32.4 1.3 %collective-permute-done.1 = f32[144,128]{1,0:T(8,128)S(1)} collective-permute-done((f32[144,128]{1,0:T(8,128)S(1)}, f32[144,128]{1,0:T(8,128)S(1)}, u32[]{:S(2)}, u32[]{:S(2)}) %collective-permute-start.1) | collective-permute-done | bytes 73760 | tf_op jit(solution)/shard_map/ppermute | solution.py:632
  33.7 1.8 %collective-permute-start.2 = (f32[144,128]{1,0:T(8,128)S(1)}, f32[144,128]{1,0:T(8,128)S(1)}, u32[]{:S(2)}, u32[]{:S(2)}) collective-permute-start(f32[144,128]{1,0:T(8,128)S(1)} %add.12), channel_id=1, source_target_pairs={{0,2},{1,3},{2,0},{3,1},{4,6},{5,7},{6,4},{7,5},{8,10},{9,11},{10,... | collective-permute-start | bytes 221192 | tf_op jit(solution)/shard_map/ppermute | solution.py:632
  35.5 2.6 %collective-permute-done.2 = f32[144,128]{1,0:T(8,128)S(1)} collective-permute-done((f32[144,128]{1,0:T(8,128)S(1)}, f32[144,128]{1,0:T(8,128)S(1)}, u32[]{:S(2)}, u32[]{:S(2)}) %collective-permute-start.2) | collective-permute-done | bytes 73760 | tf_op jit(solution)/shard_map/ppermute | solution.py:632
  38.1 0.0 copy-start.3
  38.1 1.9 %collective-permute-start.3 = (f32[144,128]{1,0:T(8,128)S(1)}, f32[144,128]{1,0:T(8,128)S(1)}, u32[]{:S(2)}, u32[]{:S(2)}) collective-permute-start(f32[144,128]{1,0:T(8,128)S(1)} %add.13), channel_id=1, source_target_pairs={{0,4},{1,5},{2,6},{3,7},{4,0},{5,1},{6,2},{7,3},{8,12},{9,13},{10,... | collective-permute-start | bytes 221192 | tf_op jit(solution)/shard_map/ppermute | solution.py:632
  40.0 2.6 %collective-permute-done.3 = f32[144,128]{1,0:T(8,128)S(1)} collective-permute-done((f32[144,128]{1,0:T(8,128)S(1)}, f32[144,128]{1,0:T(8,128)S(1)}, u32[]{:S(2)}, u32[]{:S(2)}) %collective-permute-start.3) | collective-permute-done | bytes 73760 | tf_op jit(solution)/shard_map/ppermute | solution.py:632
  42.6 0.0 copy-start.4
  42.6 2.9 %collective-permute-start.4 = (f32[144,128]{1,0:T(8,128)S(1)}, f32[144,128]{1,0:T(8,128)S(1)}, u32[]{:S(2)}, u32[]{:S(2)}) collective-permute-start(f32[144,128]{1,0:T(8,128)S(1)} %add.14), channel_id=1, source_target_pairs={{0,8},{1,9},{2,10},{3,11},{4,12},{5,13},{6,14},{7,15},{8,0},{9,1},... | collective-permute-start | bytes 221192 | tf_op jit(solution)/shard_map/ppermute | solution.py:632
  45.5 0.0 copy-done.3
  45.5 0.3 shard_map.55
  45.8 0.0 copy-done.4
  45.8 0.8 %shard_map.59.stream_ref = f32[128,2048]{1,0:T(8,128)S(1)} custom-call(s32[6,128]{1,0:T(8,128)S(1)} %copy-done.4, s32[6,128]{1,0:T(8,128)S(1)} %copy-done.3, f32[128,2048]{1,0:T(8,128)S(1)} %copy-done.1), custom_call_target="tpu_custom_call" | custom-call | bytes 1054720 | tf_op jit(solution)/shard_map/pallas_call | solution.py:617
  46.6 1.3 %collective-permute-done.4 = f32[144,128]{1,0:T(8,128)S(1)} collective-permute-done((f32[144,128]{1,0:T(8,128)S(1)}, f32[144,128]{1,0:T(8,128)S(1)}, u32[]{:S(2)}, u32[]{:S(2)}) %collective-permute-start.4) | collective-permute-done | bytes 73760 | tf_op jit(solution)/shard_map/ppermute | solution.py:632
  47.9 0.5 shard_map.58.sums_ref
  48.4 0.0 collective-permute-done.5.refs_0_
  48.4 2.1 %shard_map.61.middle_ref = f32[128,2048]{1,0:T(8,128)S(1)} custom-call(f32[144,128]{1,0:T(8,128)S(1)} %add.15.sums_ref, f32[8,128]{1,0:T(8,128)S(1)} %get-tuple-element.18.back_ref, bf16[256,128]{1,0:T(8,128)(2,1)S(1)} %get-tuple-element.15.side_ref, f32[128,2048]{1,0:T(8,128)S(1)} %copy-done.1, f32[128,2048]{1,0:T(8,128)S(1)} %shard_map.59.stream_ref, ...), custom_call_target="tpu_custom_call" | custom-call | bytes 3944448 | tf_op jit(solution)/shard_map/pallas_call | solution.py:617
  50.5 0.9 %shard_map.62.part_ref = f32[128,2048]{1,0:T(8,128)S(1)} custom-call(s32[6,128]{1,0:T(8,128)S(1)} %copy-done.4, s32[6,128]{1,0:T(8,128)S(1)} %copy-done.3, f32[128,2048]{1,0:T(8,128)S(1)} %copy-done.1, f32[128,2048]{1,0:T(8,128)S(1)} %shard_map.61.middle_ref), custom_call_target="tpu_custom_call" | custom-call | bytes 2103296 | tf_op jit(solution)/shard_map/pallas_call | solution.py:617
  51.5 2.0 %shard_map.63.part_ref = f32[128,2048]{1,0:T(8,128)S(1)} custom-call(f32[16,128]{1,0:T(8,128)S(1)} %shard_map.58.sums_ref, f32[8,128]{1,0:T(8,128)S(1)} %get-tuple-element.18.back_ref, f32[128,2048]{1,0:T(8,128)S(1)} %shard_map.61.middle_ref, f32[128,2048]{1,0:T(8,128)S(1)} %shard_map.62.part_ref, f32[128,2048]{1,0:T(8,128)S(1)} %get-tuple-element.19.shape_ref), custom_call_target="tpu_custom_call" | custom-call | bytes 3158016 | tf_op jit(solution)/shard_map/pallas_call | solution.py:617
  53.5 1.0 %shard_map.64 = (f32[128,1024]{1,0:T(8,128)S(1)}, f32[128,1024]{1,0:T(8,128)S(1)}, f32[128,1024]{1,0:T(8,128)S(1)}, f32[8,128]{1,0:T(8,128)S(1)}, f32[128,128]{1,0:T(8,128)S(1)}) custom-call(s32[1,2,64]{2,1,0:T(2,128)S(1)} %copy-done.5, s32[6,128]{1,0:T(8,128)S(1)} %copy-done.4, f32[144,1024]{1,0:T(8,128)S(1)} %collective-permute-done.5.refs_0_), custom_call_target="tpu_custom_call" | custom-call | bytes 593408 | tf_op jit(solution)/shard_map/pallas_call | solution.py:617
  54.4 1.7 %shard_map.65.plane_ref = f32[128,1024]{1,0:T(8,128)S(1)} custom-call(f32[144,128]{1,0:T(8,128)S(1)} %add.15.sums_ref, f32[8,128]{1,0:T(8,128)S(1)} %get-tuple-element.20.notes_ref, f32[128,1024]{1,0:T(8,128)S(1)} %get-tuple-element.21.base_ref, f32[128,1024]{1,0:T(8,128)S(1)} %get-tuple-element.22.shape_ref, f32[128,1024]{1,0:T(8,128)S(1)} %get-tuple-element.23.values_ref), custom_call_target="tpu_custom_call" | custom-call | bytes 1650688 | tf_op jit(solution)/shard_map/pallas_call | solution.py:617
  56.1 0.0 collective-permute-done.6.refs_0_
  56.1 1.3 %shard_map.67 = f32[128,2048]{1,0:T(8,128)} custom-call(bf16[256,128]{1,0:T(8,128)(2,1)S(1)} %get-tuple-element.15.side_ref, f32[128,2048]{1,0:T(8,128)S(1)} %shard_map.63.part_ref, f32[128,1024]{1,0:T(8,128)S(1)} %shard_map.65.plane_ref, f32[128,128]{1,0:T(8,128)S(1)} %get-tuple-element.24.open_ref, f32[128,1024]{1,0:T(8,128)S(1)} %collective-permute-done.6.refs_0_), custom_call_target="tpu_custom_call" | custom-call | bytes 2293760 | tf_op jit(solution)/shard_map/pallas_call | solution.py:617
  (4 shorter events, 0.0 us)
Async XLA Ops:
  0.0 0.7 %copy-start.5 = (s32[1,2,64]{2,1,0:T(2,128)S(1)}, s32[1,2,64]{2,1,0:T(2,128)}, u32[]{:S(2)}) copy-start(s32[1,2,64]{2,1,0:T(2,128)} %rows_ref.3) | copy-start | bytes 1540
  0.0 0.7 %copy-start.6 = (f32[128]{0:T(128)S(1)}, f32[128]{0:T(128)}, u32[]{:S(2)}) copy-start(f32[128]{0:T(128)} %param.6) | copy-start | bytes 1540
  0.7 1.2 %copy-start = (f32[128,2048]{1,0:T(8,128)S(1)}, f32[128,2048]{1,0:T(8,128)}, u32[]{:S(2)}) copy-start(f32[128,2048]{1,0:T(8,128)} %dist_ref.7) | copy-start | bytes 3145732
  1.9 0.7 %copy-start.2 = (s32[6,128]{1,0:T(8,128)S(1)}, s32[6,128]{1,0:T(8,128)}, u32[]{:S(2)}) copy-start(s32[6,128]{1,0:T(8,128)} %mask_ref.9) | copy-start | bytes 9220
  2.6 4.5 %copy-start.1 = (f32[128,2048]{1,0:T(8,128)S(1)}, f32[128,2048]{1,0:T(8,128)}, u32[]{:S(2)}) copy-start(f32[128,2048]{1,0:T(8,128)} %dist_ref.7) | copy-start | bytes 3145732
  4.0 44.4 %collective-permute-start.5 = (f32[144,1024]{1,0:T(8,128)S(1)}, f32[144,1024]{1,0:T(8,128)S(1)}, u32[]{:S(2)}, u32[]{:S(2)}) collective-permute-start(f32[144,1024]{1,0:T(8,128)S(1)} %shard_map.60), channel_id=1, source_target_pairs={{0,16},{16,0},{1,17},{17,1},{2,18},{18,2},{3,19},{19,3},{4,20},{20... | collective-permute-start | bytes 1769480 | tf_op jit(solution)/shard_map/ppermute | solution.py:642
  8.3 47.9 %collective-permute-start.6 = (f32[128,1024]{1,0:T(8,128)S(1)}, f32[128,1024]{1,0:T(8,128)S(1)}, u32[]{:S(2)}, u32[]{:S(2)}) collective-permute-start(f32[128,1024]{1,0:T(8,128)S(1)} %shard_map.66), channel_id=1, source_target_pairs={{0,16},{16,0},{1,17},{17,1},{2,18},{18,2},{3,19},{19,3},{4,20},{20... | collective-permute-start | bytes 1572872 | tf_op jit(solution)/shard_map/ppermute | solution.py:642
  9.3 23.0 %collective-permute-start = (f32[64,64]{1,0:T(8,128)S(1)}, f32[64,64]{1,0:T(8,128)S(1)}, u32[]{:S(2)}, u32[]{:S(2)}) collective-permute-start(f32[64,64]{1,0:T(8,128)S(1)} %get-tuple-element.17), channel_id=1, source_target_pairs={{0,16},{16,0},{1,17},{17,1},{2,18},{18,2},{3,19},{19,3},{4,20},{20... | collective-permute-start | bytes 49160 | tf_op jit(solution)/shard_map/ppermute | solution.py:642
  32.4 1.3 %collective-permute-start.1 = (f32[144,128]{1,0:T(8,128)S(1)}, f32[144,128]{1,0:T(8,128)S(1)}, u32[]{:S(2)}, u32[]{:S(2)}) collective-permute-start(f32[144,128]{1,0:T(8,128)S(1)} %shard_map.57), channel_id=1, source_target_pairs={{0,1},{1,0},{2,3},{3,2},{4,5},{5,4},{6,7},{7,6},{8,9},{9,8},{10,11... | collective-permute-start | bytes 221192 | tf_op jit(solution)/shard_map/ppermute | solution.py:632
  33.7 4.4 %collective-permute-start.2 = (f32[144,128]{1,0:T(8,128)S(1)}, f32[144,128]{1,0:T(8,128)S(1)}, u32[]{:S(2)}, u32[]{:S(2)}) collective-permute-start(f32[144,128]{1,0:T(8,128)S(1)} %add.12), channel_id=1, source_target_pairs={{0,2},{1,3},{2,0},{3,1},{4,6},{5,7},{6,4},{7,5},{8,10},{9,11},{10,... | collective-permute-start | bytes 221192 | tf_op jit(solution)/shard_map/ppermute | solution.py:632
  38.1 7.3 %copy-start.3 = (s32[6,128]{1,0:T(8,128)S(1)}, s32[6,128]{1,0:T(8,128)}, u32[]{:S(2)}) copy-start(s32[6,128]{1,0:T(8,128)} %mask_ref.9) | copy-start | bytes 9220
  38.1 4.4 %collective-permute-start.3 = (f32[144,128]{1,0:T(8,128)S(1)}, f32[144,128]{1,0:T(8,128)S(1)}, u32[]{:S(2)}, u32[]{:S(2)}) collective-permute-start(f32[144,128]{1,0:T(8,128)S(1)} %add.13), channel_id=1, source_target_pairs={{0,4},{1,5},{2,6},{3,7},{4,0},{5,1},{6,2},{7,3},{8,12},{9,13},{10,... | collective-permute-start | bytes 221192 | tf_op jit(solution)/shard_map/ppermute | solution.py:632
  42.6 3.2 %copy-start.4 = (s32[6,128]{1,0:T(8,128)S(1)}, s32[6,128]{1,0:T(8,128)}, u32[]{:S(2)}) copy-start(s32[6,128]{1,0:T(8,128)} %near_ref.7) | copy-start | bytes 9220
  42.6 5.3 %collective-permute-start.4 = (f32[144,128]{1,0:T(8,128)S(1)}, f32[144,128]{1,0:T(8,128)S(1)}, u32[]{:S(2)}, u32[]{:S(2)}) collective-permute-start(f32[144,128]{1,0:T(8,128)S(1)} %add.14), channel_id=1, source_target_pairs={{0,8},{1,9},{2,10},{3,11},{4,12},{5,13},{6,14},{7,15},{8,0},{9,1},... | collective-permute-start | bytes 221192 | tf_op jit(solution)/shard_map/ppermute | solution.py:632

commit v4 on v3

--- a/solution.py
+++ b/solution.py
@@ -607,7 +607,7 @@
         copy.wait()
 
 
-def call(kernel, outs, arrays, scratch=(), scalars=0, far_outs=False, flops=0):
+def call(kernel, outs, arrays, scratch=(), scalars=0, far_outs=False):
     specs = [
         pl.BlockSpec(memory_space=pltpu.SMEM if at < scalars else pltpu.VMEM)
         for at in range(len(arrays))
@@ -620,9 +620,13 @@
         in_specs=specs,
         out_specs=[pl.BlockSpec(memory_space=out_space)] * len(outs),
         scratch_shapes=list(scratch),
+        name=kernel.__name__,
         compiler_params=pltpu.CompilerParams(vmem_limit_bytes=40 * 2**20),
-        cost_estimate=pl.CostEstimate(flops=flops, bytes_accessed=size, transcendentals=0),
+        cost_estimate=pl.CostEstimate(flops=COST.get(kernel.__name__, 0), bytes_accessed=size, transcendentals=0),
     )(*arrays)
+
+
+COST = {"advance_kernel": 3 * 10**9}
 
 
 def total(value):

time: 57.6 us -> 35.1 us (0.61)
  waiting for transfers between devices: 28.7 us -> 7.17 us
  local copies, waits for them, and re-layouts: 2.61 us -> 1.92 us
    ppermute x3, waiting for transfers between devices: 21 us -> 0.01 us  [exchange(): return [lax.ppermute(send, 'space', forward)]]
    unnamed x14 -> x12, local copies, waits for them, and re-layouts: 2.61 us -> 1.92 us
    ppermute x4, starting transfers between devices: 6.53 us -> 5.86 us  [total(): lax.ppermute(value, 'vel', [(i, i ^ step) for i in range(count)])]
  transfers between devices with their start and end apart: 7 -> 7, of which waited for: 5 -> 3; matrix products, arithmetic and copies ran while one was open for 0% -> 0% of each run, Pallas kernels for 20% -> 34%
where the time goes in v4:
time: 35.1 us; the launch traced here: 34.9 us
  Pallas kernels  14.2 us (40%)
  starting transfers between devices  11.4 us (32%)
  waiting for transfers between devices  7.17 us (20%)
  local copies, waits for them, and re-layouts  1.92 us (5%)
    pallas_call x13, Pallas kernels, call(): pl.pallas_call(kernel, out_shape=[jax.ShapeDtypeStruct(shape, dtype) for...  14.2 us
    ppermute x4, waiting for transfers between devices, total(): lax.ppermute(value, 'vel', [(i, i ^ step) for i in range(count)])  7.17 us
    ppermute x4, starting transfers between devices, total(): lax.ppermute(value, 'vel', [(i, i ^ step) for i in range(count)])  5.86 us
    ppermute x3, starting transfers between devices, exchange(): return [lax.ppermute(send, 'space', forward)]  5.51 us
    unnamed x12, local copies, waits for them, and re-layouts  1.92 us
  transfers between devices with their start and end apart: 7, of which 3 were waited for; matrix products, arithmetic and copies ran while one was open for 0% of the time, Pallas kernels for 34%

profile of v4, /device:TPU:0, one launch (start us, length us, event | category | flops | bytes accessed | tf_op | source)
XLA Modules:
  0.0 34.9 jit_solution(2852964200455467548)
XLA Ops:
  0.0 0.0 copy-start
  0.0 1.2 %copy-done = f32[128,2048]{1,0:T(8,128)S(1)} copy-done((f32[128,2048]{1,0:T(8,128)S(1)}, f32[128,2048]{1,0:T(8,128)}, u32[]{:S(2)}) %copy-start) | copy-done | bytes 1048600
  1.2 0.0 copy-start.4
  1.2 0.7 %copy-done.4 = s32[1,2,64]{2,1,0:T(2,128)S(1)} copy-done((s32[1,2,64]{2,1,0:T(2,128)S(1)}, s32[1,2,64]{2,1,0:T(2,128)}, u32[]{:S(2)}) %copy-start.4) | copy-done | bytes 536
  1.9 0.0 copy-start.1
  1.9 0.0 copy-start.2
  1.9 1.0 %sums_kernel.1 = (f32[112,128]{1,0:T(8,128)S(1)}, f32[64,64]{1,0:T(8,128)S(1)}) custom-call(s32[1,2,64]{2,1,0:T(2,128)S(1)} %copy-done.4, f32[128,2048]{1,0:T(8,128)S(1)} %copy-done), custom_call_target="tpu_custom_call" | custom-call | bytes 1049088 | tf_op jit(solution)/shard_map/sums_kernel/pallas_call | solution.py:617
  2.9 0.0 copy-start.5
  2.9 3.0 %collective-permute-start = (f32[64,64]{1,0:T(8,128)S(1)}, f32[64,64]{1,0:T(8,128)S(1)}, u32[]{:S(2)}, u32[]{:S(2)}) collective-permute-start(f32[64,64]{1,0:T(8,128)S(1)} %get-tuple-element.17), channel_id=1, source_target_pairs={{0,16},{16,0},{1,17},{17,1},{2,18},{18,2},{3,19},{19,3},{4,20},{20... | collective-permute-start | bytes 49160 | tf_op jit(solution)/shard_map/ppermute | solution.py:646
  5.9 0.0 copy-done.1
  5.9 0.0 copy-done.2
  5.9 0.0 copy-done.5
  5.9 1.4 %near_plane_kernel.1 = f32[144,1024]{1,0:T(8,128)S(1)} custom-call(s32[1,2,64]{2,1,0:T(2,128)S(1)} %copy-done.4, s32[1,2,64]{2,1,0:T(2,128)S(1)} %copy-done.4, f32[1,128]{1,0:T(1,128)S(1)} %bitcast.1, s32[6,128]{1,0:T(8,128)S(1)} %copy-done.2, f32[128,2048]{1,0:T(8,128)S(1)} %copy-done.1), custom_call_target="tpu_custom_call" | custom-call | bytes 1053184 | tf_op jit(solution)/shard_map/near_plane_kernel/pallas_call | solution.py:617
  7.3 0.8 %collective-permute-start.5 = (f32[144,1024]{1,0:T(8,128)S(1)}, f32[144,1024]{1,0:T(8,128)S(1)}, u32[]{:S(2)}, u32[]{:S(2)}) collective-permute-start(f32[144,1024]{1,0:T(8,128)S(1)} %near_plane_kernel.1), channel_id=1, source_target_pairs={{0,16},{16,0},{1,17},{17,1},{2,18},{18,2},{3,19},{19,3},{4,20},{20... | collective-permute-start | bytes 1769480 | tf_op jit(solution)/shard_map/ppermute | solution.py:646
  8.1 0.0 collective-permute-done.refs_0_
  8.1 0.1 gather_kernel.1
  8.2 0.0 collective-permute-start.1
  8.2 1.2 %far_plane_kernel.1 = f32[128,1024]{1,0:T(8,128)S(1)} custom-call(s32[1,2,64]{2,1,0:T(2,128)S(1)} %copy-done.4, f32[128,2048]{1,0:T(8,128)S(1)} %copy-done.1), custom_call_target="tpu_custom_call" | custom-call | bytes 1049088 | tf_op jit(solution)/shard_map/far_plane_kernel/pallas_call | solution.py:617
  9.4 1.8 %collective-permute-start.6 = (f32[128,1024]{1,0:T(8,128)S(1)}, f32[128,1024]{1,0:T(8,128)S(1)}, u32[]{:S(2)}, u32[]{:S(2)}) collective-permute-start(f32[128,1024]{1,0:T(8,128)S(1)} %far_plane_kernel.1), channel_id=1, source_target_pairs={{0,16},{16,0},{1,17},{17,1},{2,18},{18,2},{3,19},{19,3},{4,20},{20... | collective-permute-start | bytes 1572872 | tf_op jit(solution)/shard_map/ppermute | solution.py:646
  11.1 0.0 collective-permute-done.1
  11.1 1.6 %collective-permute-start.2 = (f32[144,128]{1,0:T(8,128)S(1)}, f32[144,128]{1,0:T(8,128)S(1)}, u32[]{:S(2)}, u32[]{:S(2)}) collective-permute-start(f32[144,128]{1,0:T(8,128)S(1)} %add.12), channel_id=1, source_target_pairs={{0,2},{1,3},{2,0},{3,1},{4,6},{5,7},{6,4},{7,5},{8,10},{9,11},{10,... | collective-permute-start | bytes 221192 | tf_op jit(solution)/shard_map/ppermute | solution.py:636
  12.7 2.9 %collective-permute-done.2 = f32[144,128]{1,0:T(8,128)S(1)} collective-permute-done((f32[144,128]{1,0:T(8,128)S(1)}, f32[144,128]{1,0:T(8,128)S(1)}, u32[]{:S(2)}, u32[]{:S(2)}) %collective-permute-start.2) | collective-permute-done | bytes 73760 | tf_op jit(solution)/shard_map/ppermute | solution.py:636
  15.6 1.6 %collective-permute-start.3 = (f32[144,128]{1,0:T(8,128)S(1)}, f32[144,128]{1,0:T(8,128)S(1)}, u32[]{:S(2)}, u32[]{:S(2)}) collective-permute-start(f32[144,128]{1,0:T(8,128)S(1)} %add.13), channel_id=1, source_target_pairs={{0,4},{1,5},{2,6},{3,7},{4,0},{5,1},{6,2},{7,3},{8,12},{9,13},{10,... | collective-permute-start | bytes 221192 | tf_op jit(solution)/shard_map/ppermute | solution.py:636
  17.2 2.8 %collective-permute-done.3 = f32[144,128]{1,0:T(8,128)S(1)} collective-permute-done((f32[144,128]{1,0:T(8,128)S(1)}, f32[144,128]{1,0:T(8,128)S(1)}, u32[]{:S(2)}, u32[]{:S(2)}) %collective-permute-start.3) | collective-permute-done | bytes 73760 | tf_op jit(solution)/shard_map/ppermute | solution.py:636
  20.0 0.0 copy-start.3
  20.1 2.7 %collective-permute-start.4 = (f32[144,128]{1,0:T(8,128)S(1)}, f32[144,128]{1,0:T(8,128)S(1)}, u32[]{:S(2)}, u32[]{:S(2)}) collective-permute-start(f32[144,128]{1,0:T(8,128)S(1)} %add.14), channel_id=1, source_target_pairs={{0,8},{1,9},{2,10},{3,11},{4,12},{5,13},{6,14},{7,15},{8,0},{9,1},... | collective-permute-start | bytes 221192 | tf_op jit(solution)/shard_map/ppermute | solution.py:636
  22.7 0.3 wall_kernel.1
  23.0 0.0 copy-done.3
  23.0 0.8 %stream_kernel.1.stream_ref = f32[128,2048]{1,0:T(8,128)S(1)} custom-call(s32[6,128]{1,0:T(8,128)S(1)} %copy-done.3, s32[6,128]{1,0:T(8,128)S(1)} %copy-done.2, f32[128,2048]{1,0:T(8,128)S(1)} %copy-done.1), custom_call_target="tpu_custom_call" | custom-call | bytes 1054720 | tf_op jit(solution)/shard_map/stream_kernel/pallas_call | solution.py:617
  23.9 1.5 %collective-permute-done.4 = f32[144,128]{1,0:T(8,128)S(1)} collective-permute-done((f32[144,128]{1,0:T(8,128)S(1)}, f32[144,128]{1,0:T(8,128)S(1)}, u32[]{:S(2)}, u32[]{:S(2)}) %collective-permute-start.4) | collective-permute-done | bytes 73760 | tf_op jit(solution)/shard_map/ppermute | solution.py:636
  25.4 0.5 %advance_kernel.1.sums_ref = f32[16,128]{1,0:T(8,128)S(1)} custom-call(s32[1,2,64]{2,1,0:T(2,128)S(1)} %copy-done.4, s32[6,128]{1,0:T(8,128)S(1)} %copy-done.3, s32[6,128]{1,0:T(8,128)S(1)} %copy-done.2, f32[144,128]{1,0:T(8,128)S(1)} %add.15.sums_ref, f32[8,128]{1,0:T(8,128)S(1)} %get-tuple-element.18.back_ref), custom_call_target="tpu_custom_call" | custom-call | flops 3000000000 | bytes 84480 | tf_op jit(solution)/shard_map/advance_kernel/pallas_call | solution.py:617
  25.9 0.0 collective-permute-done.5.refs_0_
  25.9 2.1 %middle_kernel.1.middle_ref = f32[128,2048]{1,0:T(8,128)S(1)} custom-call(f32[144,128]{1,0:T(8,128)S(1)} %add.15.sums_ref, f32[8,128]{1,0:T(8,128)S(1)} %get-tuple-element.18.back_ref, bf16[256,128]{1,0:T(8,128)(2,1)S(1)} %get-tuple-element.15.side_ref, f32[128,2048]{1,0:T(8,128)S(1)} %copy-done.1, f32[128,2048]{1,0:T(8,128)S(1)} %stream_kernel.1.stream_ref, ...), custom_call_target="tpu_custom_call" | custom-call | bytes 3944448 | tf_op jit(solution)/shard_map/middle_kernel/pallas_call | solution.py:617
  28.0 0.9 %stream_last_kernel.1.part_ref = f32[128,2048]{1,0:T(8,128)S(1)} custom-call(s32[6,128]{1,0:T(8,128)S(1)} %copy-done.3, s32[6,128]{1,0:T(8,128)S(1)} %copy-done.2, f32[128,2048]{1,0:T(8,128)S(1)} %copy-done.1, f32[128,2048]{1,0:T(8,128)S(1)} %middle_kernel.1.middle_ref), custom_call_target="tpu_custom_call" | custom-call | bytes 2103296 | tf_op jit(solution)/shard_map/stream_last_kernel/pallas_call | solution.py:617
  28.9 2.0 %relax_kernel.1.part_ref = f32[128,2048]{1,0:T(8,128)S(1)} custom-call(f32[16,128]{1,0:T(8,128)S(1)} %advance_kernel.1.sums_ref, f32[8,128]{1,0:T(8,128)S(1)} %get-tuple-element.18.back_ref, f32[128,2048]{1,0:T(8,128)S(1)} %middle_kernel.1.middle_ref, f32[128,2048]{1,0:T(8,128)S(1)} %stream_last_kernel.1.part_ref, f32[128,2048]{1,0:T(8,128)S(1)} %get-tuple-element.19.shape_ref), custom_call_target="tpu_custom_call" | custom-call | bytes 3158016 | tf_op jit(solution)/shard_map/relax_kernel/pallas_call | solution.py:617
  30.9 1.0 %halo_stream_kernel.1 = (f32[128,1024]{1,0:T(8,128)S(1)}, f32[128,1024]{1,0:T(8,128)S(1)}, f32[128,1024]{1,0:T(8,128)S(1)}, f32[8,128]{1,0:T(8,128)S(1)}, f32[128,128]{1,0:T(8,128)S(1)}) custom-call(s32[1,2,64]{2,1,0:T(2,128)S(1)} %copy-done.4, s32[6,128]{1,0:T(8,128)S(1)} %copy-done.3, f32[144,1024]{1,0:T(8,128)S(1)} %collective-permute-done.5.refs_0_), custom_call_target="tpu_custom_call" | custom-call | bytes 593408 | tf_op jit(solution)/shard_map/halo_stream_kernel/pallas_call | solution.py:617
  31.9 1.7 %halo_relax_kernel.1.plane_ref = f32[128,1024]{1,0:T(8,128)S(1)} custom-call(f32[144,128]{1,0:T(8,128)S(1)} %add.15.sums_ref, f32[8,128]{1,0:T(8,128)S(1)} %get-tuple-element.20.notes_ref, f32[128,1024]{1,0:T(8,128)S(1)} %get-tuple-element.21.base_ref, f32[128,1024]{1,0:T(8,128)S(1)} %get-tuple-element.22.shape_ref, f32[128,1024]{1,0:T(8,128)S(1)} %get-tuple-element.23.values_ref), custom_call_target="tpu_custom_call" | custom-call | bytes 1650688 | tf_op jit(solution)/shard_map/halo_relax_kernel/pallas_call | solution.py:617
  33.6 0.0 collective-permute-done.6.refs_0_
  33.6 1.3 %last_kernel.1 = f32[128,2048]{1,0:T(8,128)} custom-call(bf16[256,128]{1,0:T(8,128)(2,1)S(1)} %get-tuple-element.15.side_ref, f32[128,2048]{1,0:T(8,128)S(1)} %relax_kernel.1.part_ref, f32[128,1024]{1,0:T(8,128)S(1)} %halo_relax_kernel.1.plane_ref, f32[128,128]{1,0:T(8,128)S(1)} %get-tuple-element.24.open_ref, f32[128,1024]{1,0:T(8,128)S(1)} %collective-permute-done.6.refs_0_), custom_call_target="tpu_custom_call" | custom-call | bytes 2293760 | tf_op jit(solution)/shard_map/last_kernel/pallas_call | solution.py:617
  (4 shorter events, 0.0 us)
Async XLA Ops:
  0.0 1.2 %copy-start = (f32[128,2048]{1,0:T(8,128)S(1)}, f32[128,2048]{1,0:T(8,128)}, u32[]{:S(2)}) copy-start(f32[128,2048]{1,0:T(8,128)} %dist_ref.7) | copy-start | bytes 3145732
  1.2 0.7 %copy-start.4 = (s32[1,2,64]{2,1,0:T(2,128)S(1)}, s32[1,2,64]{2,1,0:T(2,128)}, u32[]{:S(2)}) copy-start(s32[1,2,64]{2,1,0:T(2,128)} %rows_ref.3) | copy-start | bytes 1540
  1.9 4.0 %copy-start.1 = (f32[128,2048]{1,0:T(8,128)S(1)}, f32[128,2048]{1,0:T(8,128)}, u32[]{:S(2)}) copy-start(f32[128,2048]{1,0:T(8,128)} %dist_ref.7) | copy-start | bytes 3145732
  1.9 4.0 %copy-start.2 = (s32[6,128]{1,0:T(8,128)S(1)}, s32[6,128]{1,0:T(8,128)}, u32[]{:S(2)}) copy-start(s32[6,128]{1,0:T(8,128)} %mask_ref.9) | copy-start | bytes 9220
  2.9 3.0 %copy-start.5 = (f32[128]{0:T(128)S(1)}, f32[128]{0:T(128)}, u32[]{:S(2)}) copy-start(f32[128]{0:T(128)} %param.6) | copy-start | bytes 1540
  2.9 5.2 %collective-permute-start = (f32[64,64]{1,0:T(8,128)S(1)}, f32[64,64]{1,0:T(8,128)S(1)}, u32[]{:S(2)}, u32[]{:S(2)}) collective-permute-start(f32[64,64]{1,0:T(8,128)S(1)} %get-tuple-element.17), channel_id=1, source_target_pairs={{0,16},{16,0},{1,17},{17,1},{2,18},{18,2},{3,19},{19,3},{4,20},{20... | collective-permute-start | bytes 49160 | tf_op jit(solution)/shard_map/ppermute | solution.py:646
  7.3 18.6 %collective-permute-start.5 = (f32[144,1024]{1,0:T(8,128)S(1)}, f32[144,1024]{1,0:T(8,128)S(1)}, u32[]{:S(2)}, u32[]{:S(2)}) collective-permute-start(f32[144,1024]{1,0:T(8,128)S(1)} %near_plane_kernel.1), channel_id=1, source_target_pairs={{0,16},{16,0},{1,17},{17,1},{2,18},{18,2},{3,19},{19,3},{4,20},{20... | collective-permute-start | bytes 1769480 | tf_op jit(solution)/shard_map/ppermute | solution.py:646
  8.2 3.0 %collective-permute-start.1 = (f32[144,128]{1,0:T(8,128)S(1)}, f32[144,128]{1,0:T(8,128)S(1)}, u32[]{:S(2)}, u32[]{:S(2)}) collective-permute-start(f32[144,128]{1,0:T(8,128)S(1)} %gather_kernel.1), channel_id=1, source_target_pairs={{0,1},{1,0},{2,3},{3,2},{4,5},{5,4},{6,7},{7,6},{8,9},{9,8},{10,11... | collective-permute-start | bytes 221192 | tf_op jit(solution)/shard_map/ppermute | solution.py:636
  9.4 24.2 %collective-permute-start.6 = (f32[128,1024]{1,0:T(8,128)S(1)}, f32[128,1024]{1,0:T(8,128)S(1)}, u32[]{:S(2)}, u32[]{:S(2)}) collective-permute-start(f32[128,1024]{1,0:T(8,128)S(1)} %far_plane_kernel.1), channel_id=1, source_target_pairs={{0,16},{16,0},{1,17},{17,1},{2,18},{18,2},{3,19},{19,3},{4,20},{20... | collective-permute-start | bytes 1572872 | tf_op jit(solution)/shard_map/ppermute | solution.py:646
  11.1 4.5 %collective-permute-start.2 = (f32[144,128]{1,0:T(8,128)S(1)}, f32[144,128]{1,0:T(8,128)S(1)}, u32[]{:S(2)}, u32[]{:S(2)}) collective-permute-start(f32[144,128]{1,0:T(8,128)S(1)} %add.12), channel_id=1, source_target_pairs={{0,2},{1,3},{2,0},{3,1},{4,6},{5,7},{6,4},{7,5},{8,10},{9,11},{10,... | collective-permute-start | bytes 221192 | tf_op jit(solution)/shard_map/ppermute | solution.py:636
  15.6 4.4 %collective-permute-start.3 = (f32[144,128]{1,0:T(8,128)S(1)}, f32[144,128]{1,0:T(8,128)S(1)}, u32[]{:S(2)}, u32[]{:S(2)}) collective-permute-start(f32[144,128]{1,0:T(8,128)S(1)} %add.13), channel_id=1, source_target_pairs={{0,4},{1,5},{2,6},{3,7},{4,0},{5,1},{6,2},{7,3},{8,12},{9,13},{10,... | collective-permute-start | bytes 221192 | tf_op jit(solution)/shard_map/ppermute | solution.py:636
  20.0 3.0 %copy-start.3 = (s32[6,128]{1,0:T(8,128)S(1)}, s32[6,128]{1,0:T(8,128)}, u32[]{:S(2)}) copy-start(s32[6,128]{1,0:T(8,128)} %near_ref.7) | copy-start | bytes 9220
  20.1 5.3 %collective-permute-start.4 = (f32[144,128]{1,0:T(8,128)S(1)}, f32[144,128]{1,0:T(8,128)S(1)}, u32[]{:S(2)}, u32[]{:S(2)}) collective-permute-start(f32[144,128]{1,0:T(8,128)S(1)} %add.14), channel_id=1, source_target_pairs={{0,8},{1,9},{2,10},{3,11},{4,12},{5,13},{6,14},{7,15},{8,0},{9,1},... | collective-permute-start | bytes 221192 | tf_op jit(solution)/shard_map/ppermute | solution.py:636

commit v5 on v3

--- a/solution.py
+++ b/solution.py
@@ -24,6 +24,7 @@
 SUMS = 16
 FACES = 6
 NOTES = 8
+PARTS = 2
 BEND = 2.5 * math.log2(math.e)
 LOG2E = math.log2(math.e)
 F32 = jnp.float32
@@ -100,8 +101,8 @@
     return [jnp.where(row == face_ref[0, side : side + 1, :], 1.0, 0.0) for side in range(2)]
 
 
-def sums_kernel(face_ref, dist_ref, sums_ref, send_ref):
-    cells, width = dist_ref.shape
+def sums_kernel(dist_ref, sums_ref):
+    width = dist_ref.shape[1]
     planes, _ = planes_y(width)
     total = None
     for start in range(0, width, HALF):
@@ -122,10 +123,14 @@
         part = jnp.concatenate([part[:SUMS] + one[2 * rows :], part[SUMS:]], axis=0)
         total = part if total is None else total + part
     sums_ref[...] = total
-    low, high = face_hits(face_ref, cells)
-    base, from_low, from_high = total[:SUMS], total[SUMS : 2 * SUMS], total[2 * SUMS : 3 * SUMS]
-    upward = exact(jnp.concatenate([base, from_low], axis=0), high.astype(BF16))
-    downward = exact(jnp.concatenate([base, from_high], axis=0), low.astype(BF16))
+
+
+def share_kernel(face_ref, sums_ref, notes_ref, send_ref):
+    low, high = face_hits(face_ref, sums_ref.shape[1])
+    total, notes = sums_ref[: 3 * SUMS], notes_ref[...]
+    base, from_low, from_high = total[:SUMS], total[SUMS : 2 * SUMS], total[2 * SUMS :]
+    upward = exact(jnp.concatenate([base, from_low, notes], axis=0), high.astype(BF16))
+    downward = exact(jnp.concatenate([base, from_high, notes], axis=0), low.astype(BF16))
     send_ref[...] = jnp.concatenate([upward, downward], axis=0)
 
 
@@ -137,33 +142,34 @@
     return refs[0][side * half + start : side * half + stop]
 
 
-def gather_kernel(sums_ref, *refs):
-    halo_refs, out_ref = refs[:-1], refs[-1]
-    rows = sums_ref.shape[0]
-    out_ref[:rows, :] = sums_ref[...]
-    out_ref[rows:, :] = jnp.concatenate([halo_rows(halo_refs, 0), halo_rows(halo_refs, 1)], axis=1)
-
-def half_slices(width):
-    low, high = [], []
-    for plane in range(width // PLANE):
-        low.append((plane * PLANE, plane * HALF))
-        high.append((plane * PLANE + HALF, plane * HALF))
-    return low, high
-
-
-def move_rows(rows_ref, plane, value_ref, send_ref, side, first):
+def shared_rows(refs, start, stop):
+    rows = slice(start, stop)
+    return jnp.concatenate([halo_rows(refs, 0, rows), halo_rows(refs, 1, rows)], axis=1)
+
+
+def half_tiles(width, part=0, parts=1):
+    half = width // 2
+    lanes = range(part * half // parts, (part + 1) * half // parts, COLUMN_TILE)
+    low = [(lane // HALF * PLANE + lane % HALF, lane) for lane in lanes]
+    return low, [(source + HALF, target) for source, target in low]
+
+
+def move_rows(rows_ref, value_ref, send_ref, crossed, part=0, parts=1):
     cells, width = value_ref.shape
-    ranges = half_slices(width)[side]
+    count = cells // 2
+    low, high = half_tiles(width, part, parts)
+    begin = low[0][1]
 
     def move(at, _):
-        row = rows_ref[0, plane, at]
-        for source, target in ranges:
-            send_ref[pl.ds(first + at, 1), target : target + HALF] = value_ref[
-                pl.ds(row, 1), source : source + HALF
-            ]
+        for first, tiles, plane in ((0, high, 1 - crossed), (count, low, crossed)):
+            row = rows_ref[0, plane, at]
+            for source, target in tiles:
+                send_ref[pl.ds(first + at, 1), target - begin : target - begin + COLUMN_TILE] = (
+                    value_ref[pl.ds(row, 1), source : source + COLUMN_TILE]
+                )
         return 0
 
-    lax.fori_loop(0, cells // 2, move, 0, unroll=8)
+    lax.fori_loop(0, count, move, 0, unroll=True)
 
 
 def wall_rows(temp_ref):
@@ -175,22 +181,12 @@
     return 1.0 / (WEIGHT * flux * mass * mass), cooling
 
 
-def near_plane_kernel(rows_ref, face_ref, temp_ref, mask_ref, dist_ref, send_ref):
-    cells, _ = dist_ref.shape
-    count = cells // 2
-    inv_norm, cooling = wall_rows(temp_ref)
-    notes = jnp.concatenate([mask_ref[...].astype(F32), inv_norm, cooling], axis=0)
-    low, high = face_hits(face_ref, cells)
-    for side, hits in ((1, high), (0, low)):
-        first = (1 - side) * (count + NOTES)
-        send_ref[first + count : first + count + NOTES, :count] = exact(notes, hits.astype(BF16))
-        move_rows(rows_ref, side, dist_ref, send_ref, side, first)
-
-
-def far_plane_kernel(rows_ref, dist_ref, send_ref):
-    for side in (1, 0):
-        first = (1 - side) * (dist_ref.shape[0] // 2)
-        move_rows(rows_ref, 1 - side, dist_ref, send_ref, side, first)
+def near_plane_kernel(rows_ref, dist_ref, send_ref):
+    move_rows(rows_ref, dist_ref, send_ref, 0)
+
+
+def far_plane_kernel(part, rows_ref, dist_ref, *refs):
+    move_rows(rows_ref, dist_ref, refs[-1], 1, part, PARTS)
 
 
 def picks(near_ref, mask_ref, face, cell_start, cells):
@@ -247,12 +243,13 @@
     stream_tiles(near_ref, mask_ref, middle_ref, store)
 
 
-def wall_kernel(face_ref, temp_ref, mask_ref, shape_ref, back_ref, side_ref):
+def wall_kernel(face_ref, temp_ref, mask_ref, shape_ref, back_ref, side_ref, notes_ref):
     cells, width = shape_ref.shape
     count = cells // 2
     planes, _ = planes_y(width)
     inv_norm, cooling = wall_rows(temp_ref)
     mask = mask_ref[...]
+    notes_ref[...] = jnp.concatenate([mask.astype(F32), inv_norm, cooling], axis=0)
     back_ref[...] = jnp.concatenate(
         [jnp.where(mask == 1, inv_norm, 0.0), cooling, jnp.zeros((1, cells), F32)],
         axis=0,
@@ -366,26 +363,28 @@
     groups = cells // ROWS
     if half:
         low, high = range(HALF // LANES), range(HALF // LANES, PLANE // LANES)
-        lax.fori_loop(0, groups // 2, functools.partial(group, tiles=high, stride=HALF), 0)
-        lax.fori_loop(groups // 2, groups, functools.partial(group, tiles=low, stride=HALF), 0)
+        lax.fori_loop(
+            0, groups // 2, functools.partial(group, tiles=high, stride=HALF), 0, unroll=True
+        )
+        lax.fori_loop(
+            groups // 2, groups, functools.partial(group, tiles=low, stride=HALF), 0, unroll=True
+        )
     else:
-        lax.fori_loop(0, groups, group, 0)
+        lax.fori_loop(0, groups, group, 0, unroll=True)
 
 
 def middle_kernel(sums_ref, back_ref, side_ref, own_ref, stream_ref, shape_ref, *refs):
     halo_refs, (out_ref, columns_ref, base_ref) = refs[:-3], refs[-3:]
     cells, width = own_ref.shape
     columns_ref[...] = columns_of(sums_ref[:SUMS], back_ref[...], width, TIME_STEP, 1.0)
-    for side, ranges in enumerate(half_slices(width)):
+    for side, tiles in enumerate(half_tiles(width)):
         pick = side_ref[side * cells : (side + 1) * cells, :]
-        for source, target in ranges:
-            for tile in range(0, HALF, COLUMN_TILE):
-                lanes = slice(source + tile, source + tile + COLUMN_TILE)
-                vel_x, _ = lane_points(source + tile, COLUMN_TILE)
-                rows = halo_rows(halo_refs, 1 - side, slice(0, cells // 2))
-                rows = rows[:, target + tile : target + tile + COLUMN_TILE]
-                halo = dot(pick, jnp.concatenate(split(rows, 2), axis=0))
-                base_ref[:, lanes] = stream_ref[:, lanes] + (TIME_STEP * jnp.abs(vel_x)) * halo
+        for source, target in tiles:
+            lanes = slice(source, source + COLUMN_TILE)
+            vel_x, _ = lane_points(source, COLUMN_TILE)
+            rows = halo_rows(halo_refs, 1 - side)[:, target : target + COLUMN_TILE]
+            halo = dot(pick, jnp.concatenate(split(rows, 2), axis=0))
+            base_ref[:, lanes] = stream_ref[:, lanes] + (TIME_STEP * jnp.abs(vel_x)) * halo
     relax(columns_ref, base_ref, own_ref, shape_ref, out_ref)
 
 
@@ -427,9 +426,9 @@
     return result
 
 
-def advance_kernel(face_ref, near_ref, mask_ref, sums_ref, back_ref, out_ref):
+def advance_kernel(face_ref, near_ref, _, mask_ref, sums_ref, back_ref, *refs):
+    shared_refs, out_ref = refs[:-1], refs[-1]
     cells = near_ref.shape[1]
-    count = cells // 2
     cell_start = lax.axis_index("space") * cells
     sums = sums_ref[:SUMS]
     flux = [sums_ref[SUMS * (face + 1) : SUMS * (face + 2)] for face in range(FACES)]
@@ -437,11 +436,9 @@
     for face in range(FACES):
         hits = picks(near_ref, mask_ref, face, cell_start, cells).astype(BF16)
         gas += exact(flux[face], hits) - flux[face]
-    arrived = sums_ref[SUMS * (FACES + 2) :]
     for face, hits in enumerate(face_hits(face_ref, cells)):
-        found = exact(
-            arrived[:, face * count : (face + 1) * count], hits.astype(BF16), ((1,), (1,))
-        )
+        arrived = halo_rows(shared_refs, face, slice(SUMS, 2 * SUMS))
+        found = exact(arrived, hits.astype(BF16), ((1,), (1,)))
         gas += jnp.where(mask_ref[face : face + 1, :] != 1, found, 0.0)
 
     rows, returned = coefficients(sums, back_ref[...], TIME_STEP, 1.0)
@@ -508,16 +505,14 @@
 
 
 def halo_stream_kernel(face_ref, near_ref, *refs):
-    halo_refs, (base_ref, shape_ref, values_ref, notes_ref, open_ref) = refs[:-5], refs[-5:]
+    base_ref, shape_ref, values_ref, open_ref = refs[-4:]
+    refs = refs[:-4]
+    shared_refs, halo_refs = refs[: len(refs) // 2], refs[len(refs) // 2 :]
     rows, width = base_ref.shape
     count = rows // 2
     planes, upward = planes_y(2 * width)
     cell_start = lax.axis_index("space") * rows
-    notes = jnp.concatenate(
-        [halo_rows(halo_refs, side, slice(count, count + NOTES))[:, :count] for side in range(2)],
-        axis=1,
-    )
-    notes_ref[...] = notes
+    notes = shared_rows(shared_refs, 2 * SUMS, 2 * SUMS + NOTES)
     passing = jnp.where(notes[:FACES] != 1.0, 1.0, 0.0)
     lane = lax.broadcasted_iota(jnp.int32, (1, rows), 1)
     picked = [
@@ -545,7 +540,7 @@
     picks_all = jnp.concatenate([picks_all, picks_all], axis=1)
     for side in range(2):
         block = slice(side * count, (side + 1) * count)
-        values_ref[block, :] = halo_rows(halo_refs, side, slice(0, count))
+        values_ref[block, :] = halo_rows(halo_refs, side)
 
         def wide(column):
             return jnp.concatenate([column[block]] * (COLUMN_TILE // LANES), axis=1)
@@ -571,58 +566,69 @@
             shape_ref[block, lanes] = jnp.exp2(speed_sq * wide(cooling))
 
 
-def halo_relax_kernel(sums_ref, notes_ref, base_ref, shape_ref, values_ref, out_ref, columns_ref):
+def halo_relax_kernel(base_ref, shape_ref, values_ref, *refs):
     width = values_ref.shape[1]
-    sums = sums_ref[SUMS * (FACES + 1) : SUMS * (FACES + 2)]
-    notes = notes_ref[...]
+    shared_refs, (out_ref, columns_ref) = refs[:-2], refs[-2:]
+    sums = shared_rows(shared_refs, 0, SUMS)
+    notes = shared_rows(shared_refs, 2 * SUMS, 2 * SUMS + NOTES)
     back = jnp.where(notes[:FACES] == 1.0, notes[6:7], 0.0)
     columns_ref[...] = columns_of(sums, back, 2 * width, TIME_STEP, 1.0)
     relax(columns_ref, base_ref, values_ref, shape_ref, out_ref, half=True)
 
 
-def last_kernel(side_ref, part_ref, plane_ref, open_ref, *refs):
-    halo_refs, (out_ref, result_ref, sems) = refs[:-3], refs[-3:]
+def last_kernel(part, side_ref, part_ref, plane_ref, open_ref, *refs):
+    refs, (out_ref, result_ref, sems) = refs[:-3], refs[-3:]
+    halo_refs = refs[part > 0 :]
     cells, width = part_ref.shape
     count = cells // 2
     copies = []
-    for side, ranges in enumerate(half_slices(width)):
+    for side, tiles in enumerate(half_tiles(width, part, PARTS)):
         pick = side_ref[side * cells : (side + 1) * cells, :]
         block = slice((1 - side) * count, (2 - side) * count)
         gate = jnp.concatenate([open_ref[block]] * (COLUMN_TILE // LANES), axis=1)
-        for source, target in ranges:
-            for tile in range(0, HALF, COLUMN_TILE):
-                lanes = slice(source + tile, source + tile + COLUMN_TILE)
-                there = slice(target + tile, target + tile + COLUMN_TILE)
-                speed_x = jnp.abs(lane_points(source + tile, COLUMN_TILE)[0])
-                rows = halo_rows(halo_refs, 1 - side)[:, there]
-                rows = plane_ref[block, there] + gate * speed_x * rows
-                halo = dot(pick, jnp.concatenate(split(rows, 2), axis=0))
-                result_ref[:, lanes] = part_ref[:, lanes] + (0.5 * TIME_STEP * speed_x) * halo
-                copy = pltpu.make_async_copy(
-                    result_ref.at[:, lanes], out_ref.at[:, lanes], sems.at[len(copies)]
-                )
-                copy.start()
-                copies.append(copy)
+        begin = tiles[0][1]
+        for source, target in tiles:
+            lanes = slice(source, source + COLUMN_TILE)
+            speed_x = jnp.abs(lane_points(source, COLUMN_TILE)[0])
+            rows = halo_rows(halo_refs, 1 - side)[:, target - begin : target - begin + COLUMN_TILE]
+            rows = plane_ref[block, target : target + COLUMN_TILE] + gate * speed_x * rows
+            halo = dot(pick, jnp.concatenate(split(rows, 2), axis=0))
+            result_ref[:, lanes] = part_ref[:, lanes] + (0.5 * TIME_STEP * speed_x) * halo
+            copy = pltpu.make_async_copy(
+                result_ref.at[:, lanes], out_ref.at[:, lanes], sems.at[len(copies)]
+            )
+            copy.start()
+            copies.append(copy)
     for copy in copies:
         copy.wait()
 
 
-def call(kernel, outs, arrays, scratch=(), scalars=0, far_outs=False, flops=0):
-    specs = [
-        pl.BlockSpec(memory_space=pltpu.SMEM if at < scalars else pltpu.VMEM)
+def call(kernel, outs, arrays, scratch=(), scalars=0, far_outs=False, unread=(), aliases=None):
+    spaces = [
+        pltpu.SMEM if at < scalars else pl.ANY if at in unread else pltpu.VMEM
         for at in range(len(arrays))
     ]
-    out_space = pltpu.HBM if far_outs else pltpu.VMEM
+    if isinstance(kernel, functools.partial):
+        name = f"{kernel.func.__name__}_{kernel.args[0]}"
+    else:
+        name = kernel.__name__
     size = sum(math.prod(array.shape) * 4 for array in arrays)
     return pl.pallas_call(
         kernel,
         out_shape=[jax.ShapeDtypeStruct(shape, dtype) for shape, dtype in outs],
-        in_specs=specs,
-        out_specs=[pl.BlockSpec(memory_space=out_space)] * len(outs),
+        in_specs=[pl.BlockSpec(memory_space=space) for space in spaces],
+        out_specs=[pl.BlockSpec(memory_space=pl.ANY if far_outs else pltpu.VMEM)] * len(outs),
         scratch_shapes=list(scratch),
+        input_output_aliases=aliases or {},
+        name=name,
         compiler_params=pltpu.CompilerParams(vmem_limit_bytes=40 * 2**20),
-        cost_estimate=pl.CostEstimate(flops=flops, bytes_accessed=size, transcendentals=0),
+        cost_estimate=pl.CostEstimate(
+            flops=COST.get(name, 0), bytes_accessed=size, transcendentals=0
+        ),
     )(*arrays)
+
+
+COST = {"advance_kernel": 10**9, "relax_kernel": 10**9, "last_kernel_0": 10**9}
 
 
 def total(value):
@@ -655,54 +661,68 @@
     every = SUMS * (FACES + 1)
     columns = pltpu.VMEM((cells, LANES), F32)
 
-    own_sums, sent = call(
-        sums_kernel, [((every, cells), F32), ((4 * SUMS, count), F32)], [face_rows, dist]
-    )
-    halo_sums = exchange(sent)
+    (sent,) = call(near_plane_kernel, [plane], [face_rows, dist], scalars=1)
+    near = exchange(sent)
+    (sums,) = call(sums_kernel, [((every, cells), F32)], [dist])
+    sums = total(sums)
+    shape, back, side, notes = call(
+        wall_kernel,
+        [whole, ((8, cells), F32), ((2 * cells, cells), BF16), ((NOTES, cells), F32)],
+        [face_rows, temp, wall_mask],
+    )
+    (stream,) = call(stream_kernel, [whole], [neighbours, wall_mask, dist])
     (sent,) = call(
-        near_plane_kernel,
-        [((2 * (count + NOTES), half), F32)],
-        [face_rows, face_rows, temp, wall_mask, dist],
-        scalars=1,
-    )
-    near = exchange(sent)
-    (sent,) = call(far_plane_kernel, [plane], [face_rows, dist], scalars=1)
-    far = exchange(sent)
-    (sums,) = call(gather_kernel, [((every + 2 * SUMS, cells), F32)], [own_sums, *halo_sums])
-    shape, back, side = call(
-        wall_kernel,
-        [whole, ((8, cells), F32), ((2 * cells, cells), BF16)],
-        [face_rows, temp, wall_mask],
-    )
-    (stream,) = call(stream_kernel, [whole], [neighbours, wall_mask, dist])
-    base, halo_shape, values, notes, gate = call(
-        halo_stream_kernel,
-        [plane, plane, plane, ((NOTES, cells), F32), ((cells, LANES), F32)],
-        [face_rows, neighbours, *near],
-    )
-    sums = total(sums)
+        share_kernel, [((2 * (2 * SUMS + NOTES), count), F32)], [face_rows, sums, notes]
+    )
+    shared = exchange(sent)
+    far = []
+    for part in range(PARTS):
+        after = [sent] if part else []
+        (far_rows,) = call(
+            functools.partial(far_plane_kernel, part),
+            [((cells, half // PARTS), F32)],
+            [face_rows, dist, *after],
+            scalars=1,
+            unread=(2,),
+        )
+        far.append(exchange(far_rows))
     (middle,) = call(
         middle_kernel,
         [whole],
         [sums, back, side, dist, stream, shape, *near],
         [columns, pltpu.VMEM((cells, width), F32)],
     )
+    (part_sum,) = call(stream_last_kernel, [whole], [neighbours, wall_mask, dist, middle])
     (sums_two,) = call(
-        advance_kernel, [((SUMS, cells), F32)], [face_rows, neighbours, wall_mask, sums, back]
-    )
-    (part,) = call(stream_last_kernel, [whole], [neighbours, wall_mask, dist, middle])
-    (part,) = call(relax_kernel, [whole], [sums_two, back, middle, part, shape], [columns])
+        advance_kernel,
+        [((SUMS, cells), F32)],
+        [face_rows, neighbours, part_sum, wall_mask, sums, back, *shared],
+        unread=(2,),
+    )
+    (part_sum,) = call(relax_kernel, [whole], [sums_two, back, middle, part_sum, shape], [columns])
+    base, halo_shape, values, gate = call(
+        halo_stream_kernel,
+        [plane, plane, plane, ((cells, LANES), F32)],
+        [face_rows, neighbours, *shared, *near],
+    )
     (plane_one,) = call(
-        halo_relax_kernel, [plane], [sums, notes, base, halo_shape, values], [columns]
-    )
-    (result,) = call(
-        last_kernel,
-        [whole],
-        [side, part, plane_one, gate, *far],
-        [pltpu.VMEM((cells, width), F32), pltpu.SemaphoreType.DMA((width // COLUMN_TILE,))],
-        far_outs=True,
-    )
-    return result
+        halo_relax_kernel, [plane], [base, halo_shape, values, *shared], [columns]
+    )
+    result = []
+    for part in range(PARTS):
+        result = call(
+            functools.partial(last_kernel, part),
+            [whole],
+            [side, part_sum, plane_one, gate, *result, *far[part]],
+            [
+                pltpu.VMEM((cells, width), F32),
+                pltpu.SemaphoreType.DMA((width // COLUMN_TILE // PARTS,)),
+            ],
+            far_outs=True,
+            unread=(4,) if part else (),
+            aliases={4: 0} if part else None,
+        )
+    return result[0]
 
 
 def solution(mesh):

time: 57.6 us -> 35.4 us (0.61)
  waiting for transfers between devices: 28.7 us -> 9.48 us
  Pallas kernels: 14.2 us -> 11.9 us
  local copies, waits for them, and re-layouts: 2.61 us -> 1.99 us
    ppermute x3 -> x4, waiting for transfers between devices: 21 us -> 2.3 us  [exchange(): return [lax.ppermute(send, 'space', forward)]]
    pallas_call x13 -> x15, Pallas kernels: 14.2 us -> 11.9 us  [call(): pl.pallas_call(kernel, out_shape=[jax.ShapeDtypeStruct(shape, dtype) for...]
    ppermute x3 -> x4, starting transfers between devices: 5.14 us -> 5.76 us  [exchange(): return [lax.ppermute(send, 'space', forward)]]
    unnamed x14 -> x12, local copies, waits for them, and re-layouts: 2.61 us -> 1.99 us
    ppermute x4, starting transfers between devices: 6.53 us -> 5.92 us  [total(): lax.ppermute(value, 'vel', [(i, i ^ step) for i in range(count)])]
  transfers between devices with their start and end apart: 7 -> 8, of which waited for: 5 -> 5; matrix products, arithmetic and copies ran while one was open for 0% -> 0% of each run, Pallas kernels for 20% -> 28%
where the time goes in v5:
time: 35.4 us; the launch traced here: 35.2 us
  Pallas kernels  11.9 us (34%)
  starting transfers between devices  11.7 us (33%)
  waiting for transfers between devices  9.48 us (27%)
  local copies, waits for them, and re-layouts  1.99 us (6%)
    pallas_call x15, Pallas kernels, call(): pl.pallas_call(kernel, out_shape=[jax.ShapeDtypeStruct(shape, dtype) for...  11.9 us
    ppermute x4, waiting for transfers between devices, total(): lax.ppermute(value, 'vel', [(i, i ^ step) for i in range(count)])  7.18 us
    ppermute x4, starting transfers between devices, total(): lax.ppermute(value, 'vel', [(i, i ^ step) for i in range(count)])  5.92 us
    ppermute x4, starting transfers between devices, exchange(): return [lax.ppermute(send, 'space', forward)]  5.76 us
    ppermute x4, waiting for transfers between devices, exchange(): return [lax.ppermute(send, 'space', forward)]  2.3 us
    unnamed x12, local copies, waits for them, and re-layouts  1.99 us
  transfers between devices with their start and end apart: 8, of which 5 were waited for; matrix products, arithmetic and copies ran while one was open for 0% of the time, Pallas kernels for 28%

profile of v5, /device:TPU:0, one launch (start us, length us, event | category | flops | bytes accessed | tf_op | source)
XLA Modules:
  0.0 35.2 jit_solution(6235162577541312299)
XLA Ops:
  0.0 0.0 copy-start
  0.0 1.2 %copy-done = f32[128,2048]{1,0:T(8,128)S(1)} copy-done((f32[128,2048]{1,0:T(8,128)S(1)}, f32[128,2048]{1,0:T(8,128)}, u32[]{:S(2)}) %copy-start) | copy-done | bytes 1048600
  1.2 0.0 copy-start.4
  1.2 0.7 %copy-done.4 = s32[1,2,64]{2,1,0:T(2,128)S(1)} copy-done((s32[1,2,64]{2,1,0:T(2,128)S(1)}, s32[1,2,64]{2,1,0:T(2,128)}, u32[]{:S(2)}) %copy-start.4) | copy-done | bytes 536
  1.9 0.0 copy-start.1
  1.9 1.0 %near_plane_kernel.1 = f32[128,1024]{1,0:T(8,128)S(1)} custom-call(s32[1,2,64]{2,1,0:T(2,128)S(1)} %copy-done.4, f32[128,2048]{1,0:T(8,128)S(1)} %copy-done), custom_call_target="tpu_custom_call" | custom-call | bytes 1049088 | tf_op jit(solution)/shard_map/near_plane_kernel/pallas_call | solution.py:616
  2.9 3.0 %collective-permute-start.4 = (f32[128,1024]{1,0:T(8,128)S(1)}, f32[128,1024]{1,0:T(8,128)S(1)}, u32[]{:S(2)}, u32[]{:S(2)}) collective-permute-start(f32[128,1024]{1,0:T(8,128)S(1)} %near_plane_kernel.1), channel_id=1, source_target_pairs={{0,16},{16,0},{1,17},{17,1},{2,18},{18,2},{3,19},{19,3},{4,20},{20... | collective-permute-start | bytes 1572872 | tf_op jit(solution)/shard_map/ppermute | solution.py:648
  5.9 0.0 copy-done.1
  5.9 0.8 %sums_kernel.1 = f32[112,128]{1,0:T(8,128)S(1)} custom-call(f32[128,2048]{1,0:T(8,128)S(1)} %copy-done.1), custom_call_target="tpu_custom_call" | custom-call | bytes 1048576 | tf_op jit(solution)/shard_map/sums_kernel/pallas_call | solution.py:616
  6.8 0.1 collective-permute-start
  6.9 1.2 %collective-permute-done = f32[112,128]{1,0:T(8,128)S(1)} collective-permute-done((f32[112,128]{1,0:T(8,128)S(1)}, f32[112,128]{1,0:T(8,128)S(1)}, u32[]{:S(2)}, u32[]{:S(2)}) %collective-permute-start) | collective-permute-done | bytes 57376 | tf_op jit(solution)/shard_map/ppermute | solution.py:638
  8.1 1.6 %collective-permute-start.1 = (f32[112,128]{1,0:T(8,128)S(1)}, f32[112,128]{1,0:T(8,128)S(1)}, u32[]{:S(2)}, u32[]{:S(2)}) collective-permute-start(f32[112,128]{1,0:T(8,128)S(1)} %add.12), channel_id=1, source_target_pairs={{0,2},{1,3},{2,0},{3,1},{4,6},{5,7},{6,4},{7,5},{8,10},{9,11},{10,... | collective-permute-start | bytes 172040 | tf_op jit(solution)/shard_map/ppermute | solution.py:638
  9.6 2.7 %collective-permute-done.1 = f32[112,128]{1,0:T(8,128)S(1)} collective-permute-done((f32[112,128]{1,0:T(8,128)S(1)}, f32[112,128]{1,0:T(8,128)S(1)}, u32[]{:S(2)}, u32[]{:S(2)}) %collective-permute-start.1) | collective-permute-done | bytes 57376 | tf_op jit(solution)/shard_map/ppermute | solution.py:638
  12.3 1.6 %collective-permute-start.2 = (f32[112,128]{1,0:T(8,128)S(1)}, f32[112,128]{1,0:T(8,128)S(1)}, u32[]{:S(2)}, u32[]{:S(2)}) collective-permute-start(f32[112,128]{1,0:T(8,128)S(1)} %add.13), channel_id=1, source_target_pairs={{0,4},{1,5},{2,6},{3,7},{4,0},{5,1},{6,2},{7,3},{8,12},{9,13},{10,... | collective-permute-start | bytes 172040 | tf_op jit(solution)/shard_map/ppermute | solution.py:638
  14.0 2.6 %collective-permute-done.2 = f32[112,128]{1,0:T(8,128)S(1)} collective-permute-done((f32[112,128]{1,0:T(8,128)S(1)}, f32[112,128]{1,0:T(8,128)S(1)}, u32[]{:S(2)}, u32[]{:S(2)}) %collective-permute-start.2) | collective-permute-done | bytes 57376 | tf_op jit(solution)/shard_map/ppermute | solution.py:638
  16.6 2.7 %collective-permute-start.3 = (f32[112,128]{1,0:T(8,128)S(1)}, f32[112,128]{1,0:T(8,128)S(1)}, u32[]{:S(2)}, u32[]{:S(2)}) collective-permute-start(f32[112,128]{1,0:T(8,128)S(1)} %add.14), channel_id=1, source_target_pairs={{0,8},{1,9},{2,10},{3,11},{4,12},{5,13},{6,14},{7,15},{8,0},{9,1},... | collective-permute-start | bytes 172040 | tf_op jit(solution)/shard_map/ppermute | solution.py:638
  19.3 0.0 copy-start.3
  19.3 0.8 %far_plane_kernel_0.1 = f32[128,512]{1,0:T(8,128)S(1)} custom-call(s32[1,2,64]{2,1,0:T(2,128)S(1)} %copy-done.4, f32[128,2048]{1,0:T(8,128)S(1)} %copy-done.1), custom_call_target="tpu_custom_call" | custom-call | bytes 1049088 | tf_op jit(solution)/shard_map/far_plane_kernel_0/pallas_call | solution.py:616
  20.1 0.0 copy-start.5
  20.1 0.6 %collective-permute-start.6 = (f32[128,512]{1,0:T(8,128)S(1)}, f32[128,512]{1,0:T(8,128)S(1)}, u32[]{:S(2)}, u32[]{:S(2)}) collective-permute-start(f32[128,512]{1,0:T(8,128)S(1)} %far_plane_kernel_0.1), channel_id=1, source_target_pairs={{0,16},{16,0},{1,17},{17,1},{2,18},{18,2},{3,19},{19,3},{4,20},{20... | collective-permute-start | bytes 786440 | tf_op jit(solution)/shard_map/ppermute | solution.py:648
  20.7 0.0 copy-done.3
  20.7 0.1 copy-done.5
  20.8 0.3 wall_kernel.1
  21.1 0.7 %collective-permute-done.3 = f32[112,128]{1,0:T(8,128)S(1)} collective-permute-done((f32[112,128]{1,0:T(8,128)S(1)}, f32[112,128]{1,0:T(8,128)S(1)}, u32[]{:S(2)}, u32[]{:S(2)}) %collective-permute-start.3) | collective-permute-done | bytes 57376 | tf_op jit(solution)/shard_map/ppermute | solution.py:638
  21.8 0.0 copy-start.2
  21.8 0.2 share_kernel.1.refs_0_
  21.9 0.9 %collective-permute-start.5 = (f32[80,64]{1,0:T(8,128)S(1)}, f32[80,64]{1,0:T(8,128)S(1)}, u32[]{:S(2)}, u32[]{:S(2)}) collective-permute-start(f32[80,64]{1,0:T(8,128)S(1)} %share_kernel.1.refs_0_), channel_id=1, source_target_pairs={{0,16},{16,0},{1,17},{17,1},{2,18},{18,2},{3,19},{19,3},{4,20},{20... | collective-permute-start | bytes 61448 | tf_op jit(solution)/shard_map/ppermute | solution.py:648
  22.8 0.0 copy-done.2
  22.8 0.8 %stream_kernel.1.stream_ref = f32[128,2048]{1,0:T(8,128)S(1)} custom-call(s32[6,128]{1,0:T(8,128)S(1)} %copy-done.2, s32[6,128]{1,0:T(8,128)S(1)} %copy-done.3, f32[128,2048]{1,0:T(8,128)S(1)} %copy-done.1), custom_call_target="tpu_custom_call" | custom-call | bytes 1054720 | tf_op jit(solution)/shard_map/stream_kernel/pallas_call | solution.py:616
  23.6 0.8 %far_plane_kernel_1.1 = f32[128,512]{1,0:T(8,128)S(1)} custom-call(s32[1,2,64]{2,1,0:T(2,128)S(1)} %copy-done.4, f32[128,2048]{1,0:T(8,128)S(1)} %copy-done.1, f32[80,64]{1,0:T(8,128)S(1)} %share_kernel.1.refs_0_), custom_call_target="tpu_custom_call" | custom-call | bytes 1069568 | tf_op jit(solution)/shard_map/far_plane_kernel_1/pallas_call | solution.py:616
  24.5 1.3 %collective-permute-start.7 = (f32[128,512]{1,0:T(8,128)S(1)}, f32[128,512]{1,0:T(8,128)S(1)}, u32[]{:S(2)}, u32[]{:S(2)}) collective-permute-start(f32[128,512]{1,0:T(8,128)S(1)} %far_plane_kernel_1.1), channel_id=1, source_target_pairs={{0,16},{16,0},{1,17},{17,1},{2,18},{18,2},{3,19},{19,3},{4,20},{20... | collective-permute-start | bytes 786440 | tf_op jit(solution)/shard_map/ppermute | solution.py:648
  25.8 0.0 collective-permute-done.4.refs_0_.refs_1_
  25.8 1.1 %middle_kernel.1.middle_ref = f32[128,2048]{1,0:T(8,128)S(1)} custom-call(f32[112,128]{1,0:T(8,128)S(1)} %add.15.sums_ref, f32[8,128]{1,0:T(8,128)S(1)} %get-tuple-element.14.back_ref, bf16[256,128]{1,0:T(8,128)(2,1)S(1)} %get-tuple-element.13.side_ref, f32[128,2048]{1,0:T(8,128)S(1)} %copy-done.1, f32[128,2048]{1,0:T(8,128)S(1)} %stream_kernel.1.stream_ref, ...), custom_call_target="tpu_custom_call" | custom-call | bytes 3862528 | tf_op jit(solution)/shard_map/middle_kernel/pallas_call | solution.py:616
  26.9 0.9 %stream_last_kernel.1._.part_ref = f32[128,2048]{1,0:T(8,128)S(1)} custom-call(s32[6,128]{1,0:T(8,128)S(1)} %copy-done.2, s32[6,128]{1,0:T(8,128)S(1)} %copy-done.3, f32[128,2048]{1,0:T(8,128)S(1)} %copy-done.1, f32[128,2048]{1,0:T(8,128)S(1)} %middle_kernel.1.middle_ref), custom_call_target="tpu_custom_call" | custom-call | bytes 2103296 | tf_op jit(solution)/shard_map/stream_last_kernel/pallas_call | solution.py:616
  27.8 2.3 %collective-permute-done.5.refs_0_ = f32[80,64]{1,0:T(8,128)S(1)} collective-permute-done((f32[80,64]{1,0:T(8,128)S(1)}, f32[80,64]{1,0:T(8,128)S(1)}, u32[]{:S(2)}, u32[]{:S(2)}) %collective-permute-start.5) | collective-permute-done | bytes 20512 | tf_op jit(solution)/shard_map/ppermute | solution.py:648
  30.1 1.0 %halo_stream_kernel.1 = (f32[128,1024]{1,0:T(8,128)S(1)}, f32[128,1024]{1,0:T(8,128)S(1)}, f32[128,1024]{1,0:T(8,128)S(1)}, f32[128,128]{1,0:T(8,128)S(1)}) custom-call(s32[1,2,64]{2,1,0:T(2,128)S(1)} %copy-done.4, s32[6,128]{1,0:T(8,128)S(1)} %copy-done.2, f32[80,64]{1,0:T(8,128)S(1)} %collective-permute-done.5.refs_0_, ...), custom_call_target="tpu_custom_call" | custom-call | bytes 548352 | tf_op jit(solution)/shard_map/halo_stream_kernel/pallas_call | solution.py:616
  31.1 0.7 %halo_relax_kernel.1.plane_ref = f32[128,1024]{1,0:T(8,128)S(1)} custom-call(f32[128,1024]{1,0:T(8,128)S(1)} %get-tuple-element.17.base_ref, f32[128,1024]{1,0:T(8,128)S(1)} %get-tuple-element.18.shape_ref, f32[128,1024]{1,0:T(8,128)S(1)} %get-tuple-element.19.values_ref, f32[80,64]{1,0:T(8,128)S(1)} %collective-permute-done.5.refs_0_), custom_call_target="tpu_custom_call" | custom-call | bytes 1593344 | tf_op jit(solution)/shard_map/halo_relax_kernel/pallas_call | solution.py:616
  31.7 0.5 %advance_kernel.1.sums_ref = f32[16,128]{1,0:T(8,128)S(1)} custom-call(s32[1,2,64]{2,1,0:T(2,128)S(1)} %copy-done.4, s32[6,128]{1,0:T(8,128)S(1)} %copy-done.2, f32[128,2048]{1,0:T(8,128)S(1)} %stream_last_kernel.1._.part_ref, s32[6,128]{1,0:T(8,128)S(1)} %copy-done.3, f32[112,128]{1,0:T(8,128)S(1)} %add.15.sums_ref, ...), custom_call_target="tpu_custom_call" | custom-call | flops 1000000000 | bytes 1137152 | tf_op jit(solution)/shard_map/advance_kernel/pallas_call | solution.py:616
  32.2 0.9 %relax_kernel.1.part_ref = f32[128,2048]{1,0:T(8,128)S(1)} custom-call(f32[16,128]{1,0:T(8,128)S(1)} %advance_kernel.1.sums_ref, f32[8,128]{1,0:T(8,128)S(1)} %get-tuple-element.14.back_ref, f32[128,2048]{1,0:T(8,128)S(1)} %middle_kernel.1.middle_ref, f32[128,2048]{1,0:T(8,128)S(1)} %stream_last_kernel.1._.part_ref, f32[128,2048]{1,0:T(8,128)S(1)} %get-tuple-element.15.shape_ref), custom_call_target="tpu_custom_call" | custom-call | flops 1000000000 | bytes 3158016 | tf_op jit(solution)/shard_map/relax_kernel/pallas_call | solution.py:616
  33.1 0.0 collective-permute-done.6.refs_0_
  33.1 1.0 %last_kernel_0.1.refs_0_ = f32[128,2048]{1,0:T(8,128)} custom-call(bf16[256,128]{1,0:T(8,128)(2,1)S(1)} %get-tuple-element.13.side_ref, f32[128,2048]{1,0:T(8,128)S(1)} %relax_kernel.1.part_ref, f32[128,1024]{1,0:T(8,128)S(1)} %halo_relax_kernel.1.plane_ref, f32[128,128]{1,0:T(8,128)S(1)} %get-tuple-element.20.open_ref, ...), custom_call_target="tpu_custom_call" | custom-call | flops 1000000000 | bytes 2031616 | tf_op jit(solution)/shard_map/last_kernel_0/pallas_call | solution.py:616
  34.2 0.0 collective-permute-done.7.refs_1_
  34.2 1.0 %last_kernel_1.1 = f32[128,2048]{1,0:T(8,128)} custom-call(bf16[256,128]{1,0:T(8,128)(2,1)S(1)} %get-tuple-element.13.side_ref, f32[128,2048]{1,0:T(8,128)S(1)} %relax_kernel.1.part_ref, f32[128,1024]{1,0:T(8,128)S(1)} %halo_relax_kernel.1.plane_ref, f32[128,128]{1,0:T(8,128)S(1)} %get-tuple-element.20.open_ref, ...), custom_call_target="tpu_custom_call", output_to_operand_aliasing={{}: (4, {})} | custom-call | bytes 3080192 | tf_op jit(solution)/shard_map/last_kernel_1/pallas_call | solution.py:616
  (4 shorter events, 0.0 us)
Async XLA Ops:
  0.0 1.2 %copy-start = (f32[128,2048]{1,0:T(8,128)S(1)}, f32[128,2048]{1,0:T(8,128)}, u32[]{:S(2)}) copy-start(f32[128,2048]{1,0:T(8,128)} %dist_ref.9) | copy-start | bytes 3145732
  1.2 0.7 %copy-start.4 = (s32[1,2,64]{2,1,0:T(2,128)S(1)}, s32[1,2,64]{2,1,0:T(2,128)}, u32[]{:S(2)}) copy-start(s32[1,2,64]{2,1,0:T(2,128)} %rows_ref.5) | copy-start | bytes 1540
  1.9 4.0 %copy-start.1 = (f32[128,2048]{1,0:T(8,128)S(1)}, f32[128,2048]{1,0:T(8,128)}, u32[]{:S(2)}) copy-start(f32[128,2048]{1,0:T(8,128)} %dist_ref.9) | copy-start | bytes 3145732
  2.9 22.9 %collective-permute-start.4 = (f32[128,1024]{1,0:T(8,128)S(1)}, f32[128,1024]{1,0:T(8,128)S(1)}, u32[]{:S(2)}, u32[]{:S(2)}) collective-permute-start(f32[128,1024]{1,0:T(8,128)S(1)} %near_plane_kernel.1), channel_id=1, source_target_pairs={{0,16},{16,0},{1,17},{17,1},{2,18},{18,2},{3,19},{19,3},{4,20},{20... | collective-permute-start | bytes 1572872 | tf_op jit(solution)/shard_map/ppermute | solution.py:648
  6.8 1.3 %collective-permute-start = (f32[112,128]{1,0:T(8,128)S(1)}, f32[112,128]{1,0:T(8,128)S(1)}, u32[]{:S(2)}, u32[]{:S(2)}) collective-permute-start(f32[112,128]{1,0:T(8,128)S(1)} %sums_kernel.1), channel_id=1, source_target_pairs={{0,1},{1,0},{2,3},{3,2},{4,5},{5,4},{6,7},{7,6},{8,9},{9,8},{10,11... | collective-permute-start | bytes 172040 | tf_op jit(solution)/shard_map/ppermute | solution.py:638
  8.1 4.2 %collective-permute-start.1 = (f32[112,128]{1,0:T(8,128)S(1)}, f32[112,128]{1,0:T(8,128)S(1)}, u32[]{:S(2)}, u32[]{:S(2)}) collective-permute-start(f32[112,128]{1,0:T(8,128)S(1)} %add.12), channel_id=1, source_target_pairs={{0,2},{1,3},{2,0},{3,1},{4,6},{5,7},{6,4},{7,5},{8,10},{9,11},{10,... | collective-permute-start | bytes 172040 | tf_op jit(solution)/shard_map/ppermute | solution.py:638
  12.3 4.2 %collective-permute-start.2 = (f32[112,128]{1,0:T(8,128)S(1)}, f32[112,128]{1,0:T(8,128)S(1)}, u32[]{:S(2)}, u32[]{:S(2)}) collective-permute-start(f32[112,128]{1,0:T(8,128)S(1)} %add.13), channel_id=1, source_target_pairs={{0,4},{1,5},{2,6},{3,7},{4,0},{5,1},{6,2},{7,3},{8,12},{9,13},{10,... | collective-permute-start | bytes 172040 | tf_op jit(solution)/shard_map/ppermute | solution.py:638
  16.6 5.1 %collective-permute-start.3 = (f32[112,128]{1,0:T(8,128)S(1)}, f32[112,128]{1,0:T(8,128)S(1)}, u32[]{:S(2)}, u32[]{:S(2)}) collective-permute-start(f32[112,128]{1,0:T(8,128)S(1)} %add.14), channel_id=1, source_target_pairs={{0,8},{1,9},{2,10},{3,11},{4,12},{5,13},{6,14},{7,15},{8,0},{9,1},... | collective-permute-start | bytes 172040 | tf_op jit(solution)/shard_map/ppermute | solution.py:638
  19.3 1.4 %copy-start.3 = (s32[6,128]{1,0:T(8,128)S(1)}, s32[6,128]{1,0:T(8,128)}, u32[]{:S(2)}) copy-start(s32[6,128]{1,0:T(8,128)} %mask_ref.7) | copy-start | bytes 9220
  20.1 0.7 %copy-start.5 = (f32[128]{0:T(128)S(1)}, f32[128]{0:T(128)}, u32[]{:S(2)}) copy-start(f32[128]{0:T(128)} %param.6) | copy-start | bytes 1540
  20.1 13.0 %collective-permute-start.6 = (f32[128,512]{1,0:T(8,128)S(1)}, f32[128,512]{1,0:T(8,128)S(1)}, u32[]{:S(2)}, u32[]{:S(2)}) collective-permute-start(f32[128,512]{1,0:T(8,128)S(1)} %far_plane_kernel_0.1), channel_id=1, source_target_pairs={{0,16},{16,0},{1,17},{17,1},{2,18},{18,2},{3,19},{19,3},{4,20},{20... | collective-permute-start | bytes 786440 | tf_op jit(solution)/shard_map/ppermute | solution.py:648
  21.8 1.0 %copy-start.2 = (s32[6,128]{1,0:T(8,128)S(1)}, s32[6,128]{1,0:T(8,128)}, u32[]{:S(2)}) copy-start(s32[6,128]{1,0:T(8,128)} %near_ref.7) | copy-start | bytes 9220
  21.9 8.2 %collective-permute-start.5 = (f32[80,64]{1,0:T(8,128)S(1)}, f32[80,64]{1,0:T(8,128)S(1)}, u32[]{:S(2)}, u32[]{:S(2)}) collective-permute-start(f32[80,64]{1,0:T(8,128)S(1)} %share_kernel.1.refs_0_), channel_id=1, source_target_pairs={{0,16},{16,0},{1,17},{17,1},{2,18},{18,2},{3,19},{19,3},{4,20},{20... | collective-permute-start | bytes 61448 | tf_op jit(solution)/shard_map/ppermute | solution.py:648
  24.5 9.7 %collective-permute-start.7 = (f32[128,512]{1,0:T(8,128)S(1)}, f32[128,512]{1,0:T(8,128)S(1)}, u32[]{:S(2)}, u32[]{:S(2)}) collective-permute-start(f32[128,512]{1,0:T(8,128)S(1)} %far_plane_kernel_1.1), channel_id=1, source_target_pairs={{0,16},{16,0},{1,17},{17,1},{2,18},{18,2},{3,19},{19,3},{4,20},{20... | collective-permute-start | bytes 786440 | tf_op jit(solution)/shard_map/ppermute | solution.py:648

commit v6 on v5

--- a/solution.py
+++ b/solution.py
@@ -58,6 +58,31 @@
 
 def dot(left, right, dims=((1,), (0,))):
     return lax.dot_general(left, right, (dims, ((), ())), preferred_element_type=F32)
+
+
+def kept(face):
+    other = face ^ 1
+    return [*range(1, 10)] + [
+        10 + out for out in range(FACES) if out == other or out // 2 > other // 2
+    ]
+
+
+def flux_start(face):
+    return SUMS + sum(len(kept(before)) for before in range(face))
+
+
+def flux_rows(base, packed, face):
+    other = face ^ 1
+    mine = packed[face]
+    rows = [base[10 + other : 11 + other], mine[:9]]
+    for out in range(FACES):
+        if out == face:
+            rows.append(jnp.zeros_like(mine[:1]))
+            continue
+        holder, row = (face, 10 + out) if 10 + out in kept(face) else (out ^ 1, 10 + other)
+        at = kept(holder).index(row)
+        rows.append(packed[holder][at : at + 1])
+    return jnp.concatenate(rows, axis=0)
 
 
 def exact(left, right, dims=((1,), (0,))):
@@ -110,7 +135,12 @@
         vel_x, vel_z = lane_points(start, HALF)
         vel_y = jnp.full((1, HALF), planes[start // PLANE])
         base, into = weights(vel_x, vel_y, vel_z)
-        table = jnp.concatenate([base] + [base * speed for speed in into], axis=0)
+        table = [base]
+        for face, speed in enumerate(into):
+            fluxes = base * speed
+            table.append(fluxes[1:10])
+            table += [fluxes[row : row + 1] for row in kept(face)[9:]]
+        table = jnp.concatenate(table, axis=0)
         coarse, fine = split(table, 2)
         finest = split(base, 3)[2]
         pieces = split(dist_ref[:, lanes], 3)
@@ -127,11 +157,11 @@
 
 def share_kernel(face_ref, sums_ref, notes_ref, send_ref):
     low, high = face_hits(face_ref, sums_ref.shape[1])
-    total, notes = sums_ref[: 3 * SUMS], notes_ref[...]
-    base, from_low, from_high = total[:SUMS], total[SUMS : 2 * SUMS], total[2 * SUMS :]
-    upward = exact(jnp.concatenate([base, from_low, notes], axis=0), high.astype(BF16))
-    downward = exact(jnp.concatenate([base, from_high, notes], axis=0), low.astype(BF16))
-    send_ref[...] = jnp.concatenate([upward, downward], axis=0)
+    for side, hits in ((0, high), (1, low)):
+        rows = [sums_ref[:SUMS], notes_ref[...], sums_ref[flux_start(side) : flux_start(side + 1)]]
+        rows = exact(jnp.concatenate(rows, axis=0), hits.astype(BF16))
+        first = side * (send_ref.shape[0] // 2)
+        send_ref[first : first + rows.shape[0], :] = rows
 
 
 def halo_rows(refs, side, rows=slice(None)):
@@ -181,7 +211,7 @@
     return 1.0 / (WEIGHT * flux * mass * mass), cooling
 
 
-def near_plane_kernel(rows_ref, dist_ref, send_ref):
+def near_plane_kernel(rows_ref, dist_ref, _, send_ref):
     move_rows(rows_ref, dist_ref, send_ref, 0)
 
 
@@ -431,13 +461,17 @@
     cells = near_ref.shape[1]
     cell_start = lax.axis_index("space") * cells
     sums = sums_ref[:SUMS]
-    flux = [sums_ref[SUMS * (face + 1) : SUMS * (face + 2)] for face in range(FACES)]
+    packed = [sums_ref[flux_start(face) : flux_start(face + 1)] for face in range(FACES)]
+    flux = [flux_rows(sums, packed, face) for face in range(FACES)]
     gas = 0.0
     for face in range(FACES):
         hits = picks(near_ref, mask_ref, face, cell_start, cells).astype(BF16)
         gas += exact(flux[face], hits) - flux[face]
     for face, hits in enumerate(face_hits(face_ref, cells)):
-        arrived = halo_rows(shared_refs, face, slice(SUMS, 2 * SUMS))
+        base = halo_rows(shared_refs, face, slice(0, SUMS))
+        count = len(kept(face))
+        own = halo_rows(shared_refs, face, slice(SUMS + NOTES, SUMS + NOTES + count))
+        arrived = flux_rows(base, {face: own}, face)
         found = exact(arrived, hits.astype(BF16), ((1,), (1,)))
         gas += jnp.where(mask_ref[face : face + 1, :] != 1, found, 0.0)
 
@@ -512,7 +546,7 @@
     count = rows // 2
     planes, upward = planes_y(2 * width)
     cell_start = lax.axis_index("space") * rows
-    notes = shared_rows(shared_refs, 2 * SUMS, 2 * SUMS + NOTES)
+    notes = shared_rows(shared_refs, SUMS, SUMS + NOTES)
     passing = jnp.where(notes[:FACES] != 1.0, 1.0, 0.0)
     lane = lax.broadcasted_iota(jnp.int32, (1, rows), 1)
     picked = [
@@ -570,7 +604,7 @@
     width = values_ref.shape[1]
     shared_refs, (out_ref, columns_ref) = refs[:-2], refs[-2:]
     sums = shared_rows(shared_refs, 0, SUMS)
-    notes = shared_rows(shared_refs, 2 * SUMS, 2 * SUMS + NOTES)
+    notes = shared_rows(shared_refs, SUMS, SUMS + NOTES)
     back = jnp.where(notes[:FACES] == 1.0, notes[6:7], 0.0)
     columns_ref[...] = columns_of(sums, back, 2 * width, TIME_STEP, 1.0)
     relax(columns_ref, base_ref, values_ref, shape_ref, out_ref, half=True)
@@ -628,7 +662,7 @@
     )(*arrays)
 
 
-COST = {"advance_kernel": 10**9, "relax_kernel": 10**9, "last_kernel_0": 10**9}
+COST = {"advance_kernel": 13 * 10**8, "last_kernel_0": 4 * 10**9}
 
 
 def total(value):
@@ -658,12 +692,12 @@
     count, half = cells // 2, width // 2
     temp = wall_temp[None, :]
     whole, plane = ((cells, width), F32), ((cells, half), F32)
-    every = SUMS * (FACES + 1)
+    every = flux_start(FACES)
     columns = pltpu.VMEM((cells, LANES), F32)
 
-    (sent,) = call(near_plane_kernel, [plane], [face_rows, dist], scalars=1)
+    (sums,) = call(sums_kernel, [((every, cells), F32)], [dist])
+    (sent,) = call(near_plane_kernel, [plane], [face_rows, dist, sums], scalars=1, unread=(2,))
     near = exchange(sent)
-    (sums,) = call(sums_kernel, [((every, cells), F32)], [dist])
     sums = total(sums)
     shape, back, side, notes = call(
         wall_kernel,

time: 35.4 us -> 32.2 us (0.910)
  waiting for transfers between devices: 9.48 us -> 6.87 us
    ppermute x4, waiting for transfers between devices: 2.3 us -> 0.01 us  [exchange(): return [lax.ppermute(send, 'space', forward)]]
  transfers between devices with their start and end apart: 8 -> 8, of which waited for: 5 -> 4; matrix products, arithmetic and copies ran while one was open for 0% -> 0% of each run, Pallas kernels for 28% -> 28%
where the time goes in v6:
time: 32.2 us; the launch traced here: 32 us
  Pallas kernels  11.7 us (36%)
  starting transfers between devices  11.5 us (36%)
  waiting for transfers between devices  6.87 us (21%)
  local copies, waits for them, and re-layouts  1.72 us (5%)
    pallas_call x15, Pallas kernels, call(): pl.pallas_call(kernel, out_shape=[jax.ShapeDtypeStruct(shape, dtype) for...  11.7 us
    ppermute x4, waiting for transfers between devices, total(): lax.ppermute(value, 'vel', [(i, i ^ step) for i in range(count)])  6.86 us
    ppermute x4, starting transfers between devices, total(): lax.ppermute(value, 'vel', [(i, i ^ step) for i in range(count)])  5.84 us
    ppermute x4, starting transfers between devices, exchange(): return [lax.ppermute(send, 'space', forward)]  5.69 us
    unnamed x12, local copies, waits for them, and re-layouts  1.72 us
  transfers between devices with their start and end apart: 8, of which 4 were waited for; matrix products, arithmetic and copies ran while one was open for 0% of the time, Pallas kernels for 28%

profile of v6, /device:TPU:0, one launch (start us, length us, event | category | flops | bytes accessed | tf_op | source)
XLA Modules:
  0.0 32.0 jit_solution(9018739322526442957)
XLA Ops:
  0.0 0.0 copy-start
  0.0 1.2 %copy-done = f32[128,2048]{1,0:T(8,128)S(1)} copy-done((f32[128,2048]{1,0:T(8,128)S(1)}, f32[128,2048]{1,0:T(8,128)}, u32[]{:S(2)}) %copy-start) | copy-done | bytes 1048600
  1.2 0.0 copy-start.1
  1.2 0.0 copy-start.4
  1.2 0.8 %sums_kernel.1._ = f32[88,128]{1,0:T(8,128)S(1)} custom-call(f32[128,2048]{1,0:T(8,128)S(1)} %copy-done), custom_call_target="tpu_custom_call" | custom-call | bytes 1048576 | tf_op jit(solution)/shard_map/sums_kernel/pallas_call | solution.py:650
  2.0 0.4 %copy-done.1 = f32[128,2048]{1,0:T(8,128)S(1)} copy-done((f32[128,2048]{1,0:T(8,128)S(1)}, f32[128,2048]{1,0:T(8,128)}, u32[]{:S(2)}) %copy-start.1) | copy-done | bytes 1048600
  2.5 0.0 copy-done.4
  2.5 1.0 %near_plane_kernel.1 = f32[128,1024]{1,0:T(8,128)S(1)} custom-call(s32[1,2,64]{2,1,0:T(2,128)S(1)} %copy-done.4, f32[128,2048]{1,0:T(8,128)S(1)} %copy-done.1, f32[88,128]{1,0:T(8,128)S(1)} %sums_kernel.1._), custom_call_target="tpu_custom_call" | custom-call | bytes 1094144 | tf_op jit(solution)/shard_map/near_plane_kernel/pallas_call | solution.py:650
  3.4 3.0 %collective-permute-start.4 = (f32[128,1024]{1,0:T(8,128)S(1)}, f32[128,1024]{1,0:T(8,128)S(1)}, u32[]{:S(2)}, u32[]{:S(2)}) collective-permute-start(f32[128,1024]{1,0:T(8,128)S(1)} %near_plane_kernel.1), channel_id=1, source_target_pairs={{0,16},{16,0},{1,17},{17,1},{2,18},{18,2},{3,19},{19,3},{4,20},{20... | collective-permute-start | bytes 1572872 | tf_op jit(solution)/shard_map/ppermute | solution.py:682
  6.5 0.0 collective-permute-start
  6.5 1.2 %collective-permute-done = f32[88,128]{1,0:T(8,128)S(1)} collective-permute-done((f32[88,128]{1,0:T(8,128)S(1)}, f32[88,128]{1,0:T(8,128)S(1)}, u32[]{:S(2)}, u32[]{:S(2)}) %collective-permute-start) | collective-permute-done | bytes 45088 | tf_op jit(solution)/shard_map/ppermute | solution.py:672
  7.7 1.6 %collective-permute-start.1 = (f32[88,128]{1,0:T(8,128)S(1)}, f32[88,128]{1,0:T(8,128)S(1)}, u32[]{:S(2)}, u32[]{:S(2)}) collective-permute-start(f32[88,128]{1,0:T(8,128)S(1)} %add.12), channel_id=1, source_target_pairs={{0,2},{1,3},{2,0},{3,1},{4,6},{5,7},{6,4},{7,5},{8,10},{9,11},{10,... | collective-permute-start | bytes 135176 | tf_op jit(solution)/shard_map/ppermute | solution.py:672
  9.3 0.8 %far_plane_kernel_0.1 = f32[128,512]{1,0:T(8,128)S(1)} custom-call(s32[1,2,64]{2,1,0:T(2,128)S(1)} %copy-done.4, f32[128,2048]{1,0:T(8,128)S(1)} %copy-done.1), custom_call_target="tpu_custom_call" | custom-call | bytes 1049088 | tf_op jit(solution)/shard_map/far_plane_kernel_0/pallas_call | solution.py:650
  10.1 0.6 %collective-permute-start.6 = (f32[128,512]{1,0:T(8,128)S(1)}, f32[128,512]{1,0:T(8,128)S(1)}, u32[]{:S(2)}, u32[]{:S(2)}) collective-permute-start(f32[128,512]{1,0:T(8,128)S(1)} %far_plane_kernel_0.1), channel_id=1, source_target_pairs={{0,16},{16,0},{1,17},{17,1},{2,18},{18,2},{3,19},{19,3},{4,20},{20... | collective-permute-start | bytes 786440 | tf_op jit(solution)/shard_map/ppermute | solution.py:682
  10.7 1.1 %collective-permute-done.1 = f32[88,128]{1,0:T(8,128)S(1)} collective-permute-done((f32[88,128]{1,0:T(8,128)S(1)}, f32[88,128]{1,0:T(8,128)S(1)}, u32[]{:S(2)}, u32[]{:S(2)}) %collective-permute-start.1) | collective-permute-done | bytes 45088 | tf_op jit(solution)/shard_map/ppermute | solution.py:672
  11.8 1.6 %collective-permute-start.2 = (f32[88,128]{1,0:T(8,128)S(1)}, f32[88,128]{1,0:T(8,128)S(1)}, u32[]{:S(2)}, u32[]{:S(2)}) collective-permute-start(f32[88,128]{1,0:T(8,128)S(1)} %add.13), channel_id=1, source_target_pairs={{0,4},{1,5},{2,6},{3,7},{4,0},{5,1},{6,2},{7,3},{8,12},{9,13},{10,... | collective-permute-start | bytes 135176 | tf_op jit(solution)/shard_map/ppermute | solution.py:672
  13.5 2.5 %collective-permute-done.2 = f32[88,128]{1,0:T(8,128)S(1)} collective-permute-done((f32[88,128]{1,0:T(8,128)S(1)}, f32[88,128]{1,0:T(8,128)S(1)}, u32[]{:S(2)}, u32[]{:S(2)}) %collective-permute-start.2) | collective-permute-done | bytes 45088 | tf_op jit(solution)/shard_map/ppermute | solution.py:672
  15.9 0.0 copy-start.3
  15.9 0.0 copy-start.5
  16.0 2.7 %collective-permute-start.3 = (f32[88,128]{1,0:T(8,128)S(1)}, f32[88,128]{1,0:T(8,128)S(1)}, u32[]{:S(2)}, u32[]{:S(2)}) collective-permute-start(f32[88,128]{1,0:T(8,128)S(1)} %add.14), channel_id=1, source_target_pairs={{0,8},{1,9},{2,10},{3,11},{4,12},{5,13},{6,14},{7,15},{8,0},{9,1},... | collective-permute-start | bytes 135176 | tf_op jit(solution)/shard_map/ppermute | solution.py:672
  18.6 0.0 copy-done.3
  18.6 0.0 copy-done.5
  18.6 0.3 wall_kernel.1
  18.9 2.0 %collective-permute-done.3 = f32[88,128]{1,0:T(8,128)S(1)} collective-permute-done((f32[88,128]{1,0:T(8,128)S(1)}, f32[88,128]{1,0:T(8,128)S(1)}, u32[]{:S(2)}, u32[]{:S(2)}) %collective-permute-start.3) | collective-permute-done | bytes 45088 | tf_op jit(solution)/shard_map/ppermute | solution.py:672
  21.0 0.0 copy-start.2
  21.0 0.2 share_kernel.1.refs_0_
  21.1 0.4 %collective-permute-start.5 = (f32[80,64]{1,0:T(8,128)S(1)}, f32[80,64]{1,0:T(8,128)S(1)}, u32[]{:S(2)}, u32[]{:S(2)}) collective-permute-start(f32[80,64]{1,0:T(8,128)S(1)} %share_kernel.1.refs_0_), channel_id=1, source_target_pairs={{0,16},{16,0},{1,17},{17,1},{2,18},{18,2},{3,19},{19,3},{4,20},{20... | collective-permute-start | bytes 61448 | tf_op jit(solution)/shard_map/ppermute | solution.py:682
  21.6 0.1 copy-done.2
  21.7 0.8 %stream_kernel.1.stream_ref = f32[128,2048]{1,0:T(8,128)S(1)} custom-call(s32[6,128]{1,0:T(8,128)S(1)} %copy-done.2, s32[6,128]{1,0:T(8,128)S(1)} %copy-done.3, f32[128,2048]{1,0:T(8,128)S(1)} %copy-done.1), custom_call_target="tpu_custom_call" | custom-call | bytes 1054720 | tf_op jit(solution)/shard_map/stream_kernel/pallas_call | solution.py:650
  22.5 0.8 %far_plane_kernel_1.1 = f32[128,512]{1,0:T(8,128)S(1)} custom-call(s32[1,2,64]{2,1,0:T(2,128)S(1)} %copy-done.4, f32[128,2048]{1,0:T(8,128)S(1)} %copy-done.1, f32[80,64]{1,0:T(8,128)S(1)} %share_kernel.1.refs_0_), custom_call_target="tpu_custom_call" | custom-call | bytes 1069568 | tf_op jit(solution)/shard_map/far_plane_kernel_1/pallas_call | solution.py:650
  23.3 1.6 %collective-permute-start.7 = (f32[128,512]{1,0:T(8,128)S(1)}, f32[128,512]{1,0:T(8,128)S(1)}, u32[]{:S(2)}, u32[]{:S(2)}) collective-permute-start(f32[128,512]{1,0:T(8,128)S(1)} %far_plane_kernel_1.1), channel_id=1, source_target_pairs={{0,16},{16,0},{1,17},{17,1},{2,18},{18,2},{3,19},{19,3},{4,20},{20... | collective-permute-start | bytes 786440 | tf_op jit(solution)/shard_map/ppermute | solution.py:682
  25.0 0.0 collective-permute-done.4.refs_0_.refs_1_
  25.0 1.0 %middle_kernel.1.middle_ref = f32[128,2048]{1,0:T(8,128)S(1)} custom-call(f32[88,128]{1,0:T(8,128)S(1)} %add.15.sums_ref, f32[8,128]{1,0:T(8,128)S(1)} %get-tuple-element.14.back_ref, bf16[256,128]{1,0:T(8,128)(2,1)S(1)} %get-tuple-element.13.side_ref, f32[128,2048]{1,0:T(8,128)S(1)} %copy-done.1, f32[128,2048]{1,0:T(8,128)S(1)} %stream_kernel.1.stream_ref, ...), custom_call_target="tpu_custom_call" | custom-call | bytes 3850240 | tf_op jit(solution)/shard_map/middle_kernel/pallas_call | solution.py:650
  26.0 0.9 %stream_last_kernel.1._.part_ref = f32[128,2048]{1,0:T(8,128)S(1)} custom-call(s32[6,128]{1,0:T(8,128)S(1)} %copy-done.2, s32[6,128]{1,0:T(8,128)S(1)} %copy-done.3, f32[128,2048]{1,0:T(8,128)S(1)} %copy-done.1, f32[128,2048]{1,0:T(8,128)S(1)} %middle_kernel.1.middle_ref), custom_call_target="tpu_custom_call" | custom-call | bytes 2103296 | tf_op jit(solution)/shard_map/stream_last_kernel/pallas_call | solution.py:650
  26.9 0.0 collective-permute-done.5.refs_0_
  27.0 0.4 %advance_kernel.1.sums_ref = f32[16,128]{1,0:T(8,128)S(1)} custom-call(s32[1,2,64]{2,1,0:T(2,128)S(1)} %copy-done.4, s32[6,128]{1,0:T(8,128)S(1)} %copy-done.2, f32[128,2048]{1,0:T(8,128)S(1)} %stream_last_kernel.1._.part_ref, s32[6,128]{1,0:T(8,128)S(1)} %copy-done.3, f32[88,128]{1,0:T(8,128)S(1)} %add.15.sums_ref, ...), custom_call_target="tpu_custom_call" | custom-call | flops 1300000000 | bytes 1124864 | tf_op jit(solution)/shard_map/advance_kernel/pallas_call | solution.py:650
  27.4 0.9 %relax_kernel.1.part_ref = f32[128,2048]{1,0:T(8,128)S(1)} custom-call(f32[16,128]{1,0:T(8,128)S(1)} %advance_kernel.1.sums_ref, f32[8,128]{1,0:T(8,128)S(1)} %get-tuple-element.14.back_ref, f32[128,2048]{1,0:T(8,128)S(1)} %middle_kernel.1.middle_ref, f32[128,2048]{1,0:T(8,128)S(1)} %stream_last_kernel.1._.part_ref, f32[128,2048]{1,0:T(8,128)S(1)} %get-tuple-element.15.shape_ref), custom_call_target="tpu_custom_call" | custom-call | bytes 3158016 | tf_op jit(solution)/shard_map/relax_kernel/pallas_call | solution.py:650
  28.3 1.0 %halo_stream_kernel.1 = (f32[128,1024]{1,0:T(8,128)S(1)}, f32[128,1024]{1,0:T(8,128)S(1)}, f32[128,1024]{1,0:T(8,128)S(1)}, f32[128,128]{1,0:T(8,128)S(1)}) custom-call(s32[1,2,64]{2,1,0:T(2,128)S(1)} %copy-done.4, s32[6,128]{1,0:T(8,128)S(1)} %copy-done.2, f32[80,64]{1,0:T(8,128)S(1)} %collective-permute-done.5.refs_0_, ...), custom_call_target="tpu_custom_call" | custom-call | bytes 548352 | tf_op jit(solution)/shard_map/halo_stream_kernel/pallas_call | solution.py:650
  29.3 0.7 %halo_relax_kernel.1.plane_ref = f32[128,1024]{1,0:T(8,128)S(1)} custom-call(f32[128,1024]{1,0:T(8,128)S(1)} %get-tuple-element.17.base_ref, f32[128,1024]{1,0:T(8,128)S(1)} %get-tuple-element.18.shape_ref, f32[128,1024]{1,0:T(8,128)S(1)} %get-tuple-element.19.values_ref, f32[80,64]{1,0:T(8,128)S(1)} %collective-permute-done.5.refs_0_), custom_call_target="tpu_custom_call" | custom-call | bytes 1593344 | tf_op jit(solution)/shard_map/halo_relax_kernel/pallas_call | solution.py:650
  29.9 0.0 collective-permute-done.6.refs_0_
  30.0 1.0 %last_kernel_0.1.refs_0_ = f32[128,2048]{1,0:T(8,128)} custom-call(bf16[256,128]{1,0:T(8,128)(2,1)S(1)} %get-tuple-element.13.side_ref, f32[128,2048]{1,0:T(8,128)S(1)} %relax_kernel.1.part_ref, f32[128,1024]{1,0:T(8,128)S(1)} %halo_relax_kernel.1.plane_ref, f32[128,128]{1,0:T(8,128)S(1)} %get-tuple-element.20.open_ref, ...), custom_call_target="tpu_custom_call" | custom-call | flops 4000000000 | bytes 2031616 | tf_op jit(solution)/shard_map/last_kernel_0/pallas_call | solution.py:650
  31.0 0.0 collective-permute-done.7.refs_1_
  31.0 1.0 %last_kernel_1.1 = f32[128,2048]{1,0:T(8,128)} custom-call(bf16[256,128]{1,0:T(8,128)(2,1)S(1)} %get-tuple-element.13.side_ref, f32[128,2048]{1,0:T(8,128)S(1)} %relax_kernel.1.part_ref, f32[128,1024]{1,0:T(8,128)S(1)} %halo_relax_kernel.1.plane_ref, f32[128,128]{1,0:T(8,128)S(1)} %get-tuple-element.20.open_ref, ...), custom_call_target="tpu_custom_call", output_to_operand_aliasing={{}: (4, {})} | custom-call | bytes 3080192 | tf_op jit(solution)/shard_map/last_kernel_1/pallas_call | solution.py:650
  (4 shorter events, 0.0 us)
Async XLA Ops:
  0.0 1.2 %copy-start = (f32[128,2048]{1,0:T(8,128)S(1)}, f32[128,2048]{1,0:T(8,128)}, u32[]{:S(2)}) copy-start(f32[128,2048]{1,0:T(8,128)} %dist_ref.9) | copy-start | bytes 3145732
  1.2 1.2 %copy-start.1 = (f32[128,2048]{1,0:T(8,128)S(1)}, f32[128,2048]{1,0:T(8,128)}, u32[]{:S(2)}) copy-start(f32[128,2048]{1,0:T(8,128)} %dist_ref.9) | copy-start | bytes 3145732
  1.2 1.2 %copy-start.4 = (s32[1,2,64]{2,1,0:T(2,128)S(1)}, s32[1,2,64]{2,1,0:T(2,128)}, u32[]{:S(2)}) copy-start(s32[1,2,64]{2,1,0:T(2,128)} %rows_ref.5) | copy-start | bytes 1540
  3.4 21.5 %collective-permute-start.4 = (f32[128,1024]{1,0:T(8,128)S(1)}, f32[128,1024]{1,0:T(8,128)S(1)}, u32[]{:S(2)}, u32[]{:S(2)}) collective-permute-start(f32[128,1024]{1,0:T(8,128)S(1)} %near_plane_kernel.1), channel_id=1, source_target_pairs={{0,16},{16,0},{1,17},{17,1},{2,18},{18,2},{3,19},{19,3},{4,20},{20... | collective-permute-start | bytes 1572872 | tf_op jit(solution)/shard_map/ppermute | solution.py:682
  6.5 1.2 %collective-permute-start = (f32[88,128]{1,0:T(8,128)S(1)}, f32[88,128]{1,0:T(8,128)S(1)}, u32[]{:S(2)}, u32[]{:S(2)}) collective-permute-start(f32[88,128]{1,0:T(8,128)S(1)} %sums_kernel.1._), channel_id=1, source_target_pairs={{0,1},{1,0},{2,3},{3,2},{4,5},{5,4},{6,7},{7,6},{8,9},{9,8},{10,11... | collective-permute-start | bytes 135176 | tf_op jit(solution)/shard_map/ppermute | solution.py:672
  7.7 4.1 %collective-permute-start.1 = (f32[88,128]{1,0:T(8,128)S(1)}, f32[88,128]{1,0:T(8,128)S(1)}, u32[]{:S(2)}, u32[]{:S(2)}) collective-permute-start(f32[88,128]{1,0:T(8,128)S(1)} %add.12), channel_id=1, source_target_pairs={{0,2},{1,3},{2,0},{3,1},{4,6},{5,7},{6,4},{7,5},{8,10},{9,11},{10,... | collective-permute-start | bytes 135176 | tf_op jit(solution)/shard_map/ppermute | solution.py:672
  10.1 19.8 %collective-permute-start.6 = (f32[128,512]{1,0:T(8,128)S(1)}, f32[128,512]{1,0:T(8,128)S(1)}, u32[]{:S(2)}, u32[]{:S(2)}) collective-permute-start(f32[128,512]{1,0:T(8,128)S(1)} %far_plane_kernel_0.1), channel_id=1, source_target_pairs={{0,16},{16,0},{1,17},{17,1},{2,18},{18,2},{3,19},{19,3},{4,20},{20... | collective-permute-start | bytes 786440 | tf_op jit(solution)/shard_map/ppermute | solution.py:682
  11.8 4.1 %collective-permute-start.2 = (f32[88,128]{1,0:T(8,128)S(1)}, f32[88,128]{1,0:T(8,128)S(1)}, u32[]{:S(2)}, u32[]{:S(2)}) collective-permute-start(f32[88,128]{1,0:T(8,128)S(1)} %add.13), channel_id=1, source_target_pairs={{0,4},{1,5},{2,6},{3,7},{4,0},{5,1},{6,2},{7,3},{8,12},{9,13},{10,... | collective-permute-start | bytes 135176 | tf_op jit(solution)/shard_map/ppermute | solution.py:672
  15.9 2.7 %copy-start.3 = (s32[6,128]{1,0:T(8,128)S(1)}, s32[6,128]{1,0:T(8,128)}, u32[]{:S(2)}) copy-start(s32[6,128]{1,0:T(8,128)} %mask_ref.7) | copy-start | bytes 9220
  15.9 2.7 %copy-start.5 = (f32[128]{0:T(128)S(1)}, f32[128]{0:T(128)}, u32[]{:S(2)}) copy-start(f32[128]{0:T(128)} %param.6) | copy-start | bytes 1540
  16.0 5.0 %collective-permute-start.3 = (f32[88,128]{1,0:T(8,128)S(1)}, f32[88,128]{1,0:T(8,128)S(1)}, u32[]{:S(2)}, u32[]{:S(2)}) collective-permute-start(f32[88,128]{1,0:T(8,128)S(1)} %add.14), channel_id=1, source_target_pairs={{0,8},{1,9},{2,10},{3,11},{4,12},{5,13},{6,14},{7,15},{8,0},{9,1},... | collective-permute-start | bytes 135176 | tf_op jit(solution)/shard_map/ppermute | solution.py:672
  21.0 0.7 %copy-start.2 = (s32[6,128]{1,0:T(8,128)S(1)}, s32[6,128]{1,0:T(8,128)}, u32[]{:S(2)}) copy-start(s32[6,128]{1,0:T(8,128)} %near_ref.7) | copy-start | bytes 9220
  21.1 5.8 %collective-permute-start.5 = (f32[80,64]{1,0:T(8,128)S(1)}, f32[80,64]{1,0:T(8,128)S(1)}, u32[]{:S(2)}, u32[]{:S(2)}) collective-permute-start(f32[80,64]{1,0:T(8,128)S(1)} %share_kernel.1.refs_0_), channel_id=1, source_target_pairs={{0,16},{16,0},{1,17},{17,1},{2,18},{18,2},{3,19},{19,3},{4,20},{20... | collective-permute-start | bytes 61448 | tf_op jit(solution)/shard_map/ppermute | solution.py:682
  23.3 7.6 %collective-permute-start.7 = (f32[128,512]{1,0:T(8,128)S(1)}, f32[128,512]{1,0:T(8,128)S(1)}, u32[]{:S(2)}, u32[]{:S(2)}) collective-permute-start(f32[128,512]{1,0:T(8,128)S(1)} %far_plane_kernel_1.1), channel_id=1, source_target_pairs={{0,16},{16,0},{1,17},{17,1},{2,18},{18,2},{3,19},{19,3},{4,20},{20... | collective-permute-start | bytes 786440 | tf_op jit(solution)/shard_map/ppermute | solution.py:682

commit v7 on v6

--- a/solution.py
+++ b/solution.py
@@ -155,7 +155,7 @@
     sums_ref[...] = total
 
 
-def share_kernel(face_ref, sums_ref, notes_ref, send_ref):
+def share_kernel(face_ref, sums_ref, notes_ref, _, send_ref):
     low, high = face_hits(face_ref, sums_ref.shape[1])
     for side, hits in ((0, high), (1, low)):
         rows = [sums_ref[:SUMS], notes_ref[...], sums_ref[flux_start(side) : flux_start(side + 1)]]
@@ -189,13 +189,15 @@
     count = cells // 2
     low, high = half_tiles(width, part, parts)
     begin = low[0][1]
+    piece = min(HALF, send_ref.shape[1])
+    step = piece // COLUMN_TILE
 
     def move(at, _):
         for first, tiles, plane in ((0, high, 1 - crossed), (count, low, crossed)):
             row = rows_ref[0, plane, at]
-            for source, target in tiles:
-                send_ref[pl.ds(first + at, 1), target - begin : target - begin + COLUMN_TILE] = (
-                    value_ref[pl.ds(row, 1), source : source + COLUMN_TILE]
+            for source, target in tiles[::step]:
+                send_ref[pl.ds(first + at, 1), target - begin : target - begin + piece] = (
+                    value_ref[pl.ds(row, 1), source : source + piece]
                 )
         return 0
 
@@ -211,12 +213,17 @@
     return 1.0 / (WEIGHT * flux * mass * mass), cooling
 
 
-def near_plane_kernel(rows_ref, dist_ref, _, send_ref):
+def near_plane_kernel(rows_ref, dist_ref, send_ref):
     move_rows(rows_ref, dist_ref, send_ref, 0)
 
 
-def far_plane_kernel(part, rows_ref, dist_ref, *refs):
-    move_rows(rows_ref, dist_ref, refs[-1], 1, part, PARTS)
+def far_plane_kernel(rows_ref, dist_ref, *send_refs):
+    for part, send_ref in enumerate(send_refs):
+        move_rows(rows_ref, dist_ref, send_ref, 1, part, PARTS)
+
+
+def pass_kernel(value_ref, after_ref, out_ref):
+    pass
 
 
 def picks(near_ref, mask_ref, face, cell_start, cells):
@@ -337,20 +344,22 @@
     return rows, returned
 
 
-def columns_of(sums, back, width, step, keep):
+def columns_of(sums, back, width, step, keep, more=()):
     _, upward = planes_y(width)
     rows, returned = coefficients(sums, back, step, keep)
     rows += [
         jnp.where(upward, returned[2:3], returned[3:4]),
         returned[0:2],
         returned[4:6],
-        jnp.zeros((LANES - 14, sums.shape[1]), F32),
+        *more,
+        jnp.zeros((LANES - 14 - sum(row.shape[0] for row in more), sums.shape[1]), F32),
     ]
     return jnp.concatenate(rows, axis=0).T
 
 
-def relax(columns_ref, base_ref, value_ref, shape_ref, out_ref, half=False):
+def relax(columns_ref, base_ref, value_ref, shape_ref, out_ref, planes_refs=None):
     cells, width = value_ref.shape
+    half = planes_refs is not None
     planes, _ = planes_y(2 * width if half else width)
     lane = lax.broadcasted_iota(jnp.int32, (ROWS, LANES), 1)
     first_x, vel_z = point((lane >> 5) & (NV - 1)), point(lane & (NV - 1))
@@ -360,8 +369,12 @@
         rows = pl.ds(pl.multiple_of(at * ROWS, ROWS), ROWS)
         columns = columns_ref[rows, :]
         flow_x, flow_y, flow_z, cool, heat_x, heat_y, heat_z, gain, keep, back_y, *back = (
-            jnp.broadcast_to(columns[:, column : column + 1], (ROWS, LANES)) for column in range(14)
+            jnp.broadcast_to(columns[:, column : column + 1], (ROWS, LANES))
+            for column in range(18 if half else 14)
         )
+        if half:
+            open_y, open_low, open_high, cooling = back[4:]
+            open_z = jnp.where(vel_z > 0, open_low, open_high)
         rel_z = vel_z - flow_z
         square_z = rel_z * rel_z * cool
         heat_of_z = rel_z * heat_z
@@ -382,11 +395,19 @@
                 lanes = slice(start, start + LANES)
                 square = square_xz + square_y
                 skew = (heat_xz + heat_of_y) * (square + 2.5 * LOG2E) + 1.0
+                base = base_ref[rows, lanes]
+                if half:
+                    from_y_ref, from_z_ref = planes_refs
+                    base += open_y * from_y_ref[rows, lanes] + open_z * from_z_ref[rows, lanes]
+                    speed_sq = vel_x * vel_x + vel_z * vel_z + planes[plane] * planes[plane]
+                    shape = jnp.exp2(speed_sq * cooling)
+                else:
+                    shape = shape_ref[rows, lanes]
                 out_ref[rows, lanes] = (
-                    base_ref[rows, lanes]
+                    base
                     + keep * value_ref[rows, lanes]
                     + gain * jnp.exp2(square) * skew
-                    + shape_ref[rows, lanes] * (back_xz + back_of_y)
+                    + shape * (back_xz + back_of_y)
                 )
         return 0
 
@@ -456,7 +477,7 @@
     return result
 
 
-def advance_kernel(face_ref, near_ref, _, mask_ref, sums_ref, back_ref, *refs):
+def advance_kernel(face_ref, near_ref, _, __, mask_ref, sums_ref, back_ref, *refs):
     shared_refs, out_ref = refs[:-1], refs[-1]
     cells = near_ref.shape[1]
     cell_start = lax.axis_index("space") * cells
@@ -539,28 +560,11 @@
 
 
 def halo_stream_kernel(face_ref, near_ref, *refs):
-    base_ref, shape_ref, values_ref, open_ref = refs[-4:]
-    refs = refs[:-4]
-    shared_refs, halo_refs = refs[: len(refs) // 2], refs[len(refs) // 2 :]
+    halo_refs, (base_ref, from_y_ref, from_z_ref, values_ref) = refs[:-4], refs[-4:]
     rows, width = base_ref.shape
     count = rows // 2
     planes, upward = planes_y(2 * width)
     cell_start = lax.axis_index("space") * rows
-    notes = shared_rows(shared_refs, SUMS, SUMS + NOTES)
-    passing = jnp.where(notes[:FACES] != 1.0, 1.0, 0.0)
-    lane = lax.broadcasted_iota(jnp.int32, (1, rows), 1)
-    picked = [
-        jnp.where(lane < count, passing[0:1], passing[1:2]),
-        jnp.where(upward, passing[2:3], passing[3:4]),
-        passing[4:6],
-        notes[7:8],
-        jnp.zeros((LANES - 5, rows), F32),
-    ]
-    columns = jnp.concatenate(picked, axis=0).T
-    open_x, open_y, open_low, open_high, cooling = (
-        jnp.broadcast_to(columns[:, at : at + 1], (rows, LANES)) for at in range(5)
-    )
-    open_ref[...] = TIME_STEP * open_x
     low = face_hits(face_ref, rows)[0]
     low_flipped, low = low.T.astype(BF16), low.astype(BF16)
     row = lax.broadcasted_iota(jnp.int32, (rows, rows), 0)
@@ -575,10 +579,6 @@
     for side in range(2):
         block = slice(side * count, (side + 1) * count)
         values_ref[block, :] = halo_rows(halo_refs, side)
-
-        def wide(column):
-            return jnp.concatenate([column[block]] * (COLUMN_TILE // LANES), axis=1)
-
         for start in range(0, width, COLUMN_TILE):
             lanes = slice(start, start + COLUMN_TILE)
             vel_x, vel_z = lane_points((1 - side) * HALF + start % HALF, COLUMN_TILE)
@@ -586,28 +586,31 @@
             values = values_ref[block, lanes]
             moved = dot(picks_all, jnp.concatenate(split(values, 2), axis=0))
             speed_x, speed_y, speed_z = jnp.abs(vel_x), jnp.abs(vel_y), jnp.abs(vel_z)
-            from_z = jnp.where(
-                vel_z > 0,
-                wide(open_low) * moved[count : 2 * count],
-                wide(open_high) * moved[2 * count :],
-            )
-            base_ref[block, lanes] = TIME_STEP * (
-                speed_y * (wide(open_y) * moved[:count])
-                + speed_z * from_z
-                - (speed_x + speed_y + speed_z) * values
-            )
-            speed_sq = vel_x * vel_x + vel_y * vel_y + vel_z * vel_z
-            shape_ref[block, lanes] = jnp.exp2(speed_sq * wide(cooling))
-
-
-def halo_relax_kernel(base_ref, shape_ref, values_ref, *refs):
-    width = values_ref.shape[1]
-    shared_refs, (out_ref, columns_ref) = refs[:-2], refs[-2:]
+            from_z = jnp.where(vel_z > 0, moved[count : 2 * count], moved[2 * count :])
+            from_y_ref[block, lanes] = (TIME_STEP * speed_y) * moved[:count]
+            from_z_ref[block, lanes] = (TIME_STEP * speed_z) * from_z
+            base_ref[block, lanes] = -TIME_STEP * (speed_x + speed_y + speed_z) * values
+
+
+def halo_relax_kernel(base_ref, from_y_ref, from_z_ref, values_ref, *refs):
+    shared_refs, (out_ref, open_ref, columns_ref) = refs[:-3], refs[-3:]
+    rows, width = values_ref.shape
+    _, upward = planes_y(2 * width)
     sums = shared_rows(shared_refs, 0, SUMS)
     notes = shared_rows(shared_refs, SUMS, SUMS + NOTES)
     back = jnp.where(notes[:FACES] == 1.0, notes[6:7], 0.0)
-    columns_ref[...] = columns_of(sums, back, 2 * width, TIME_STEP, 1.0)
-    relax(columns_ref, base_ref, values_ref, shape_ref, out_ref, half=True)
+    passing = jnp.where(notes[:FACES] != 1.0, 1.0, 0.0)
+    lane = lax.broadcasted_iota(jnp.int32, (1, rows), 1)
+    more = [
+        jnp.where(upward, passing[2:3], passing[3:4]),
+        passing[4:6],
+        notes[7:8],
+        TIME_STEP * jnp.where(lane < rows // 2, passing[0:1], passing[1:2]),
+    ]
+    columns = columns_of(sums, back, 2 * width, TIME_STEP, 1.0, more)
+    columns_ref[...] = columns
+    open_ref[...] = jnp.broadcast_to(columns[:, 18:19], (rows, LANES))
+    relax(columns_ref, base_ref, values_ref, None, out_ref, (from_y_ref, from_z_ref))
 
 
 def last_kernel(part, side_ref, part_ref, plane_ref, open_ref, *refs):
@@ -662,7 +665,7 @@
     )(*arrays)
 
 
-COST = {"advance_kernel": 13 * 10**8, "last_kernel_0": 4 * 10**9}
+COST = {"advance_kernel": 14 * 10**8, "last_kernel_0": 4 * 10**9}
 
 
 def total(value):
@@ -695,9 +698,10 @@
     every = flux_start(FACES)
     columns = pltpu.VMEM((cells, LANES), F32)
 
+    face_rows = jnp.clip(face_rows, 0, cells - 1)
+    (sent,) = call(near_plane_kernel, [plane], [face_rows, dist], scalars=1)
+    near = exchange(sent)
     (sums,) = call(sums_kernel, [((every, cells), F32)], [dist])
-    (sent,) = call(near_plane_kernel, [plane], [face_rows, dist, sums], scalars=1, unread=(2,))
-    near = exchange(sent)
     sums = total(sums)
     shape, back, side, notes = call(
         wall_kernel,
@@ -706,20 +710,27 @@
     )
     (stream,) = call(stream_kernel, [whole], [neighbours, wall_mask, dist])
     (sent,) = call(
-        share_kernel, [((2 * (2 * SUMS + NOTES), count), F32)], [face_rows, sums, notes]
+        share_kernel,
+        [((2 * (2 * SUMS + NOTES), count), F32)],
+        [face_rows, sums, notes, stream],
+        unread=(3,),
     )
     shared = exchange(sent)
+    part_shape = ((cells, half // PARTS), F32)
+    far_rows = call(far_plane_kernel, [part_shape] * PARTS, [face_rows, dist], scalars=1)
     far = []
     for part in range(PARTS):
-        after = [sent] if part else []
-        (far_rows,) = call(
-            functools.partial(far_plane_kernel, part),
-            [((cells, half // PARTS), F32)],
-            [face_rows, dist, *after],
-            scalars=1,
-            unread=(2,),
-        )
-        far.append(exchange(far_rows))
+        rows = far_rows[part]
+        if part:
+            (rows,) = call(
+                pass_kernel,
+                [part_shape],
+                [rows, sent],
+                far_outs=True,
+                unread=(0, 1),
+                aliases={0: 0},
+            )
+        far.append(exchange(rows))
     (middle,) = call(
         middle_kernel,
         [whole],
@@ -727,20 +738,16 @@
         [columns, pltpu.VMEM((cells, width), F32)],
     )
     (part_sum,) = call(stream_last_kernel, [whole], [neighbours, wall_mask, dist, middle])
+    halo_parts = call(halo_stream_kernel, [plane] * 4, [face_rows, neighbours, *near])
     (sums_two,) = call(
         advance_kernel,
         [((SUMS, cells), F32)],
-        [face_rows, neighbours, part_sum, wall_mask, sums, back, *shared],
-        unread=(2,),
+        [face_rows, neighbours, part_sum, halo_parts[0], wall_mask, sums, back, *shared],
+        unread=(2, 3),
     )
     (part_sum,) = call(relax_kernel, [whole], [sums_two, back, middle, part_sum, shape], [columns])
-    base, halo_shape, values, gate = call(
-        halo_stream_kernel,
-        [plane, plane, plane, ((cells, LANES), F32)],
-        [face_rows, neighbours, *shared, *near],
-    )
-    (plane_one,) = call(
-        halo_relax_kernel, [plane], [base, halo_shape, values, *shared], [columns]
+    plane_one, gate = call(
+        halo_relax_kernel, [plane, ((cells, LANES), F32)], [*halo_parts, *shared], [columns]
     )
     result = []
     for part in range(PARTS):

time: 32.2 us -> 31 us (0.963)
  Pallas kernels: 11.7 us -> 10.8 us
  other arithmetic: 0.03 us -> 0.71 us
  waiting for transfers between devices: 6.87 us -> 6.29 us
  local copies, waits for them, and re-layouts: 1.72 us -> 1.24 us
    ppermute x4, waiting for transfers between devices: 6.86 us -> 5.88 us  [total(): lax.ppermute(value, 'vel', [(i, i ^ step) for i in range(count)])]
    pallas_call x15, Pallas kernels: 11.7 us -> 10.8 us  [call(): pl.pallas_call(kernel, out_shape=[jax.ShapeDtypeStruct(shape, dtype) for...]
    min x0 -> x1, other arithmetic: none -> 0.68 us  [on_device(): face_rows = jnp.clip(face_rows, 0, cells - 1)]
    unnamed x12 -> x10, local copies, waits for them, and re-layouts: 1.72 us -> 1.24 us
    ppermute x4, waiting for transfers between devices: 0.01 us -> 0.41 us  [exchange(): return [lax.ppermute(send, 'space', forward)]]
  transfers between devices with their start and end apart: 8 -> 8, of which waited for: 4 -> 5; matrix products, arithmetic and copies ran while one was open for 0% -> 0% of each run, Pallas kernels for 28% -> 29%
where the time goes in v7:
time: 31 us; the launch traced here: 30.8 us
  starting transfers between devices  11.6 us (37%)
  Pallas kernels  10.8 us (35%)
  waiting for transfers between devices  6.29 us (20%)
  local copies, waits for them, and re-layouts  1.24 us (4%)
  other arithmetic  0.71 us (2%)
    pallas_call x15, Pallas kernels, call(): pl.pallas_call(kernel, out_shape=[jax.ShapeDtypeStruct(shape, dtype) for...  10.8 us
    ppermute x4, starting transfers between devices, total(): lax.ppermute(value, 'vel', [(i, i ^ step) for i in range(count)])  5.91 us
    ppermute x4, waiting for transfers between devices, total(): lax.ppermute(value, 'vel', [(i, i ^ step) for i in range(count)])  5.88 us
    ppermute x4, starting transfers between devices, exchange(): return [lax.ppermute(send, 'space', forward)]  5.69 us
    unnamed x10, local copies, waits for them, and re-layouts  1.24 us
    min x1, other arithmetic, on_device(): face_rows = jnp.clip(face_rows, 0, cells - 1)  0.68 us
  transfers between devices with their start and end apart: 8, of which 5 were waited for; matrix products, arithmetic and copies ran while one was open for 0% of the time, Pallas kernels for 29%

profile of v7, /device:TPU:0, one launch (start us, length us, event | category | flops | bytes accessed | tf_op | source)
XLA Modules:
  0.0 30.8 jit_solution(15521693434219756089)
XLA Ops:
  0.0 0.7 %broadcast_clamp_fusion.face_ref.rows_ref = s32[1,2,64]{2,1,0:T(2,128)S(1)} fusion(s32[1,2,64]{2,1,0:T(2,128)} %param.9), kind=kLoop, calls=%fused_computation | loop fusion | flops 128 | bytes 1024 | tf_op jit(solution)/shard_map/jit(clip)/min | solution.py:701
  0.7 0.0 copy-start
  0.7 1.2 %copy-done = f32[128,2048]{1,0:T(8,128)S(1)} copy-done((f32[128,2048]{1,0:T(8,128)S(1)}, f32[128,2048]{1,0:T(8,128)}, u32[]{:S(2)}) %copy-start) | copy-done | bytes 1048600
  1.9 0.0 copy-start.1
  1.9 0.8 %near_plane_kernel.1 = f32[128,1024]{1,0:T(8,128)S(1)} custom-call(s32[1,2,64]{2,1,0:T(2,128)S(1)} %broadcast_clamp_fusion.face_ref.rows_ref, f32[128,2048]{1,0:T(8,128)S(1)} %copy-done), custom_call_target="tpu_custom_call" | custom-call | bytes 1049088 | tf_op jit(solution)/shard_map/near_plane_kernel/pallas_call | solution.py:653
  2.7 3.0 %collective-permute-start.4 = (f32[128,1024]{1,0:T(8,128)S(1)}, f32[128,1024]{1,0:T(8,128)S(1)}, u32[]{:S(2)}, u32[]{:S(2)}) collective-permute-start(f32[128,1024]{1,0:T(8,128)S(1)} %near_plane_kernel.1), channel_id=1, source_target_pairs={{0,16},{16,0},{1,17},{17,1},{2,18},{18,2},{3,19},{19,3},{4,20},{20... | collective-permute-start | bytes 1572872 | tf_op jit(solution)/shard_map/ppermute | solution.py:685
  5.8 0.0 copy-done.1
  5.8 0.8 %sums_kernel.1 = f32[88,128]{1,0:T(8,128)S(1)} custom-call(f32[128,2048]{1,0:T(8,128)S(1)} %copy-done.1), custom_call_target="tpu_custom_call" | custom-call | bytes 1048576 | tf_op jit(solution)/shard_map/sums_kernel/pallas_call | solution.py:653
  6.6 0.1 collective-permute-start
  6.6 1.2 %collective-permute-done = f32[88,128]{1,0:T(8,128)S(1)} collective-permute-done((f32[88,128]{1,0:T(8,128)S(1)}, f32[88,128]{1,0:T(8,128)S(1)}, u32[]{:S(2)}, u32[]{:S(2)}) %collective-permute-start) | collective-permute-done | bytes 45088 | tf_op jit(solution)/shard_map/ppermute | solution.py:675
  7.9 1.6 %collective-permute-start.1 = (f32[88,128]{1,0:T(8,128)S(1)}, f32[88,128]{1,0:T(8,128)S(1)}, u32[]{:S(2)}, u32[]{:S(2)}) collective-permute-start(f32[88,128]{1,0:T(8,128)S(1)} %add.12), channel_id=1, source_target_pairs={{0,2},{1,3},{2,0},{3,1},{4,6},{5,7},{6,4},{7,5},{8,10},{9,11},{10,... | collective-permute-start | bytes 135176 | tf_op jit(solution)/shard_map/ppermute | solution.py:675
  9.4 1.0 %far_plane_kernel.1 = (f32[128,512]{1,0:T(8,128)S(1)}, f32[128,512]{1,0:T(8,128)S(1)}) custom-call(s32[1,2,64]{2,1,0:T(2,128)S(1)} %broadcast_clamp_fusion.face_ref.rows_ref, f32[128,2048]{1,0:T(8,128)S(1)} %copy-done.1), custom_call_target="tpu_custom_call" | custom-call | bytes 1049088 | tf_op jit(solution)/shard_map/far_plane_kernel/pallas_call | solution.py:653
  10.4 0.6 %collective-permute-start.6 = (f32[128,512]{1,0:T(8,128)S(1)}, f32[128,512]{1,0:T(8,128)S(1)}, u32[]{:S(2)}, u32[]{:S(2)}) collective-permute-start(f32[128,512]{1,0:T(8,128)S(1)} %get-tuple-element.27), channel_id=1, source_target_pairs={{0,16},{16,0},{1,17},{17,1},{2,18},{18,2},{3,19},{19,3},{4,20},{20... | collective-permute-start | bytes 786440 | tf_op jit(solution)/shard_map/ppermute | solution.py:685
  11.0 1.0 %collective-permute-done.1 = f32[88,128]{1,0:T(8,128)S(1)} collective-permute-done((f32[88,128]{1,0:T(8,128)S(1)}, f32[88,128]{1,0:T(8,128)S(1)}, u32[]{:S(2)}, u32[]{:S(2)}) %collective-permute-start.1) | collective-permute-done | bytes 45088 | tf_op jit(solution)/shard_map/ppermute | solution.py:675
  12.0 1.6 %collective-permute-start.2 = (f32[88,128]{1,0:T(8,128)S(1)}, f32[88,128]{1,0:T(8,128)S(1)}, u32[]{:S(2)}, u32[]{:S(2)}) collective-permute-start(f32[88,128]{1,0:T(8,128)S(1)} %add.13), channel_id=1, source_target_pairs={{0,4},{1,5},{2,6},{3,7},{4,0},{5,1},{6,2},{7,3},{8,12},{9,13},{10,... | collective-permute-start | bytes 135176 | tf_op jit(solution)/shard_map/ppermute | solution.py:675
  13.6 2.5 %collective-permute-done.2 = f32[88,128]{1,0:T(8,128)S(1)} collective-permute-done((f32[88,128]{1,0:T(8,128)S(1)}, f32[88,128]{1,0:T(8,128)S(1)}, u32[]{:S(2)}, u32[]{:S(2)}) %collective-permute-start.2) | collective-permute-done | bytes 45088 | tf_op jit(solution)/shard_map/ppermute | solution.py:675
  16.1 0.0 copy-start.3
  16.1 0.0 copy-start.4
  16.1 0.0 copy-start.2
  16.1 2.7 %collective-permute-start.3 = (f32[88,128]{1,0:T(8,128)S(1)}, f32[88,128]{1,0:T(8,128)S(1)}, u32[]{:S(2)}, u32[]{:S(2)}) collective-permute-start(f32[88,128]{1,0:T(8,128)S(1)} %add.14), channel_id=1, source_target_pairs={{0,8},{1,9},{2,10},{3,11},{4,12},{5,13},{6,14},{7,15},{8,0},{9,1},... | collective-permute-start | bytes 135176 | tf_op jit(solution)/shard_map/ppermute | solution.py:675
  18.8 0.0 copy-done.3
  18.8 0.0 copy-done.4
  18.8 0.3 %wall_kernel.1 = (f32[128,2048]{1,0:T(8,128)S(1)}, f32[8,128]{1,0:T(8,128)S(1)}, bf16[256,128]{1,0:T(8,128)(2,1)S(1)}, f32[8,128]{1,0:T(8,128)S(1)}) custom-call(s32[1,2,64]{2,1,0:T(2,128)S(1)} %broadcast_clamp_fusion.face_ref.rows_ref, f32[1,128]{1,0:T(1,128)S(1)} %bitcast.1, s32[6,128]{1,0:T(8,128)S(1)} %copy-done.3), custom_call_target="tpu_custom_call" | custom-call | bytes 4096 | tf_op jit(solution)/shard_map/wall_kernel/pallas_call | solution.py:653
  19.1 0.0 copy-done.2
  19.1 0.8 %stream_kernel.1.stream_ref._ = f32[128,2048]{1,0:T(8,128)S(1)} custom-call(s32[6,128]{1,0:T(8,128)S(1)} %copy-done.2, s32[6,128]{1,0:T(8,128)S(1)} %copy-done.3, f32[128,2048]{1,0:T(8,128)S(1)} %copy-done.1), custom_call_target="tpu_custom_call" | custom-call | bytes 1054720 | tf_op jit(solution)/shard_map/stream_kernel/pallas_call | solution.py:653
  19.9 1.2 %collective-permute-done.3 = f32[88,128]{1,0:T(8,128)S(1)} collective-permute-done((f32[88,128]{1,0:T(8,128)S(1)}, f32[88,128]{1,0:T(8,128)S(1)}, u32[]{:S(2)}, u32[]{:S(2)}) %collective-permute-start.3) | collective-permute-done | bytes 45088 | tf_op jit(solution)/shard_map/ppermute | solution.py:675
  21.1 0.2 share_kernel.1.after_ref
  21.3 0.6 %collective-permute-start.5 = (f32[80,64]{1,0:T(8,128)S(1)}, f32[80,64]{1,0:T(8,128)S(1)}, u32[]{:S(2)}, u32[]{:S(2)}) collective-permute-start(f32[80,64]{1,0:T(8,128)S(1)} %share_kernel.1.after_ref), channel_id=1, source_target_pairs={{0,16},{16,0},{1,17},{17,1},{2,18},{18,2},{3,19},{19,3},{4,20},{20... | collective-permute-start | bytes 61448 | tf_op jit(solution)/shard_map/ppermute | solution.py:685
  21.9 1.5 %collective-permute-start.7 = (f32[128,512]{1,0:T(8,128)S(1)}, f32[128,512]{1,0:T(8,128)S(1)}, u32[]{:S(2)}, u32[]{:S(2)}) collective-permute-start(f32[128,512]{1,0:T(8,128)S(1)} %pass_kernel.1), channel_id=1, source_target_pairs={{0,16},{16,0},{1,17},{17,1},{2,18},{18,2},{3,19},{19,3},{4,20},{20... | collective-permute-start | bytes 786440 | tf_op jit(solution)/shard_map/ppermute | solution.py:685
  23.4 0.0 collective-permute-done.4.refs_0_
  23.4 1.0 %middle_kernel.1.middle_ref = f32[128,2048]{1,0:T(8,128)S(1)} custom-call(f32[88,128]{1,0:T(8,128)S(1)} %add.15.sums_ref, f32[8,128]{1,0:T(8,128)S(1)} %get-tuple-element.18.back_ref, bf16[256,128]{1,0:T(8,128)(2,1)S(1)} %get-tuple-element.17.side_ref, f32[128,2048]{1,0:T(8,128)S(1)} %copy-done.1, f32[128,2048]{1,0:T(8,128)S(1)} %stream_kernel.1.stream_ref._, ...), custom_call_target="tpu_custom_call" | custom-call | bytes 3850240 | tf_op jit(solution)/shard_map/middle_kernel/pallas_call | solution.py:653
  24.4 0.9 %stream_last_kernel.1._.part_ref = f32[128,2048]{1,0:T(8,128)S(1)} custom-call(s32[6,128]{1,0:T(8,128)S(1)} %copy-done.2, s32[6,128]{1,0:T(8,128)S(1)} %copy-done.3, f32[128,2048]{1,0:T(8,128)S(1)} %copy-done.1, f32[128,2048]{1,0:T(8,128)S(1)} %middle_kernel.1.middle_ref), custom_call_target="tpu_custom_call" | custom-call | bytes 2103296 | tf_op jit(solution)/shard_map/stream_last_kernel/pallas_call | solution.py:653
  25.3 0.8 %halo_stream_kernel.1 = (f32[128,1024]{1,0:T(8,128)S(1)}, f32[128,1024]{1,0:T(8,128)S(1)}, f32[128,1024]{1,0:T(8,128)S(1)}, f32[128,1024]{1,0:T(8,128)S(1)}) custom-call(s32[1,2,64]{2,1,0:T(2,128)S(1)} %broadcast_clamp_fusion.face_ref.rows_ref, s32[6,128]{1,0:T(8,128)S(1)} %copy-done.2, f32[128,1024]{1,0:T(8,128)S(1)} %collective-permute-done.4.refs_0_), custom_call_target="tpu_custom_call" | custom-call | bytes 527872 | tf_op jit(solution)/shard_map/halo_stream_kernel/pallas_call | solution.py:653
  26.1 0.0 collective-permute-done.5.refs_0_
  26.2 0.4 %advance_kernel.1.sums_ref = f32[16,128]{1,0:T(8,128)S(1)} custom-call(s32[1,2,64]{2,1,0:T(2,128)S(1)} %broadcast_clamp_fusion.face_ref.rows_ref, s32[6,128]{1,0:T(8,128)S(1)} %copy-done.2, f32[128,2048]{1,0:T(8,128)S(1)} %stream_last_kernel.1._.part_ref, f32[128,1024]{1,0:T(8,128)S(1)} %get-tuple-element.20.__.base_ref, s32[6,128]{1,0:T(8,128)S(1)} %copy-done.3, ...), custom_call_target="tpu_custom_call" | custom-call | flops 1400000000 | bytes 1649152 | tf_op jit(solution)/shard_map/advance_kernel/pallas_call | solution.py:653
  26.6 0.9 %relax_kernel.1.part_ref = f32[128,2048]{1,0:T(8,128)S(1)} custom-call(f32[16,128]{1,0:T(8,128)S(1)} %advance_kernel.1.sums_ref, f32[8,128]{1,0:T(8,128)S(1)} %get-tuple-element.18.back_ref, f32[128,2048]{1,0:T(8,128)S(1)} %middle_kernel.1.middle_ref, f32[128,2048]{1,0:T(8,128)S(1)} %stream_last_kernel.1._.part_ref, f32[128,2048]{1,0:T(8,128)S(1)} %get-tuple-element.19.shape_ref), custom_call_target="tpu_custom_call" | custom-call | bytes 3158016 | tf_op jit(solution)/shard_map/relax_kernel/pallas_call | solution.py:653
  27.5 0.9 %halo_relax_kernel.1 = (f32[128,1024]{1,0:T(8,128)S(1)}, f32[128,128]{1,0:T(8,128)S(1)}) custom-call(f32[128,1024]{1,0:T(8,128)S(1)} %get-tuple-element.20.__.base_ref, f32[128,1024]{1,0:T(8,128)S(1)} %get-tuple-element.22.from_y_ref, f32[128,1024]{1,0:T(8,128)S(1)} %get-tuple-element.23.from_z_ref, f32[128,1024]{1,0:T(8,128)S(1)} %get-tuple-element.24.values_ref, ...), custom_call_target="tpu_custom_call" | custom-call | bytes 2117632 | tf_op jit(solution)/shard_map/halo_relax_kernel/pallas_call | solution.py:653
  28.3 0.0 collective-permute-done.6.refs_0_
  28.3 1.0 %last_kernel_0.1.refs_0_ = f32[128,2048]{1,0:T(8,128)} custom-call(bf16[256,128]{1,0:T(8,128)(2,1)S(1)} %get-tuple-element.17.side_ref, f32[128,2048]{1,0:T(8,128)S(1)} %relax_kernel.1.part_ref, f32[128,1024]{1,0:T(8,128)S(1)} %get-tuple-element.25.plane_ref, f32[128,128]{1,0:T(8,128)S(1)} %get-tuple-element.26.open_ref, ...), custom_call_target="tpu_custom_call" | custom-call | flops 4000000000 | bytes 2031616 | tf_op jit(solution)/shard_map/last_kernel_0/pallas_call | solution.py:653
  29.4 0.4 %collective-permute-done.7.refs_1_ = f32[128,512]{1,0:T(8,128)S(1)} collective-permute-done((f32[128,512]{1,0:T(8,128)S(1)}, f32[128,512]{1,0:T(8,128)S(1)}, u32[]{:S(2)}, u32[]{:S(2)}) %collective-permute-start.7) | collective-permute-done | bytes 262176 | tf_op jit(solution)/shard_map/ppermute | solution.py:685
  29.8 1.0 %last_kernel_1.1 = f32[128,2048]{1,0:T(8,128)} custom-call(bf16[256,128]{1,0:T(8,128)(2,1)S(1)} %get-tuple-element.17.side_ref, f32[128,2048]{1,0:T(8,128)S(1)} %relax_kernel.1.part_ref, f32[128,1024]{1,0:T(8,128)S(1)} %get-tuple-element.25.plane_ref, f32[128,128]{1,0:T(8,128)S(1)} %get-tuple-element.26.open_ref, ...), custom_call_target="tpu_custom_call", output_to_operand_aliasing={{}: (4, {})} | custom-call | bytes 3080192 | tf_op jit(solution)/shard_map/last_kernel_1/pallas_call | solution.py:653
  (5 shorter events, 0.0 us)
Async XLA Ops:
  0.7 1.2 %copy-start = (f32[128,2048]{1,0:T(8,128)S(1)}, f32[128,2048]{1,0:T(8,128)}, u32[]{:S(2)}) copy-start(f32[128,2048]{1,0:T(8,128)} %dist_ref.7) | copy-start | bytes 3145732
  1.9 3.8 %copy-start.1 = (f32[128,2048]{1,0:T(8,128)S(1)}, f32[128,2048]{1,0:T(8,128)}, u32[]{:S(2)}) copy-start(f32[128,2048]{1,0:T(8,128)} %dist_ref.7) | copy-start | bytes 3145732
  2.7 20.7 %collective-permute-start.4 = (f32[128,1024]{1,0:T(8,128)S(1)}, f32[128,1024]{1,0:T(8,128)S(1)}, u32[]{:S(2)}, u32[]{:S(2)}) collective-permute-start(f32[128,1024]{1,0:T(8,128)S(1)} %near_plane_kernel.1), channel_id=1, source_target_pairs={{0,16},{16,0},{1,17},{17,1},{2,18},{18,2},{3,19},{19,3},{4,20},{20... | collective-permute-start | bytes 1572872 | tf_op jit(solution)/shard_map/ppermute | solution.py:685
  6.6 1.3 %collective-permute-start = (f32[88,128]{1,0:T(8,128)S(1)}, f32[88,128]{1,0:T(8,128)S(1)}, u32[]{:S(2)}, u32[]{:S(2)}) collective-permute-start(f32[88,128]{1,0:T(8,128)S(1)} %sums_kernel.1), channel_id=1, source_target_pairs={{0,1},{1,0},{2,3},{3,2},{4,5},{5,4},{6,7},{7,6},{8,9},{9,8},{10,11... | collective-permute-start | bytes 135176 | tf_op jit(solution)/shard_map/ppermute | solution.py:675
  7.9 4.1 %collective-permute-start.1 = (f32[88,128]{1,0:T(8,128)S(1)}, f32[88,128]{1,0:T(8,128)S(1)}, u32[]{:S(2)}, u32[]{:S(2)}) collective-permute-start(f32[88,128]{1,0:T(8,128)S(1)} %add.12), channel_id=1, source_target_pairs={{0,2},{1,3},{2,0},{3,1},{4,6},{5,7},{6,4},{7,5},{8,10},{9,11},{10,... | collective-permute-start | bytes 135176 | tf_op jit(solution)/shard_map/ppermute | solution.py:675
  10.4 18.0 %collective-permute-start.6 = (f32[128,512]{1,0:T(8,128)S(1)}, f32[128,512]{1,0:T(8,128)S(1)}, u32[]{:S(2)}, u32[]{:S(2)}) collective-permute-start(f32[128,512]{1,0:T(8,128)S(1)} %get-tuple-element.27), channel_id=1, source_target_pairs={{0,16},{16,0},{1,17},{17,1},{2,18},{18,2},{3,19},{19,3},{4,20},{20... | collective-permute-start | bytes 786440 | tf_op jit(solution)/shard_map/ppermute | solution.py:685
  12.0 4.1 %collective-permute-start.2 = (f32[88,128]{1,0:T(8,128)S(1)}, f32[88,128]{1,0:T(8,128)S(1)}, u32[]{:S(2)}, u32[]{:S(2)}) collective-permute-start(f32[88,128]{1,0:T(8,128)S(1)} %add.13), channel_id=1, source_target_pairs={{0,4},{1,5},{2,6},{3,7},{4,0},{5,1},{6,2},{7,3},{8,12},{9,13},{10,... | collective-permute-start | bytes 135176 | tf_op jit(solution)/shard_map/ppermute | solution.py:675
  16.1 2.7 %copy-start.3 = (s32[6,128]{1,0:T(8,128)S(1)}, s32[6,128]{1,0:T(8,128)}, u32[]{:S(2)}) copy-start(s32[6,128]{1,0:T(8,128)} %mask_ref.7) | copy-start | bytes 9220
  16.1 2.7 %copy-start.4 = (f32[128]{0:T(128)S(1)}, f32[128]{0:T(128)}, u32[]{:S(2)}) copy-start(f32[128]{0:T(128)} %param.6) | copy-start | bytes 1540
  16.1 3.0 %copy-start.2 = (s32[6,128]{1,0:T(8,128)S(1)}, s32[6,128]{1,0:T(8,128)}, u32[]{:S(2)}) copy-start(s32[6,128]{1,0:T(8,128)} %near_ref.7) | copy-start | bytes 9220
  16.1 5.0 %collective-permute-start.3 = (f32[88,128]{1,0:T(8,128)S(1)}, f32[88,128]{1,0:T(8,128)S(1)}, u32[]{:S(2)}, u32[]{:S(2)}) collective-permute-start(f32[88,128]{1,0:T(8,128)S(1)} %add.14), channel_id=1, source_target_pairs={{0,8},{1,9},{2,10},{3,11},{4,12},{5,13},{6,14},{7,15},{8,0},{9,1},... | collective-permute-start | bytes 135176 | tf_op jit(solution)/shard_map/ppermute | solution.py:675
  21.3 4.9 %collective-permute-start.5 = (f32[80,64]{1,0:T(8,128)S(1)}, f32[80,64]{1,0:T(8,128)S(1)}, u32[]{:S(2)}, u32[]{:S(2)}) collective-permute-start(f32[80,64]{1,0:T(8,128)S(1)} %share_kernel.1.after_ref), channel_id=1, source_target_pairs={{0,16},{16,0},{1,17},{17,1},{2,18},{18,2},{3,19},{19,3},{4,20},{20... | collective-permute-start | bytes 61448 | tf_op jit(solution)/shard_map/ppermute | solution.py:685
  21.9 7.9 %collective-permute-start.7 = (f32[128,512]{1,0:T(8,128)S(1)}, f32[128,512]{1,0:T(8,128)S(1)}, u32[]{:S(2)}, u32[]{:S(2)}) collective-permute-start(f32[128,512]{1,0:T(8,128)S(1)} %pass_kernel.1), channel_id=1, source_target_pairs={{0,16},{16,0},{1,17},{17,1},{2,18},{18,2},{3,19},{19,3},{4,20},{20... | collective-permute-start | bytes 786440 | tf_op jit(solution)/shard_map/ppermute | solution.py:685

commit v8 on v7

--- a/solution.py
+++ b/solution.py
@@ -184,16 +184,16 @@
     return low, [(source + HALF, target) for source, target in low]
 
 
-def move_rows(rows_ref, value_ref, send_ref, crossed, part=0, parts=1):
+def move_rows(rows_ref, value_ref, send_ref, part):
     cells, width = value_ref.shape
     count = cells // 2
-    low, high = half_tiles(width, part, parts)
+    low, high = half_tiles(width, part, PARTS)
     begin = low[0][1]
     piece = min(HALF, send_ref.shape[1])
     step = piece // COLUMN_TILE
 
     def move(at, _):
-        for first, tiles, plane in ((0, high, 1 - crossed), (count, low, crossed)):
+        for first, tiles, plane in ((0, high, 0), (count, low, 1)):
             row = rows_ref[0, plane, at]
             for source, target in tiles[::step]:
                 send_ref[pl.ds(first + at, 1), target - begin : target - begin + piece] = (
@@ -213,13 +213,38 @@
     return 1.0 / (WEIGHT * flux * mass * mass), cooling
 
 
-def near_plane_kernel(rows_ref, dist_ref, send_ref):
-    move_rows(rows_ref, dist_ref, send_ref, 0)
+def near_plane_kernel(face_ref, dist_ref, own_ref, send_ref, rows_ref, row_sem, sems):
+    cells, width = dist_ref.shape
+    count = cells // 2
+    rows_copy = pltpu.make_async_copy(face_ref, rows_ref, row_sem)
+    rows_copy.start()
+    copies = []
+    for start in range(0, width, HALF):
+        lanes = slice(start, start + HALF)
+        copy = pltpu.make_async_copy(
+            dist_ref.at[:, lanes], own_ref.at[:, lanes], sems.at[len(copies)]
+        )
+        copy.start()
+        copies.append(copy)
+    rows_copy.wait()
+    for at, copy in enumerate(copies):
+        copy.wait()
+        side = at % 2
+        source, target, first = at * HALF, at // 2 * HALF, (1 - side) * count
+
+        def move(at, _):
+            row = rows_ref[0, side, at]
+            send_ref[pl.ds(first + at, 1), target : target + HALF] = own_ref[
+                pl.ds(row, 1), source : source + HALF
+            ]
+            return 0
+
+        lax.fori_loop(0, count, move, 0, unroll=True)
 
 
 def far_plane_kernel(rows_ref, dist_ref, *send_refs):
     for part, send_ref in enumerate(send_refs):
-        move_rows(rows_ref, dist_ref, send_ref, 1, part, PARTS)
+        move_rows(rows_ref, dist_ref, send_ref, part)
 
 
 def pass_kernel(value_ref, after_ref, out_ref):
@@ -698,8 +723,20 @@
     every = flux_start(FACES)
     columns = pltpu.VMEM((cells, LANES), F32)
 
-    face_rows = jnp.clip(face_rows, 0, cells - 1)
-    (sent,) = call(near_plane_kernel, [plane], [face_rows, dist], scalars=1)
+    dist, sent = call(
+        near_plane_kernel,
+        [whole, plane],
+        [
+            pltpu.with_memory_space_constraint(face_rows, pltpu.HBM),
+            pltpu.with_memory_space_constraint(dist, pltpu.HBM),
+        ],
+        [
+            pltpu.SMEM(face_rows.shape, jnp.int32),
+            pltpu.SemaphoreType.DMA(()),
+            pltpu.SemaphoreType.DMA((width // HALF,)),
+        ],
+        unread=(0, 1),
+    )
     near = exchange(sent)
     (sums,) = call(sums_kernel, [((every, cells), F32)], [dist])
     sums = total(sums)

time: 31 us -> 29.7 us (0.958)
  other arithmetic: 0.71 us -> 0.03 us
  waiting for transfers between devices: 6.29 us -> 5.63 us
  Pallas kernels: 10.8 us -> 11.4 us
  local copies, waits for them, and re-layouts: 1.24 us -> 0.67 us
    min x1 -> x0, other arithmetic: 0.68 us -> none  [on_device(): face_rows = jnp.clip(face_rows, 0, cells - 1)]
    ppermute x4, waiting for transfers between devices: 5.88 us -> 5.23 us  [total(): lax.ppermute(value, 'vel', [(i, i ^ step) for i in range(count)])]
    pallas_call x15, Pallas kernels: 10.8 us -> 11.4 us  [call(): pl.pallas_call(kernel, out_shape=[jax.ShapeDtypeStruct(shape, dtype) for...]
    unnamed x10 -> x8, local copies, waits for them, and re-layouts: 1.24 us -> 0.67 us
  transfers between devices with their start and end apart: 8 -> 8, of which waited for: 5 -> 5; matrix products, arithmetic and copies ran while one was open for 0% -> 0% of each run, Pallas kernels for 29% -> 30%
where the time goes in v8:
time: 29.7 us; the launch traced here: 29.5 us
  starting transfers between devices  11.6 us (39%)
  Pallas kernels  11.4 us (38%)
  waiting for transfers between devices  5.63 us (19%)
  local copies, waits for them, and re-layouts  0.67 us (2%)
    pallas_call x15, Pallas kernels, call(): pl.pallas_call(kernel, out_shape=[jax.ShapeDtypeStruct(shape, dtype) for...  11.4 us
    ppermute x4, starting transfers between devices, total(): lax.ppermute(value, 'vel', [(i, i ^ step) for i in range(count)])  5.92 us
    ppermute x4, starting transfers between devices, exchange(): return [lax.ppermute(send, 'space', forward)]  5.69 us
    ppermute x4, waiting for transfers between devices, total(): lax.ppermute(value, 'vel', [(i, i ^ step) for i in range(count)])  5.23 us
    unnamed x8, local copies, waits for them, and re-layouts  0.67 us
  transfers between devices with their start and end apart: 8, of which 5 were waited for; matrix products, arithmetic and copies ran while one was open for 0% of the time, Pallas kernels for 30%

profile of v8, /device:TPU:0, one launch (start us, length us, event | category | flops | bytes accessed | tf_op | source)
XLA Modules:
  0.0 29.5 jit_solution(13949135274172307522)
XLA Ops:
  0.0 1.4 %near_plane_kernel.1 = (f32[128,2048]{1,0:T(8,128)S(1)}, f32[128,1024]{1,0:T(8,128)S(1)}) custom-call(s32[1,2,64]{2,1,0:T(2,128)} %rows_ref.1, f32[128,2048]{1,0:T(8,128)} %dist_ref.1), custom_call_target="tpu_custom_call" | custom-call | bytes 1049088 | tf_op jit(solution)/shard_map/near_plane_kernel/pallas_call | solution.py:678
  1.4 3.0 %collective-permute-start.4 = (f32[128,1024]{1,0:T(8,128)S(1)}, f32[128,1024]{1,0:T(8,128)S(1)}, u32[]{:S(2)}, u32[]{:S(2)}) collective-permute-start(f32[128,1024]{1,0:T(8,128)S(1)} %get-tuple-element.23), channel_id=1, source_target_pairs={{0,16},{16,0},{1,17},{17,1},{2,18},{18,2},{3,19},{19,3},{4,20},{20... | collective-permute-start | bytes 1572872 | tf_op jit(solution)/shard_map/ppermute | solution.py:710
  4.4 0.8 %sums_kernel.1 = f32[88,128]{1,0:T(8,128)S(1)} custom-call(f32[128,2048]{1,0:T(8,128)S(1)} %get-tuple-element.20.dist_ref.value_ref.own_ref), custom_call_target="tpu_custom_call" | custom-call | bytes 1048576 | tf_op jit(solution)/shard_map/sums_kernel/pallas_call | solution.py:678
  5.2 0.0 copy-start.2
  5.3 0.1 collective-permute-start
  5.3 1.2 %collective-permute-done = f32[88,128]{1,0:T(8,128)S(1)} collective-permute-done((f32[88,128]{1,0:T(8,128)S(1)}, f32[88,128]{1,0:T(8,128)S(1)}, u32[]{:S(2)}, u32[]{:S(2)}) %collective-permute-start) | collective-permute-done | bytes 45088 | tf_op jit(solution)/shard_map/ppermute | solution.py:700
  6.6 1.6 %collective-permute-start.1 = (f32[88,128]{1,0:T(8,128)S(1)}, f32[88,128]{1,0:T(8,128)S(1)}, u32[]{:S(2)}, u32[]{:S(2)}) collective-permute-start(f32[88,128]{1,0:T(8,128)S(1)} %add.12), channel_id=1, source_target_pairs={{0,2},{1,3},{2,0},{3,1},{4,6},{5,7},{6,4},{7,5},{8,10},{9,11},{10,... | collective-permute-start | bytes 135176 | tf_op jit(solution)/shard_map/ppermute | solution.py:700
  8.1 0.0 copy-done.2
  8.1 1.0 %far_plane_kernel.1 = (f32[128,512]{1,0:T(8,128)S(1)}, f32[128,512]{1,0:T(8,128)S(1)}) custom-call(s32[1,2,64]{2,1,0:T(2,128)S(1)} %copy-done.2, f32[128,2048]{1,0:T(8,128)S(1)} %get-tuple-element.20.dist_ref.value_ref.own_ref), custom_call_target="tpu_custom_call" | custom-call | bytes 1049088 | tf_op jit(solution)/shard_map/far_plane_kernel/pallas_call | solution.py:678
  9.1 0.6 %collective-permute-start.6 = (f32[128,512]{1,0:T(8,128)S(1)}, f32[128,512]{1,0:T(8,128)S(1)}, u32[]{:S(2)}, u32[]{:S(2)}) collective-permute-start(f32[128,512]{1,0:T(8,128)S(1)} %get-tuple-element.31), channel_id=1, source_target_pairs={{0,16},{16,0},{1,17},{17,1},{2,18},{18,2},{3,19},{19,3},{4,20},{20... | collective-permute-start | bytes 786440 | tf_op jit(solution)/shard_map/ppermute | solution.py:710
  9.7 1.0 %collective-permute-done.1 = f32[88,128]{1,0:T(8,128)S(1)} collective-permute-done((f32[88,128]{1,0:T(8,128)S(1)}, f32[88,128]{1,0:T(8,128)S(1)}, u32[]{:S(2)}, u32[]{:S(2)}) %collective-permute-start.1) | collective-permute-done | bytes 45088 | tf_op jit(solution)/shard_map/ppermute | solution.py:700
  10.7 0.0 copy-start
  10.7 0.0 copy-start.1
  10.7 1.6 %collective-permute-start.2 = (f32[88,128]{1,0:T(8,128)S(1)}, f32[88,128]{1,0:T(8,128)S(1)}, u32[]{:S(2)}, u32[]{:S(2)}) collective-permute-start(f32[88,128]{1,0:T(8,128)S(1)} %add.13), channel_id=1, source_target_pairs={{0,4},{1,5},{2,6},{3,7},{4,0},{5,1},{6,2},{7,3},{8,12},{9,13},{10,... | collective-permute-start | bytes 135176 | tf_op jit(solution)/shard_map/ppermute | solution.py:700
  12.3 2.5 %collective-permute-done.2 = f32[88,128]{1,0:T(8,128)S(1)} collective-permute-done((f32[88,128]{1,0:T(8,128)S(1)}, f32[88,128]{1,0:T(8,128)S(1)}, u32[]{:S(2)}, u32[]{:S(2)}) %collective-permute-start.2) | collective-permute-done | bytes 45088 | tf_op jit(solution)/shard_map/ppermute | solution.py:700
  14.8 2.6 %collective-permute-start.3 = (f32[88,128]{1,0:T(8,128)S(1)}, f32[88,128]{1,0:T(8,128)S(1)}, u32[]{:S(2)}, u32[]{:S(2)}) collective-permute-start(f32[88,128]{1,0:T(8,128)S(1)} %add.14), channel_id=1, source_target_pairs={{0,8},{1,9},{2,10},{3,11},{4,12},{5,13},{6,14},{7,15},{8,0},{9,1},... | collective-permute-start | bytes 135176 | tf_op jit(solution)/shard_map/ppermute | solution.py:700
  17.5 0.0 copy-done
  17.5 0.0 copy-done.1
  17.5 0.8 %stream_kernel.1.stream_ref._ = f32[128,2048]{1,0:T(8,128)S(1)} custom-call(s32[6,128]{1,0:T(8,128)S(1)} %copy-done, s32[6,128]{1,0:T(8,128)S(1)} %copy-done.1, f32[128,2048]{1,0:T(8,128)S(1)} %get-tuple-element.20.dist_ref.value_ref.own_ref), custom_call_target="tpu_custom_call" | custom-call | bytes 1054720 | tf_op jit(solution)/shard_map/stream_kernel/pallas_call | solution.py:678
  18.3 0.0 copy-start.3
  18.3 0.6 %copy-done.3 = f32[128]{0:T(128)S(1)} copy-done((f32[128]{0:T(128)S(1)}, f32[128]{0:T(128)}, u32[]{:S(2)}) %copy-start.3) | copy-done | bytes 536
  19.0 0.3 %wall_kernel.1 = (f32[128,2048]{1,0:T(8,128)S(1)}, f32[8,128]{1,0:T(8,128)S(1)}, bf16[256,128]{1,0:T(8,128)(2,1)S(1)}, f32[8,128]{1,0:T(8,128)S(1)}) custom-call(s32[1,2,64]{2,1,0:T(2,128)S(1)} %copy-done.2, f32[1,128]{1,0:T(1,128)S(1)} %bitcast.1, s32[6,128]{1,0:T(8,128)S(1)} %copy-done.1), custom_call_target="tpu_custom_call" | custom-call | bytes 4096 | tf_op jit(solution)/shard_map/wall_kernel/pallas_call | solution.py:678
  19.3 0.5 %collective-permute-done.3 = f32[88,128]{1,0:T(8,128)S(1)} collective-permute-done((f32[88,128]{1,0:T(8,128)S(1)}, f32[88,128]{1,0:T(8,128)S(1)}, u32[]{:S(2)}, u32[]{:S(2)}) %collective-permute-start.3) | collective-permute-done | bytes 45088 | tf_op jit(solution)/shard_map/ppermute | solution.py:700
  19.8 0.2 share_kernel.1.after_ref
  20.0 0.6 %collective-permute-start.5 = (f32[80,64]{1,0:T(8,128)S(1)}, f32[80,64]{1,0:T(8,128)S(1)}, u32[]{:S(2)}, u32[]{:S(2)}) collective-permute-start(f32[80,64]{1,0:T(8,128)S(1)} %share_kernel.1.after_ref), channel_id=1, source_target_pairs={{0,16},{16,0},{1,17},{17,1},{2,18},{18,2},{3,19},{19,3},{4,20},{20... | collective-permute-start | bytes 61448 | tf_op jit(solution)/shard_map/ppermute | solution.py:710
  20.6 1.5 %collective-permute-start.7 = (f32[128,512]{1,0:T(8,128)S(1)}, f32[128,512]{1,0:T(8,128)S(1)}, u32[]{:S(2)}, u32[]{:S(2)}) collective-permute-start(f32[128,512]{1,0:T(8,128)S(1)} %pass_kernel.1), channel_id=1, source_target_pairs={{0,16},{16,0},{1,17},{17,1},{2,18},{18,2},{3,19},{19,3},{4,20},{20... | collective-permute-start | bytes 786440 | tf_op jit(solution)/shard_map/ppermute | solution.py:710
  22.1 0.0 collective-permute-done.4.refs_0_
  22.1 1.0 %middle_kernel.1.middle_ref = f32[128,2048]{1,0:T(8,128)S(1)} custom-call(f32[88,128]{1,0:T(8,128)S(1)} %add.15.sums_ref, f32[8,128]{1,0:T(8,128)S(1)} %get-tuple-element.21.back_ref, bf16[256,128]{1,0:T(8,128)(2,1)S(1)} %get-tuple-element.19.side_ref, f32[128,2048]{1,0:T(8,128)S(1)} %get-tuple-element.20.dist_ref.value_ref.own_ref, ...), custom_call_target="tpu_custom_call" | custom-call | bytes 3850240 | tf_op jit(solution)/shard_map/middle_kernel/pallas_call | solution.py:678
  23.1 0.9 %stream_last_kernel.1._.part_ref = f32[128,2048]{1,0:T(8,128)S(1)} custom-call(s32[6,128]{1,0:T(8,128)S(1)} %copy-done, s32[6,128]{1,0:T(8,128)S(1)} %copy-done.1, f32[128,2048]{1,0:T(8,128)S(1)} %get-tuple-element.20.dist_ref.value_ref.own_ref, f32[128,2048]{1,0:T(8,128)S(1)} %middle_kernel.1.middle_ref), custom_call_target="tpu_custom_call" | custom-call | bytes 2103296 | tf_op jit(solution)/shard_map/stream_last_kernel/pallas_call | solution.py:678
  24.0 0.8 %halo_stream_kernel.1 = (f32[128,1024]{1,0:T(8,128)S(1)}, f32[128,1024]{1,0:T(8,128)S(1)}, f32[128,1024]{1,0:T(8,128)S(1)}, f32[128,1024]{1,0:T(8,128)S(1)}) custom-call(s32[1,2,64]{2,1,0:T(2,128)S(1)} %copy-done.2, s32[6,128]{1,0:T(8,128)S(1)} %copy-done, f32[128,1024]{1,0:T(8,128)S(1)} %collective-permute-done.4.refs_0_), custom_call_target="tpu_custom_call" | custom-call | bytes 527872 | tf_op jit(solution)/shard_map/halo_stream_kernel/pallas_call | solution.py:678
  24.8 0.0 collective-permute-done.5.refs_0_
  24.8 0.4 %advance_kernel.1.sums_ref = f32[16,128]{1,0:T(8,128)S(1)} custom-call(s32[1,2,64]{2,1,0:T(2,128)S(1)} %copy-done.2, s32[6,128]{1,0:T(8,128)S(1)} %copy-done, f32[128,2048]{1,0:T(8,128)S(1)} %stream_last_kernel.1._.part_ref, f32[128,1024]{1,0:T(8,128)S(1)} %get-tuple-element.24.__.base_ref, s32[6,128]{1,0:T(8,128)S(1)} %copy-done.1, ...), custom_call_target="tpu_custom_call" | custom-call | flops 1400000000 | bytes 1649152 | tf_op jit(solution)/shard_map/advance_kernel/pallas_call | solution.py:678
  25.3 0.9 %relax_kernel.1.part_ref = f32[128,2048]{1,0:T(8,128)S(1)} custom-call(f32[16,128]{1,0:T(8,128)S(1)} %advance_kernel.1.sums_ref, f32[8,128]{1,0:T(8,128)S(1)} %get-tuple-element.21.back_ref, f32[128,2048]{1,0:T(8,128)S(1)} %middle_kernel.1.middle_ref, f32[128,2048]{1,0:T(8,128)S(1)} %stream_last_kernel.1._.part_ref, f32[128,2048]{1,0:T(8,128)S(1)} %get-tuple-element.22.shape_ref), custom_call_target="tpu_custom_call" | custom-call | bytes 3158016 | tf_op jit(solution)/shard_map/relax_kernel/pallas_call | solution.py:678
  26.2 0.9 %halo_relax_kernel.1 = (f32[128,1024]{1,0:T(8,128)S(1)}, f32[128,128]{1,0:T(8,128)S(1)}) custom-call(f32[128,1024]{1,0:T(8,128)S(1)} %get-tuple-element.24.__.base_ref, f32[128,1024]{1,0:T(8,128)S(1)} %get-tuple-element.26.from_y_ref, f32[128,1024]{1,0:T(8,128)S(1)} %get-tuple-element.27.from_z_ref, f32[128,1024]{1,0:T(8,128)S(1)} %get-tuple-element.28.values_ref, ...), custom_call_target="tpu_custom_call" | custom-call | bytes 2117632 | tf_op jit(solution)/shard_map/halo_relax_kernel/pallas_call | solution.py:678
  27.0 0.0 collective-permute-done.6.refs_0_
  27.0 1.0 %last_kernel_0.1.refs_0_ = f32[128,2048]{1,0:T(8,128)} custom-call(bf16[256,128]{1,0:T(8,128)(2,1)S(1)} %get-tuple-element.19.side_ref, f32[128,2048]{1,0:T(8,128)S(1)} %relax_kernel.1.part_ref, f32[128,1024]{1,0:T(8,128)S(1)} %get-tuple-element.29.plane_ref, f32[128,128]{1,0:T(8,128)S(1)} %get-tuple-element.30.open_ref, ...), custom_call_target="tpu_custom_call" | custom-call | flops 4000000000 | bytes 2031616 | tf_op jit(solution)/shard_map/last_kernel_0/pallas_call | solution.py:678
  28.1 0.4 %collective-permute-done.7.refs_1_ = f32[128,512]{1,0:T(8,128)S(1)} collective-permute-done((f32[128,512]{1,0:T(8,128)S(1)}, f32[128,512]{1,0:T(8,128)S(1)}, u32[]{:S(2)}, u32[]{:S(2)}) %collective-permute-start.7) | collective-permute-done | bytes 262176 | tf_op jit(solution)/shard_map/ppermute | solution.py:710
  28.5 1.0 %last_kernel_1.1 = f32[128,2048]{1,0:T(8,128)} custom-call(bf16[256,128]{1,0:T(8,128)(2,1)S(1)} %get-tuple-element.19.side_ref, f32[128,2048]{1,0:T(8,128)S(1)} %relax_kernel.1.part_ref, f32[128,1024]{1,0:T(8,128)S(1)} %get-tuple-element.29.plane_ref, f32[128,128]{1,0:T(8,128)S(1)} %get-tuple-element.30.open_ref, ...), custom_call_target="tpu_custom_call", output_to_operand_aliasing={{}: (4, {})} | custom-call | bytes 3080192 | tf_op jit(solution)/shard_map/last_kernel_1/pallas_call | solution.py:678
  (5 shorter events, 0.0 us)
Async XLA Ops:
  1.4 20.7 %collective-permute-start.4 = (f32[128,1024]{1,0:T(8,128)S(1)}, f32[128,1024]{1,0:T(8,128)S(1)}, u32[]{:S(2)}, u32[]{:S(2)}) collective-permute-start(f32[128,1024]{1,0:T(8,128)S(1)} %get-tuple-element.23), channel_id=1, source_target_pairs={{0,16},{16,0},{1,17},{17,1},{2,18},{18,2},{3,19},{19,3},{4,20},{20... | collective-permute-start | bytes 1572872 | tf_op jit(solution)/shard_map/ppermute | solution.py:710
  5.2 2.9 %copy-start.2 = (s32[1,2,64]{2,1,0:T(2,128)S(1)}, s32[1,2,64]{2,1,0:T(2,128)}, u32[]{:S(2)}) copy-start(s32[1,2,64]{2,1,0:T(2,128)} %rows_ref.1) | copy-start | bytes 1540
  5.3 1.3 %collective-permute-start = (f32[88,128]{1,0:T(8,128)S(1)}, f32[88,128]{1,0:T(8,128)S(1)}, u32[]{:S(2)}, u32[]{:S(2)}) collective-permute-start(f32[88,128]{1,0:T(8,128)S(1)} %sums_kernel.1), channel_id=1, source_target_pairs={{0,1},{1,0},{2,3},{3,2},{4,5},{5,4},{6,7},{7,6},{8,9},{9,8},{10,11... | collective-permute-start | bytes 135176 | tf_op jit(solution)/shard_map/ppermute | solution.py:700
  6.6 4.1 %collective-permute-start.1 = (f32[88,128]{1,0:T(8,128)S(1)}, f32[88,128]{1,0:T(8,128)S(1)}, u32[]{:S(2)}, u32[]{:S(2)}) collective-permute-start(f32[88,128]{1,0:T(8,128)S(1)} %add.12), channel_id=1, source_target_pairs={{0,2},{1,3},{2,0},{3,1},{4,6},{5,7},{6,4},{7,5},{8,10},{9,11},{10,... | collective-permute-start | bytes 135176 | tf_op jit(solution)/shard_map/ppermute | solution.py:700
  9.1 18.0 %collective-permute-start.6 = (f32[128,512]{1,0:T(8,128)S(1)}, f32[128,512]{1,0:T(8,128)S(1)}, u32[]{:S(2)}, u32[]{:S(2)}) collective-permute-start(f32[128,512]{1,0:T(8,128)S(1)} %get-tuple-element.31), channel_id=1, source_target_pairs={{0,16},{16,0},{1,17},{17,1},{2,18},{18,2},{3,19},{19,3},{4,20},{20... | collective-permute-start | bytes 786440 | tf_op jit(solution)/shard_map/ppermute | solution.py:710
  10.7 6.8 %copy-start = (s32[6,128]{1,0:T(8,128)S(1)}, s32[6,128]{1,0:T(8,128)}, u32[]{:S(2)}) copy-start(s32[6,128]{1,0:T(8,128)} %near_ref.7) | copy-start | bytes 9220
  10.7 6.8 %copy-start.1 = (s32[6,128]{1,0:T(8,128)S(1)}, s32[6,128]{1,0:T(8,128)}, u32[]{:S(2)}) copy-start(s32[6,128]{1,0:T(8,128)} %mask_ref.7) | copy-start | bytes 9220
  10.7 4.1 %collective-permute-start.2 = (f32[88,128]{1,0:T(8,128)S(1)}, f32[88,128]{1,0:T(8,128)S(1)}, u32[]{:S(2)}, u32[]{:S(2)}) collective-permute-start(f32[88,128]{1,0:T(8,128)S(1)} %add.13), channel_id=1, source_target_pairs={{0,4},{1,5},{2,6},{3,7},{4,0},{5,1},{6,2},{7,3},{8,12},{9,13},{10,... | collective-permute-start | bytes 135176 | tf_op jit(solution)/shard_map/ppermute | solution.py:700
  14.8 5.0 %collective-permute-start.3 = (f32[88,128]{1,0:T(8,128)S(1)}, f32[88,128]{1,0:T(8,128)S(1)}, u32[]{:S(2)}, u32[]{:S(2)}) collective-permute-start(f32[88,128]{1,0:T(8,128)S(1)} %add.14), channel_id=1, source_target_pairs={{0,8},{1,9},{2,10},{3,11},{4,12},{5,13},{6,14},{7,15},{8,0},{9,1},... | collective-permute-start | bytes 135176 | tf_op jit(solution)/shard_map/ppermute | solution.py:700
  18.3 0.7 %copy-start.3 = (f32[128]{0:T(128)S(1)}, f32[128]{0:T(128)}, u32[]{:S(2)}) copy-start(f32[128]{0:T(128)} %param.6) | copy-start | bytes 1540
  20.0 4.9 %collective-permute-start.5 = (f32[80,64]{1,0:T(8,128)S(1)}, f32[80,64]{1,0:T(8,128)S(1)}, u32[]{:S(2)}, u32[]{:S(2)}) collective-permute-start(f32[80,64]{1,0:T(8,128)S(1)} %share_kernel.1.after_ref), channel_id=1, source_target_pairs={{0,16},{16,0},{1,17},{17,1},{2,18},{18,2},{3,19},{19,3},{4,20},{20... | collective-permute-start | bytes 61448 | tf_op jit(solution)/shard_map/ppermute | solution.py:710
  20.6 7.9 %collective-permute-start.7 = (f32[128,512]{1,0:T(8,128)S(1)}, f32[128,512]{1,0:T(8,128)S(1)}, u32[]{:S(2)}, u32[]{:S(2)}) collective-permute-start(f32[128,512]{1,0:T(8,128)S(1)} %pass_kernel.1), channel_id=1, source_target_pairs={{0,16},{16,0},{1,17},{17,1},{2,18},{18,2},{3,19},{19,3},{4,20},{20... | collective-permute-start | bytes 786440 | tf_op jit(solution)/shard_map/ppermute | solution.py:710

commit v9 on v8

--- a/solution.py
+++ b/solution.py
@@ -24,7 +24,6 @@
 SUMS = 16
 FACES = 6
 NOTES = 8
-PARTS = 2
 BEND = 2.5 * math.log2(math.e)
 LOG2E = math.log2(math.e)
 F32 = jnp.float32
@@ -155,7 +154,7 @@
     sums_ref[...] = total
 
 
-def share_kernel(face_ref, sums_ref, notes_ref, _, send_ref):
+def share_kernel(face_ref, sums_ref, notes_ref, send_ref):
     low, high = face_hits(face_ref, sums_ref.shape[1])
     for side, hits in ((0, high), (1, low)):
         rows = [sums_ref[:SUMS], notes_ref[...], sums_ref[flux_start(side) : flux_start(side + 1)]]
@@ -177,28 +176,38 @@
     return jnp.concatenate([halo_rows(refs, 0, rows), halo_rows(refs, 1, rows)], axis=1)
 
 
-def half_tiles(width, part=0, parts=1):
-    half = width // 2
-    lanes = range(part * half // parts, (part + 1) * half // parts, COLUMN_TILE)
-    low = [(lane // HALF * PLANE + lane % HALF, lane) for lane in lanes]
-    return low, [(source + HALF, target) for source, target in low]
-
-
-def move_rows(rows_ref, value_ref, send_ref, part):
+def half_tiles(start, stop, most):
+    low, high = [], []
+    while start < stop:
+        size = min(start // most * most + most, stop) - start
+        source = start // HALF * PLANE + start % HALF
+        low.append((source, start, size))
+        high.append((source + HALF, start, size))
+        start += size
+    return low, high
+
+
+def far_parts(half):
+    tiles = half // LANES
+    cut = (5 * tiles + 7) // 8 * LANES
+    return [(0, cut), (cut, half)]
+
+
+def move_rows(rows_ref, value_ref, send_ref, start, stop):
     cells, width = value_ref.shape
     count = cells // 2
-    low, high = half_tiles(width, part, PARTS)
-    begin = low[0][1]
-    piece = min(HALF, send_ref.shape[1])
-    step = piece // COLUMN_TILE
+    low, high = half_tiles(start, stop, HALF)
 
     def move(at, _):
         for first, tiles, plane in ((0, high, 0), (count, low, 1)):
             row = rows_ref[0, plane, at]
-            for source, target in tiles[::step]:
-                send_ref[pl.ds(first + at, 1), target - begin : target - begin + piece] = (
-                    value_ref[pl.ds(row, 1), source : source + piece]
-                )
+            for source, target, size in tiles:
+                wide = max(size, 2 * LANES)
+                begin = min(source, width - wide)
+                values = value_ref[pl.ds(row, 1), begin : begin + wide]
+                send_ref[pl.ds(first + at, 1), target - start : target - start + size] = values[
+                    :, source - begin : source - begin + size
+                ]
         return 0
 
     lax.fori_loop(0, count, move, 0, unroll=True)
@@ -243,8 +252,8 @@
 
 
 def far_plane_kernel(rows_ref, dist_ref, *send_refs):
-    for part, send_ref in enumerate(send_refs):
-        move_rows(rows_ref, dist_ref, send_ref, part)
+    for (start, stop), send_ref in zip(far_parts(dist_ref.shape[1] // 2), send_refs):
+        move_rows(rows_ref, dist_ref, send_ref, start, stop)
 
 
 def pass_kernel(value_ref, after_ref, out_ref):
@@ -453,9 +462,9 @@
     halo_refs, (out_ref, columns_ref, base_ref) = refs[:-3], refs[-3:]
     cells, width = own_ref.shape
     columns_ref[...] = columns_of(sums_ref[:SUMS], back_ref[...], width, TIME_STEP, 1.0)
-    for side, tiles in enumerate(half_tiles(width)):
+    for side, tiles in enumerate(half_tiles(0, width // 2, COLUMN_TILE)):
         pick = side_ref[side * cells : (side + 1) * cells, :]
-        for source, target in tiles:
+        for source, target, _ in tiles:
             lanes = slice(source, source + COLUMN_TILE)
             vel_x, _ = lane_points(source, COLUMN_TILE)
             rows = halo_rows(halo_refs, 1 - side)[:, target : target + COLUMN_TILE]
@@ -502,7 +511,7 @@
     return result
 
 
-def advance_kernel(face_ref, near_ref, _, __, mask_ref, sums_ref, back_ref, *refs):
+def advance_kernel(face_ref, near_ref, mask_ref, sums_ref, back_ref, *refs):
     shared_refs, out_ref = refs[:-1], refs[-1]
     cells = near_ref.shape[1]
     cell_start = lax.axis_index("space") * cells
@@ -638,29 +647,58 @@
     relax(columns_ref, base_ref, values_ref, None, out_ref, (from_y_ref, from_z_ref))
 
 
-def last_kernel(part, side_ref, part_ref, plane_ref, open_ref, *refs):
+def second_kernel(
+    face_ref, near_ref, mask_ref, sums_ref, back_ref, side_ref, dist_ref, stream_ref, shape_ref, *refs
+):
+    halo_refs, refs = refs[:-8], refs[-8:]
+    middle_ref, part_ref, *plane_refs, columns_ref, base_ref = refs
+    middle_kernel(
+        sums_ref,
+        back_ref,
+        side_ref,
+        dist_ref,
+        stream_ref,
+        shape_ref,
+        *halo_refs,
+        middle_ref,
+        columns_ref,
+        base_ref,
+    )
+    stream_last_kernel(near_ref, mask_ref, dist_ref, middle_ref, part_ref)
+    halo_stream_kernel(face_ref, near_ref, *halo_refs, *plane_refs)
+
+
+def third_kernel(face_ref, near_ref, mask_ref, sums_ref, back_ref, shape_ref, *refs):
+    middle_ref, part_ref, *plane_refs = refs[:6]
+    shared_refs, (out_ref, plane_ref, open_ref, next_ref, columns_ref) = refs[6:-5], refs[-5:]
+    advance_kernel(face_ref, near_ref, mask_ref, sums_ref, back_ref, *shared_refs, next_ref)
+    relax_kernel(next_ref, back_ref, middle_ref, part_ref, shape_ref, out_ref, columns_ref)
+    halo_relax_kernel(*plane_refs, *shared_refs, plane_ref, open_ref, columns_ref)
+
+
+def last_kernel(side_ref, part_ref, plane_ref, open_ref, *refs):
     refs, (out_ref, result_ref, sems) = refs[:-3], refs[-3:]
-    halo_refs = refs[part > 0 :]
     cells, width = part_ref.shape
     count = cells // 2
     copies = []
-    for side, tiles in enumerate(half_tiles(width, part, PARTS)):
-        pick = side_ref[side * cells : (side + 1) * cells, :]
-        block = slice((1 - side) * count, (2 - side) * count)
-        gate = jnp.concatenate([open_ref[block]] * (COLUMN_TILE // LANES), axis=1)
-        begin = tiles[0][1]
-        for source, target in tiles:
-            lanes = slice(source, source + COLUMN_TILE)
-            speed_x = jnp.abs(lane_points(source, COLUMN_TILE)[0])
-            rows = halo_rows(halo_refs, 1 - side)[:, target - begin : target - begin + COLUMN_TILE]
-            rows = plane_ref[block, target : target + COLUMN_TILE] + gate * speed_x * rows
-            halo = dot(pick, jnp.concatenate(split(rows, 2), axis=0))
-            result_ref[:, lanes] = part_ref[:, lanes] + (0.5 * TIME_STEP * speed_x) * halo
-            copy = pltpu.make_async_copy(
-                result_ref.at[:, lanes], out_ref.at[:, lanes], sems.at[len(copies)]
-            )
-            copy.start()
-            copies.append(copy)
+    for part, (start, stop) in enumerate(far_parts(width // 2)):
+        halo_refs = refs[part * len(refs) // 2 : (part + 1) * len(refs) // 2]
+        for side, tiles in enumerate(half_tiles(start, stop, COLUMN_TILE)):
+            pick = side_ref[side * cells : (side + 1) * cells, :]
+            block = slice((1 - side) * count, (2 - side) * count)
+            for source, target, size in tiles:
+                lanes = slice(source, source + size)
+                gate = jnp.concatenate([open_ref[block]] * (size // LANES), axis=1)
+                speed_x = jnp.abs(lane_points(source, size)[0])
+                rows = halo_rows(halo_refs, 1 - side)[:, target - start : target - start + size]
+                rows = plane_ref[block, target : target + size] + gate * speed_x * rows
+                halo = dot(pick, jnp.concatenate(split(rows, 2), axis=0))
+                result_ref[:, lanes] = part_ref[:, lanes] + (0.5 * TIME_STEP * speed_x) * halo
+                copy = pltpu.make_async_copy(
+                    result_ref.at[:, lanes], out_ref.at[:, lanes], sems.at[len(copies)]
+                )
+                copy.start()
+                copies.append(copy)
     for copy in copies:
         copy.wait()
 
@@ -670,10 +708,7 @@
         pltpu.SMEM if at < scalars else pl.ANY if at in unread else pltpu.VMEM
         for at in range(len(arrays))
     ]
-    if isinstance(kernel, functools.partial):
-        name = f"{kernel.func.__name__}_{kernel.args[0]}"
-    else:
-        name = kernel.__name__
+    name = kernel.__name__
     size = sum(math.prod(array.shape) * 4 for array in arrays)
     return pl.pallas_call(
         kernel,
@@ -690,7 +725,18 @@
     )(*arrays)
 
 
-COST = {"advance_kernel": 14 * 10**8, "last_kernel_0": 4 * 10**9}
+COST = {"third_kernel": 2 * 10**9, "second_kernel": 10**9}
+
+
+def passed(value, after):
+    return call(
+        pass_kernel,
+        [(value.shape, value.dtype)],
+        [value, after],
+        far_outs=True,
+        unread=(0, 1),
+        aliases={0: 0},
+    )[0]
 
 
 def total(value):
@@ -739,68 +785,42 @@
     )
     near = exchange(sent)
     (sums,) = call(sums_kernel, [((every, cells), F32)], [dist])
-    sums = total(sums)
     shape, back, side, notes = call(
         wall_kernel,
         [whole, ((8, cells), F32), ((2 * cells, cells), BF16), ((NOTES, cells), F32)],
         [face_rows, temp, wall_mask],
     )
     (stream,) = call(stream_kernel, [whole], [neighbours, wall_mask, dist])
+    sums = total(sums)
     (sent,) = call(
         share_kernel,
         [((2 * (2 * SUMS + NOTES), count), F32)],
-        [face_rows, sums, notes, stream],
-        unread=(3,),
+        [face_rows, sums, notes],
     )
     shared = exchange(sent)
-    part_shape = ((cells, half // PARTS), F32)
-    far_rows = call(far_plane_kernel, [part_shape] * PARTS, [face_rows, dist], scalars=1)
-    far = []
-    for part in range(PARTS):
-        rows = far_rows[part]
-        if part:
-            (rows,) = call(
-                pass_kernel,
-                [part_shape],
-                [rows, sent],
-                far_outs=True,
-                unread=(0, 1),
-                aliases={0: 0},
-            )
-        far.append(exchange(rows))
-    (middle,) = call(
-        middle_kernel,
-        [whole],
-        [sums, back, side, dist, stream, shape, *near],
+    far_shapes = [((cells, stop - start), F32) for start, stop in far_parts(half)]
+    far_rows = call(far_plane_kernel, far_shapes, [face_rows, dist], scalars=1)
+    far = [exchange(far_rows[0]), exchange(passed(far_rows[1], sent))]
+    middle, part, *planes = call(
+        second_kernel,
+        [whole, whole, plane, plane, plane, plane],
+        [face_rows, neighbours, wall_mask, sums, back, side, dist, stream, shape, *near],
         [columns, pltpu.VMEM((cells, width), F32)],
     )
-    (part_sum,) = call(stream_last_kernel, [whole], [neighbours, wall_mask, dist, middle])
-    halo_parts = call(halo_stream_kernel, [plane] * 4, [face_rows, neighbours, *near])
-    (sums_two,) = call(
-        advance_kernel,
-        [((SUMS, cells), F32)],
-        [face_rows, neighbours, part_sum, halo_parts[0], wall_mask, sums, back, *shared],
-        unread=(2, 3),
+    part, plane_one, gate = call(
+        third_kernel,
+        [whole, plane, ((cells, LANES), F32)],
+        [face_rows, neighbours, wall_mask, sums, back, shape, middle, part, *planes, *shared],
+        [pltpu.VMEM((SUMS, cells), F32), columns],
     )
-    (part_sum,) = call(relax_kernel, [whole], [sums_two, back, middle, part_sum, shape], [columns])
-    plane_one, gate = call(
-        halo_relax_kernel, [plane, ((cells, LANES), F32)], [*halo_parts, *shared], [columns]
+    (result,) = call(
+        last_kernel,
+        [whole],
+        [side, part, plane_one, gate, *far[0], *far[1]],
+        [pltpu.VMEM((cells, width), F32), pltpu.SemaphoreType.DMA((width // LANES,))],
+        far_outs=True,
     )
-    result = []
-    for part in range(PARTS):
-        result = call(
-            functools.partial(last_kernel, part),
-            [whole],
-            [side, part_sum, plane_one, gate, *result, *far[part]],
-            [
-                pltpu.VMEM((cells, width), F32),
-                pltpu.SemaphoreType.DMA((width // COLUMN_TILE // PARTS,)),
-            ],
-            far_outs=True,
-            unread=(4,) if part else (),
-            aliases={4: 0} if part else None,
-        )
-    return result[0]
+    return result
 
 
 def solution(mesh):

time: 29.7 us -> 29.9 us (level)
  waiting for transfers between devices: 5.63 us -> 6.56 us
  Pallas kernels: 11.4 us -> 10.8 us
    ppermute x4, waiting for transfers between devices: 0.4 us -> 1.41 us  [exchange(): return [lax.ppermute(send, 'space', forward)]]
    pallas_call x15 -> x10, Pallas kernels: 11.4 us -> 10.8 us  [call(): pl.pallas_call(kernel, out_shape=[jax.ShapeDtypeStruct(shape, dtype) for...]
  transfers between devices with their start and end apart: 8 -> 8, of which waited for: 5 -> 6; matrix products, arithmetic and copies ran while one was open for 0% -> 0% of each run, Pallas kernels for 30% -> 27%
where the time goes in v9:
time: 29.9 us; the launch traced here: 29.8 us
  starting transfers between devices  11.6 us (39%)
  Pallas kernels  10.8 us (36%)
  waiting for transfers between devices  6.56 us (22%)
  local copies, waits for them, and re-layouts  0.67 us (2%)
    pallas_call x10, Pallas kernels, call(): pl.pallas_call(kernel, out_shape=[jax.ShapeDtypeStruct(shape, dtype) for...  10.8 us
    ppermute x4, starting transfers between devices, total(): lax.ppermute(value, 'vel', [(i, i ^ step) for i in range(count)])  5.91 us
    ppermute x4, starting transfers between devices, exchange(): return [lax.ppermute(send, 'space', forward)]  5.69 us
    ppermute x4, waiting for transfers between devices, total(): lax.ppermute(value, 'vel', [(i, i ^ step) for i in range(count)])  5.15 us
    ppermute x4, waiting for transfers between devices, exchange(): return [lax.ppermute(send, 'space', forward)]  1.41 us
    unnamed x8, local copies, waits for them, and re-layouts  0.67 us
  transfers between devices with their start and end apart: 8, of which 6 were waited for; matrix products, arithmetic and copies ran while one was open for 0% of the time, Pallas kernels for 27%

profile of v9, /device:TPU:0, one launch (start us, length us, event | category | flops | bytes accessed | tf_op | source)
XLA Modules:
  0.0 29.8 jit_solution(17934123672329391570)
XLA Ops:
  0.0 1.4 %near_plane_kernel.1 = (f32[128,2048]{1,0:T(8,128)S(1)}, f32[128,1024]{1,0:T(8,128)S(1)}) custom-call(s32[1,2,64]{2,1,0:T(2,128)} %rows_ref.1, f32[128,2048]{1,0:T(8,128)} %dist_ref.1), custom_call_target="tpu_custom_call" | custom-call | bytes 1049088 | tf_op jit(solution)/shard_map/near_plane_kernel/pallas_call | solution.py:713
  1.4 3.0 %collective-permute-start.4 = (f32[128,1024]{1,0:T(8,128)S(1)}, f32[128,1024]{1,0:T(8,128)S(1)}, u32[]{:S(2)}, u32[]{:S(2)}) collective-permute-start(f32[128,1024]{1,0:T(8,128)S(1)} %get-tuple-element.26), channel_id=1, source_target_pairs={{0,16},{16,0},{1,17},{17,1},{2,18},{18,2},{3,19},{19,3},{4,20},{20... | collective-permute-start | bytes 1572872 | tf_op jit(solution)/shard_map/ppermute | solution.py:756
  4.4 0.8 %sums_kernel.1 = f32[88,128]{1,0:T(8,128)S(1)} custom-call(f32[128,2048]{1,0:T(8,128)S(1)} %get-tuple-element.23.dist_ref.value_ref), custom_call_target="tpu_custom_call" | custom-call | bytes 1048576 | tf_op jit(solution)/shard_map/sums_kernel/pallas_call | solution.py:713
  5.3 0.1 collective-permute-start
  5.3 1.2 %collective-permute-done = f32[88,128]{1,0:T(8,128)S(1)} collective-permute-done((f32[88,128]{1,0:T(8,128)S(1)}, f32[88,128]{1,0:T(8,128)S(1)}, u32[]{:S(2)}, u32[]{:S(2)}) %collective-permute-start) | collective-permute-done | bytes 45088 | tf_op jit(solution)/shard_map/ppermute | solution.py:746
  6.6 0.0 copy-start.1
  6.6 1.6 %collective-permute-start.1 = (f32[88,128]{1,0:T(8,128)S(1)}, f32[88,128]{1,0:T(8,128)S(1)}, u32[]{:S(2)}, u32[]{:S(2)}) collective-permute-start(f32[88,128]{1,0:T(8,128)S(1)} %add.12), channel_id=1, source_target_pairs={{0,2},{1,3},{2,0},{3,1},{4,6},{5,7},{6,4},{7,5},{8,10},{9,11},{10,... | collective-permute-start | bytes 135176 | tf_op jit(solution)/shard_map/ppermute | solution.py:746
  8.1 2.6 %collective-permute-done.1 = f32[88,128]{1,0:T(8,128)S(1)} collective-permute-done((f32[88,128]{1,0:T(8,128)S(1)}, f32[88,128]{1,0:T(8,128)S(1)}, u32[]{:S(2)}, u32[]{:S(2)}) %collective-permute-start.1) | collective-permute-done | bytes 45088 | tf_op jit(solution)/shard_map/ppermute | solution.py:746
  10.7 1.6 %collective-permute-start.2 = (f32[88,128]{1,0:T(8,128)S(1)}, f32[88,128]{1,0:T(8,128)S(1)}, u32[]{:S(2)}, u32[]{:S(2)}) collective-permute-start(f32[88,128]{1,0:T(8,128)S(1)} %add.13), channel_id=1, source_target_pairs={{0,4},{1,5},{2,6},{3,7},{4,0},{5,1},{6,2},{7,3},{8,12},{9,13},{10,... | collective-permute-start | bytes 135176 | tf_op jit(solution)/shard_map/ppermute | solution.py:746
  12.3 0.0 copy-done.1
  12.3 1.0 %far_plane_kernel.1 = (f32[128,640]{1,0:T(8,128)S(1)}, f32[128,384]{1,0:T(8,128)S(1)}) custom-call(s32[1,2,64]{2,1,0:T(2,128)S(1)} %copy-done.1, f32[128,2048]{1,0:T(8,128)S(1)} %get-tuple-element.23.dist_ref.value_ref), custom_call_target="tpu_custom_call" | custom-call | bytes 1049088 | tf_op jit(solution)/shard_map/far_plane_kernel/pallas_call | solution.py:713
  13.3 0.0 copy-start
  13.3 0.0 copy-start.2
  13.4 0.6 %collective-permute-start.6 = (f32[128,640]{1,0:T(8,128)S(1)}, f32[128,640]{1,0:T(8,128)S(1)}, u32[]{:S(2)}, u32[]{:S(2)}) collective-permute-start(f32[128,640]{1,0:T(8,128)S(1)} %get-tuple-element.37), channel_id=1, source_target_pairs={{0,16},{16,0},{1,17},{17,1},{2,18},{18,2},{3,19},{19,3},{4,20},{20... | collective-permute-start | bytes 983048 | tf_op jit(solution)/shard_map/ppermute | solution.py:756
  13.9 0.9 %collective-permute-done.2 = f32[88,128]{1,0:T(8,128)S(1)} collective-permute-done((f32[88,128]{1,0:T(8,128)S(1)}, f32[88,128]{1,0:T(8,128)S(1)}, u32[]{:S(2)}, u32[]{:S(2)}) %collective-permute-start.2) | collective-permute-done | bytes 45088 | tf_op jit(solution)/shard_map/ppermute | solution.py:746
  14.8 2.6 %collective-permute-start.3 = (f32[88,128]{1,0:T(8,128)S(1)}, f32[88,128]{1,0:T(8,128)S(1)}, u32[]{:S(2)}, u32[]{:S(2)}) collective-permute-start(f32[88,128]{1,0:T(8,128)S(1)} %add.14), channel_id=1, source_target_pairs={{0,8},{1,9},{2,10},{3,11},{4,12},{5,13},{6,14},{7,15},{8,0},{9,1},... | collective-permute-start | bytes 135176 | tf_op jit(solution)/shard_map/ppermute | solution.py:746
  17.4 0.0 copy-done
  17.4 0.0 copy-done.2
  17.5 0.8 %stream_kernel.1.stream_ref = f32[128,2048]{1,0:T(8,128)S(1)} custom-call(s32[6,128]{1,0:T(8,128)S(1)} %copy-done.2, s32[6,128]{1,0:T(8,128)S(1)} %copy-done, f32[128,2048]{1,0:T(8,128)S(1)} %get-tuple-element.23.dist_ref.value_ref), custom_call_target="tpu_custom_call" | custom-call | bytes 1054720 | tf_op jit(solution)/shard_map/stream_kernel/pallas_call | solution.py:713
  18.3 0.0 copy-start.3
  18.3 0.6 %copy-done.3 = f32[128]{0:T(128)S(1)} copy-done((f32[128]{0:T(128)S(1)}, f32[128]{0:T(128)}, u32[]{:S(2)}) %copy-start.3) | copy-done | bytes 536
  19.0 0.3 %wall_kernel.1 = (f32[128,2048]{1,0:T(8,128)S(1)}, f32[8,128]{1,0:T(8,128)S(1)}, bf16[256,128]{1,0:T(8,128)(2,1)S(1)}, f32[8,128]{1,0:T(8,128)S(1)}) custom-call(s32[1,2,64]{2,1,0:T(2,128)S(1)} %copy-done.1, f32[1,128]{1,0:T(1,128)S(1)} %bitcast.1, s32[6,128]{1,0:T(8,128)S(1)} %copy-done), custom_call_target="tpu_custom_call" | custom-call | bytes 4096 | tf_op jit(solution)/shard_map/wall_kernel/pallas_call | solution.py:713
  19.3 0.5 %collective-permute-done.3 = f32[88,128]{1,0:T(8,128)S(1)} collective-permute-done((f32[88,128]{1,0:T(8,128)S(1)}, f32[88,128]{1,0:T(8,128)S(1)}, u32[]{:S(2)}, u32[]{:S(2)}) %collective-permute-start.3) | collective-permute-done | bytes 45088 | tf_op jit(solution)/shard_map/ppermute | solution.py:746
  19.8 0.2 share_kernel.1.after_ref
  20.0 0.7 %collective-permute-start.5 = (f32[80,64]{1,0:T(8,128)S(1)}, f32[80,64]{1,0:T(8,128)S(1)}, u32[]{:S(2)}, u32[]{:S(2)}) collective-permute-start(f32[80,64]{1,0:T(8,128)S(1)} %share_kernel.1.after_ref), channel_id=1, source_target_pairs={{0,16},{16,0},{1,17},{17,1},{2,18},{18,2},{3,19},{19,3},{4,20},{20... | collective-permute-start | bytes 61448 | tf_op jit(solution)/shard_map/ppermute | solution.py:756
  20.7 1.4 %collective-permute-start.7 = (f32[128,384]{1,0:T(8,128)S(1)}, f32[128,384]{1,0:T(8,128)S(1)}, u32[]{:S(2)}, u32[]{:S(2)}) collective-permute-start(f32[128,384]{1,0:T(8,128)S(1)} %pass_kernel.1), channel_id=1, source_target_pairs={{0,16},{16,0},{1,17},{17,1},{2,18},{18,2},{3,19},{19,3},{4,20},{20... | collective-permute-start | bytes 589832 | tf_op jit(solution)/shard_map/ppermute | solution.py:756
  22.1 0.0 collective-permute-done.4.refs_0_
  22.1 2.6 %second_kernel.1 = (f32[128,2048]{1,0:T(8,128)S(1)}, f32[128,2048]{1,0:T(8,128)S(1)}, f32[128,1024]{1,0:T(8,128)S(1)}, f32[128,1024]{1,0:T(8,128)S(1)}, f32[128,...) custom-call(s32[1,2,64]{2,1,0:T(2,128)S(1)} %copy-done.1, s32[6,128]{1,0:T(8,128)S(1)} %copy-done.2, s32[6,128]{1,0:T(8,128)S(1)} %copy-done, ...), custom_call_target="tpu_custom_call" | custom-call | flops 1000000000 | bytes 3856896 | tf_op jit(solution)/shard_map/second_kernel/pallas_call | solution.py:713
  24.7 0.4 %collective-permute-done.5.refs_6_ = f32[80,64]{1,0:T(8,128)S(1)} collective-permute-done((f32[80,64]{1,0:T(8,128)S(1)}, f32[80,64]{1,0:T(8,128)S(1)}, u32[]{:S(2)}, u32[]{:S(2)}) %collective-permute-start.5) | collective-permute-done | bytes 20512 | tf_op jit(solution)/shard_map/ppermute | solution.py:756
  25.1 2.4 %third_kernel.1 = (f32[128,2048]{1,0:T(8,128)S(1)}, f32[128,1024]{1,0:T(8,128)S(1)}, f32[128,128]{1,0:T(8,128)S(1)}) custom-call(s32[1,2,64]{2,1,0:T(2,128)S(1)} %copy-done.1, s32[6,128]{1,0:T(8,128)S(1)} %copy-done.2, s32[6,128]{1,0:T(8,128)S(1)} %copy-done, f32[88,128]{1,0:T(8,128)S(1)} %add.15.sums_ref, f32[8,128]{1,0:T(8,128)S(1)} %get-tuple-element.24.back_ref, ...), custom_call_target="tpu_custom_call" | custom-call | flops 2000000000 | bytes 5319168 | tf_op jit(solution)/shard_map/third_kernel/pallas_call | solution.py:713
  27.5 0.0 collective-permute-done.6.refs_0_
  27.5 1.0 %collective-permute-done.7.refs_1_ = f32[128,384]{1,0:T(8,128)S(1)} collective-permute-done((f32[128,384]{1,0:T(8,128)S(1)}, f32[128,384]{1,0:T(8,128)S(1)}, u32[]{:S(2)}, u32[]{:S(2)}) %collective-permute-start.7) | collective-permute-done | bytes 196640 | tf_op jit(solution)/shard_map/ppermute | solution.py:756
  28.5 1.3 %last_kernel.1 = f32[128,2048]{1,0:T(8,128)} custom-call(bf16[256,128]{1,0:T(8,128)(2,1)S(1)} %get-tuple-element.22.side_ref, f32[128,2048]{1,0:T(8,128)S(1)} %get-tuple-element.34.part_ref, f32[128,1024]{1,0:T(8,128)S(1)} %get-tuple-element.35.plane_ref, f32[128,128]{1,0:T(8,128)S(1)} %get-tuple-element.36.open_ref, ...), custom_call_target="tpu_custom_call" | custom-call | bytes 2293760 | tf_op jit(solution)/shard_map/last_kernel/pallas_call | solution.py:713
  (5 shorter events, 0.0 us)
Async XLA Ops:
  1.4 20.7 %collective-permute-start.4 = (f32[128,1024]{1,0:T(8,128)S(1)}, f32[128,1024]{1,0:T(8,128)S(1)}, u32[]{:S(2)}, u32[]{:S(2)}) collective-permute-start(f32[128,1024]{1,0:T(8,128)S(1)} %get-tuple-element.26), channel_id=1, source_target_pairs={{0,16},{16,0},{1,17},{17,1},{2,18},{18,2},{3,19},{19,3},{4,20},{20... | collective-permute-start | bytes 1572872 | tf_op jit(solution)/shard_map/ppermute | solution.py:756
  5.3 1.3 %collective-permute-start = (f32[88,128]{1,0:T(8,128)S(1)}, f32[88,128]{1,0:T(8,128)S(1)}, u32[]{:S(2)}, u32[]{:S(2)}) collective-permute-start(f32[88,128]{1,0:T(8,128)S(1)} %sums_kernel.1), channel_id=1, source_target_pairs={{0,1},{1,0},{2,3},{3,2},{4,5},{5,4},{6,7},{7,6},{8,9},{9,8},{10,11... | collective-permute-start | bytes 135176 | tf_op jit(solution)/shard_map/ppermute | solution.py:746
  6.6 5.8 %copy-start.1 = (s32[1,2,64]{2,1,0:T(2,128)S(1)}, s32[1,2,64]{2,1,0:T(2,128)}, u32[]{:S(2)}) copy-start(s32[1,2,64]{2,1,0:T(2,128)} %rows_ref.1) | copy-start | bytes 1540
  6.6 4.1 %collective-permute-start.1 = (f32[88,128]{1,0:T(8,128)S(1)}, f32[88,128]{1,0:T(8,128)S(1)}, u32[]{:S(2)}, u32[]{:S(2)}) collective-permute-start(f32[88,128]{1,0:T(8,128)S(1)} %add.12), channel_id=1, source_target_pairs={{0,2},{1,3},{2,0},{3,1},{4,6},{5,7},{6,4},{7,5},{8,10},{9,11},{10,... | collective-permute-start | bytes 135176 | tf_op jit(solution)/shard_map/ppermute | solution.py:746
  10.7 4.1 %collective-permute-start.2 = (f32[88,128]{1,0:T(8,128)S(1)}, f32[88,128]{1,0:T(8,128)S(1)}, u32[]{:S(2)}, u32[]{:S(2)}) collective-permute-start(f32[88,128]{1,0:T(8,128)S(1)} %add.13), channel_id=1, source_target_pairs={{0,4},{1,5},{2,6},{3,7},{4,0},{5,1},{6,2},{7,3},{8,12},{9,13},{10,... | collective-permute-start | bytes 135176 | tf_op jit(solution)/shard_map/ppermute | solution.py:746
  13.3 4.1 %copy-start = (s32[6,128]{1,0:T(8,128)S(1)}, s32[6,128]{1,0:T(8,128)}, u32[]{:S(2)}) copy-start(s32[6,128]{1,0:T(8,128)} %mask_ref.7) | copy-start | bytes 9220
  13.3 4.1 %copy-start.2 = (s32[6,128]{1,0:T(8,128)S(1)}, s32[6,128]{1,0:T(8,128)}, u32[]{:S(2)}) copy-start(s32[6,128]{1,0:T(8,128)} %near_ref.5) | copy-start | bytes 9220
  13.4 14.1 %collective-permute-start.6 = (f32[128,640]{1,0:T(8,128)S(1)}, f32[128,640]{1,0:T(8,128)S(1)}, u32[]{:S(2)}, u32[]{:S(2)}) collective-permute-start(f32[128,640]{1,0:T(8,128)S(1)} %get-tuple-element.37), channel_id=1, source_target_pairs={{0,16},{16,0},{1,17},{17,1},{2,18},{18,2},{3,19},{19,3},{4,20},{20... | collective-permute-start | bytes 983048 | tf_op jit(solution)/shard_map/ppermute | solution.py:756
  14.8 5.0 %collective-permute-start.3 = (f32[88,128]{1,0:T(8,128)S(1)}, f32[88,128]{1,0:T(8,128)S(1)}, u32[]{:S(2)}, u32[]{:S(2)}) collective-permute-start(f32[88,128]{1,0:T(8,128)S(1)} %add.14), channel_id=1, source_target_pairs={{0,8},{1,9},{2,10},{3,11},{4,12},{5,13},{6,14},{7,15},{8,0},{9,1},... | collective-permute-start | bytes 135176 | tf_op jit(solution)/shard_map/ppermute | solution.py:746
  18.3 0.7 %copy-start.3 = (f32[128]{0:T(128)S(1)}, f32[128]{0:T(128)}, u32[]{:S(2)}) copy-start(f32[128]{0:T(128)} %param.6) | copy-start | bytes 1540
  20.0 5.1 %collective-permute-start.5 = (f32[80,64]{1,0:T(8,128)S(1)}, f32[80,64]{1,0:T(8,128)S(1)}, u32[]{:S(2)}, u32[]{:S(2)}) collective-permute-start(f32[80,64]{1,0:T(8,128)S(1)} %share_kernel.1.after_ref), channel_id=1, source_target_pairs={{0,16},{16,0},{1,17},{17,1},{2,18},{18,2},{3,19},{19,3},{4,20},{20... | collective-permute-start | bytes 61448 | tf_op jit(solution)/shard_map/ppermute | solution.py:756
  20.7 7.8 %collective-permute-start.7 = (f32[128,384]{1,0:T(8,128)S(1)}, f32[128,384]{1,0:T(8,128)S(1)}, u32[]{:S(2)}, u32[]{:S(2)}) collective-permute-start(f32[128,384]{1,0:T(8,128)S(1)} %pass_kernel.1), channel_id=1, source_target_pairs={{0,16},{16,0},{1,17},{17,1},{2,18},{18,2},{3,19},{19,3},{4,20},{20... | collective-permute-start | bytes 589832 | tf_op jit(solution)/shard_map/ppermute | solution.py:756

commit v10 on v8

--- a/solution.py
+++ b/solution.py
@@ -184,6 +184,16 @@
     return low, [(source + HALF, target) for source, target in low]
 
 
+def gathered(rows_ref, plane, group, value_ref, source, size):
+    below = lax.broadcasted_iota(jnp.int32, (ROWS, size), 0)
+    found = None
+    for at in range(ROWS):
+        row = value_ref[pl.ds(rows_ref[0, plane, group + at], 1), source : source + size]
+        row = jnp.broadcast_to(row, (ROWS, size))
+        found = row if found is None else jnp.where(below == at, row, found)
+    return found
+
+
 def move_rows(rows_ref, value_ref, send_ref, part):
     cells, width = value_ref.shape
     count = cells // 2
@@ -192,16 +202,13 @@
     piece = min(HALF, send_ref.shape[1])
     step = piece // COLUMN_TILE
 
-    def move(at, _):
-        for first, tiles, plane in ((0, high, 0), (count, low, 1)):
-            row = rows_ref[0, plane, at]
-            for source, target in tiles[::step]:
-                send_ref[pl.ds(first + at, 1), target - begin : target - begin + piece] = (
-                    value_ref[pl.ds(row, 1), source : source + piece]
+    for first, tiles, plane in ((0, high, 0), (count, low, 1)):
+        for source, target in tiles[::step]:
+            for group in range(0, count, ROWS):
+                rows = slice(first + group, first + group + ROWS)
+                send_ref[rows, target - begin : target - begin + piece] = gathered(
+                    rows_ref, plane, group, value_ref, source, piece
                 )
-        return 0
-
-    lax.fori_loop(0, count, move, 0, unroll=True)
 
 
 def wall_rows(temp_ref):
@@ -232,14 +239,10 @@
         side = at % 2
         source, target, first = at * HALF, at // 2 * HALF, (1 - side) * count
 
-        def move(at, _):
-            row = rows_ref[0, side, at]
-            send_ref[pl.ds(first + at, 1), target : target + HALF] = own_ref[
-                pl.ds(row, 1), source : source + HALF
-            ]
-            return 0
-
-        lax.fori_loop(0, count, move, 0, unroll=True)
+        for group in range(0, count, ROWS):
+            send_ref[first + group : first + group + ROWS, target : target + HALF] = gathered(
+                rows_ref, side, group, own_ref, source, HALF
+            )
 
 
 def far_plane_kernel(rows_ref, dist_ref, *send_refs):

time: 29.7 us -> 29.7 us (level)
  transfers between devices with their start and end apart: 8 -> 8, of which waited for: 5 -> 5; matrix products, arithmetic and copies ran while one was open for 0% -> 0% of each run, Pallas kernels for 30% -> 31%
where the time goes in v10:
time: 29.7 us; the launch traced here: 29.5 us
  starting transfers between devices  11.6 us (39%)
  Pallas kernels  11.5 us (39%)
  waiting for transfers between devices  5.61 us (19%)
  local copies, waits for them, and re-layouts  0.67 us (2%)
    pallas_call x15, Pallas kernels, call(): pl.pallas_call(kernel, out_shape=[jax.ShapeDtypeStruct(shape, dtype) for...  11.5 us
    ppermute x4, starting transfers between devices, total(): lax.ppermute(value, 'vel', [(i, i ^ step) for i in range(count)])  5.92 us
    ppermute x4, starting transfers between devices, exchange(): return [lax.ppermute(send, 'space', forward)]  5.69 us
    ppermute x4, waiting for transfers between devices, total(): lax.ppermute(value, 'vel', [(i, i ^ step) for i in range(count)])  5.2 us
    unnamed x8, local copies, waits for them, and re-layouts  0.67 us
  transfers between devices with their start and end apart: 8, of which 5 were waited for; matrix products, arithmetic and copies ran while one was open for 0% of the time, Pallas kernels for 31%

profile of v10, /device:TPU:0, one launch (start us, length us, event | category | flops | bytes accessed | tf_op | source)
XLA Modules:
  0.0 29.5 jit_solution(4746884265803812341)
XLA Ops:
  0.0 1.4 %near_plane_kernel.1 = (f32[128,2048]{1,0:T(8,128)S(1)}, f32[128,1024]{1,0:T(8,128)S(1)}) custom-call(s32[1,2,64]{2,1,0:T(2,128)} %rows_ref.1, f32[128,2048]{1,0:T(8,128)} %dist_ref.1), custom_call_target="tpu_custom_call" | custom-call | bytes 1049088 | tf_op jit(solution)/shard_map/near_plane_kernel/pallas_call | solution.py:681
  1.4 3.0 %collective-permute-start.4 = (f32[128,1024]{1,0:T(8,128)S(1)}, f32[128,1024]{1,0:T(8,128)S(1)}, u32[]{:S(2)}, u32[]{:S(2)}) collective-permute-start(f32[128,1024]{1,0:T(8,128)S(1)} %get-tuple-element.23), channel_id=1, source_target_pairs={{0,16},{16,0},{1,17},{17,1},{2,18},{18,2},{3,19},{19,3},{4,20},{20... | collective-permute-start | bytes 1572872 | tf_op jit(solution)/shard_map/ppermute | solution.py:713
  4.5 0.8 %sums_kernel.1 = f32[88,128]{1,0:T(8,128)S(1)} custom-call(f32[128,2048]{1,0:T(8,128)S(1)} %get-tuple-element.20.dist_ref.value_ref.own_ref), custom_call_target="tpu_custom_call" | custom-call | bytes 1048576 | tf_op jit(solution)/shard_map/sums_kernel/pallas_call | solution.py:681
  5.3 0.0 copy-start.2
  5.3 0.1 collective-permute-start
  5.4 1.2 %collective-permute-done = f32[88,128]{1,0:T(8,128)S(1)} collective-permute-done((f32[88,128]{1,0:T(8,128)S(1)}, f32[88,128]{1,0:T(8,128)S(1)}, u32[]{:S(2)}, u32[]{:S(2)}) %collective-permute-start) | collective-permute-done | bytes 45088 | tf_op jit(solution)/shard_map/ppermute | solution.py:703
  6.6 1.6 %collective-permute-start.1 = (f32[88,128]{1,0:T(8,128)S(1)}, f32[88,128]{1,0:T(8,128)S(1)}, u32[]{:S(2)}, u32[]{:S(2)}) collective-permute-start(f32[88,128]{1,0:T(8,128)S(1)} %add.12), channel_id=1, source_target_pairs={{0,2},{1,3},{2,0},{3,1},{4,6},{5,7},{6,4},{7,5},{8,10},{9,11},{10,... | collective-permute-start | bytes 135176 | tf_op jit(solution)/shard_map/ppermute | solution.py:703
  8.1 0.0 copy-done.2
  8.1 1.0 %far_plane_kernel.1 = (f32[128,512]{1,0:T(8,128)S(1)}, f32[128,512]{1,0:T(8,128)S(1)}) custom-call(s32[1,2,64]{2,1,0:T(2,128)S(1)} %copy-done.2, f32[128,2048]{1,0:T(8,128)S(1)} %get-tuple-element.20.dist_ref.value_ref.own_ref), custom_call_target="tpu_custom_call" | custom-call | bytes 1049088 | tf_op jit(solution)/shard_map/far_plane_kernel/pallas_call | solution.py:681
  9.1 0.6 %collective-permute-start.6 = (f32[128,512]{1,0:T(8,128)S(1)}, f32[128,512]{1,0:T(8,128)S(1)}, u32[]{:S(2)}, u32[]{:S(2)}) collective-permute-start(f32[128,512]{1,0:T(8,128)S(1)} %get-tuple-element.31), channel_id=1, source_target_pairs={{0,16},{16,0},{1,17},{17,1},{2,18},{18,2},{3,19},{19,3},{4,20},{20... | collective-permute-start | bytes 786440 | tf_op jit(solution)/shard_map/ppermute | solution.py:713
  9.7 1.0 %collective-permute-done.1 = f32[88,128]{1,0:T(8,128)S(1)} collective-permute-done((f32[88,128]{1,0:T(8,128)S(1)}, f32[88,128]{1,0:T(8,128)S(1)}, u32[]{:S(2)}, u32[]{:S(2)}) %collective-permute-start.1) | collective-permute-done | bytes 45088 | tf_op jit(solution)/shard_map/ppermute | solution.py:703
  10.7 0.0 copy-start
  10.7 0.0 copy-start.1
  10.7 1.6 %collective-permute-start.2 = (f32[88,128]{1,0:T(8,128)S(1)}, f32[88,128]{1,0:T(8,128)S(1)}, u32[]{:S(2)}, u32[]{:S(2)}) collective-permute-start(f32[88,128]{1,0:T(8,128)S(1)} %add.13), channel_id=1, source_target_pairs={{0,4},{1,5},{2,6},{3,7},{4,0},{5,1},{6,2},{7,3},{8,12},{9,13},{10,... | collective-permute-start | bytes 135176 | tf_op jit(solution)/shard_map/ppermute | solution.py:703
  12.4 2.5 %collective-permute-done.2 = f32[88,128]{1,0:T(8,128)S(1)} collective-permute-done((f32[88,128]{1,0:T(8,128)S(1)}, f32[88,128]{1,0:T(8,128)S(1)}, u32[]{:S(2)}, u32[]{:S(2)}) %collective-permute-start.2) | collective-permute-done | bytes 45088 | tf_op jit(solution)/shard_map/ppermute | solution.py:703
  14.8 2.7 %collective-permute-start.3 = (f32[88,128]{1,0:T(8,128)S(1)}, f32[88,128]{1,0:T(8,128)S(1)}, u32[]{:S(2)}, u32[]{:S(2)}) collective-permute-start(f32[88,128]{1,0:T(8,128)S(1)} %add.14), channel_id=1, source_target_pairs={{0,8},{1,9},{2,10},{3,11},{4,12},{5,13},{6,14},{7,15},{8,0},{9,1},... | collective-permute-start | bytes 135176 | tf_op jit(solution)/shard_map/ppermute | solution.py:703
  17.5 0.0 copy-done
  17.5 0.0 copy-done.1
  17.5 0.8 %stream_kernel.1.stream_ref._ = f32[128,2048]{1,0:T(8,128)S(1)} custom-call(s32[6,128]{1,0:T(8,128)S(1)} %copy-done, s32[6,128]{1,0:T(8,128)S(1)} %copy-done.1, f32[128,2048]{1,0:T(8,128)S(1)} %get-tuple-element.20.dist_ref.value_ref.own_ref), custom_call_target="tpu_custom_call" | custom-call | bytes 1054720 | tf_op jit(solution)/shard_map/stream_kernel/pallas_call | solution.py:681
  18.3 0.0 copy-start.3
  18.3 0.6 %copy-done.3 = f32[128]{0:T(128)S(1)} copy-done((f32[128]{0:T(128)S(1)}, f32[128]{0:T(128)}, u32[]{:S(2)}) %copy-start.3) | copy-done | bytes 536
  19.0 0.3 %wall_kernel.1 = (f32[128,2048]{1,0:T(8,128)S(1)}, f32[8,128]{1,0:T(8,128)S(1)}, bf16[256,128]{1,0:T(8,128)(2,1)S(1)}, f32[8,128]{1,0:T(8,128)S(1)}) custom-call(s32[1,2,64]{2,1,0:T(2,128)S(1)} %copy-done.2, f32[1,128]{1,0:T(1,128)S(1)} %bitcast.1, s32[6,128]{1,0:T(8,128)S(1)} %copy-done.1), custom_call_target="tpu_custom_call" | custom-call | bytes 4096 | tf_op jit(solution)/shard_map/wall_kernel/pallas_call | solution.py:681
  19.3 0.5 %collective-permute-done.3 = f32[88,128]{1,0:T(8,128)S(1)} collective-permute-done((f32[88,128]{1,0:T(8,128)S(1)}, f32[88,128]{1,0:T(8,128)S(1)}, u32[]{:S(2)}, u32[]{:S(2)}) %collective-permute-start.3) | collective-permute-done | bytes 45088 | tf_op jit(solution)/shard_map/ppermute | solution.py:703
  19.9 0.2 share_kernel.1.after_ref
  20.0 0.6 %collective-permute-start.5 = (f32[80,64]{1,0:T(8,128)S(1)}, f32[80,64]{1,0:T(8,128)S(1)}, u32[]{:S(2)}, u32[]{:S(2)}) collective-permute-start(f32[80,64]{1,0:T(8,128)S(1)} %share_kernel.1.after_ref), channel_id=1, source_target_pairs={{0,16},{16,0},{1,17},{17,1},{2,18},{18,2},{3,19},{19,3},{4,20},{20... | collective-permute-start | bytes 61448 | tf_op jit(solution)/shard_map/ppermute | solution.py:713
  20.6 1.5 %collective-permute-start.7 = (f32[128,512]{1,0:T(8,128)S(1)}, f32[128,512]{1,0:T(8,128)S(1)}, u32[]{:S(2)}, u32[]{:S(2)}) collective-permute-start(f32[128,512]{1,0:T(8,128)S(1)} %pass_kernel.1), channel_id=1, source_target_pairs={{0,16},{16,0},{1,17},{17,1},{2,18},{18,2},{3,19},{19,3},{4,20},{20... | collective-permute-start | bytes 786440 | tf_op jit(solution)/shard_map/ppermute | solution.py:713
  22.1 0.0 collective-permute-done.4.refs_0_
  22.1 1.0 %middle_kernel.1.middle_ref = f32[128,2048]{1,0:T(8,128)S(1)} custom-call(f32[88,128]{1,0:T(8,128)S(1)} %add.15.sums_ref, f32[8,128]{1,0:T(8,128)S(1)} %get-tuple-element.21.back_ref, bf16[256,128]{1,0:T(8,128)(2,1)S(1)} %get-tuple-element.19.side_ref, f32[128,2048]{1,0:T(8,128)S(1)} %get-tuple-element.20.dist_ref.value_ref.own_ref, ...), custom_call_target="tpu_custom_call" | custom-call | bytes 3850240 | tf_op jit(solution)/shard_map/middle_kernel/pallas_call | solution.py:681
  23.1 0.9 %stream_last_kernel.1._.part_ref = f32[128,2048]{1,0:T(8,128)S(1)} custom-call(s32[6,128]{1,0:T(8,128)S(1)} %copy-done, s32[6,128]{1,0:T(8,128)S(1)} %copy-done.1, f32[128,2048]{1,0:T(8,128)S(1)} %get-tuple-element.20.dist_ref.value_ref.own_ref, f32[128,2048]{1,0:T(8,128)S(1)} %middle_kernel.1.middle_ref), custom_call_target="tpu_custom_call" | custom-call | bytes 2103296 | tf_op jit(solution)/shard_map/stream_last_kernel/pallas_call | solution.py:681
  24.1 0.8 %halo_stream_kernel.1 = (f32[128,1024]{1,0:T(8,128)S(1)}, f32[128,1024]{1,0:T(8,128)S(1)}, f32[128,1024]{1,0:T(8,128)S(1)}, f32[128,1024]{1,0:T(8,128)S(1)}) custom-call(s32[1,2,64]{2,1,0:T(2,128)S(1)} %copy-done.2, s32[6,128]{1,0:T(8,128)S(1)} %copy-done, f32[128,1024]{1,0:T(8,128)S(1)} %collective-permute-done.4.refs_0_), custom_call_target="tpu_custom_call" | custom-call | bytes 527872 | tf_op jit(solution)/shard_map/halo_stream_kernel/pallas_call | solution.py:681
  24.9 0.0 collective-permute-done.5.refs_0_
  24.9 0.4 %advance_kernel.1.sums_ref = f32[16,128]{1,0:T(8,128)S(1)} custom-call(s32[1,2,64]{2,1,0:T(2,128)S(1)} %copy-done.2, s32[6,128]{1,0:T(8,128)S(1)} %copy-done, f32[128,2048]{1,0:T(8,128)S(1)} %stream_last_kernel.1._.part_ref, f32[128,1024]{1,0:T(8,128)S(1)} %get-tuple-element.24.__.base_ref, s32[6,128]{1,0:T(8,128)S(1)} %copy-done.1, ...), custom_call_target="tpu_custom_call" | custom-call | flops 1400000000 | bytes 1649152 | tf_op jit(solution)/shard_map/advance_kernel/pallas_call | solution.py:681
  25.3 0.9 %relax_kernel.1.part_ref = f32[128,2048]{1,0:T(8,128)S(1)} custom-call(f32[16,128]{1,0:T(8,128)S(1)} %advance_kernel.1.sums_ref, f32[8,128]{1,0:T(8,128)S(1)} %get-tuple-element.21.back_ref, f32[128,2048]{1,0:T(8,128)S(1)} %middle_kernel.1.middle_ref, f32[128,2048]{1,0:T(8,128)S(1)} %stream_last_kernel.1._.part_ref, f32[128,2048]{1,0:T(8,128)S(1)} %get-tuple-element.22.shape_ref), custom_call_target="tpu_custom_call" | custom-call | bytes 3158016 | tf_op jit(solution)/shard_map/relax_kernel/pallas_call | solution.py:681
  26.2 0.9 %halo_relax_kernel.1 = (f32[128,1024]{1,0:T(8,128)S(1)}, f32[128,128]{1,0:T(8,128)S(1)}) custom-call(f32[128,1024]{1,0:T(8,128)S(1)} %get-tuple-element.24.__.base_ref, f32[128,1024]{1,0:T(8,128)S(1)} %get-tuple-element.26.from_y_ref, f32[128,1024]{1,0:T(8,128)S(1)} %get-tuple-element.27.from_z_ref, f32[128,1024]{1,0:T(8,128)S(1)} %get-tuple-element.28.values_ref, ...), custom_call_target="tpu_custom_call" | custom-call | bytes 2117632 | tf_op jit(solution)/shard_map/halo_relax_kernel/pallas_call | solution.py:681
  27.1 0.0 collective-permute-done.6.refs_0_
  27.1 1.0 %last_kernel_0.1.refs_0_ = f32[128,2048]{1,0:T(8,128)} custom-call(bf16[256,128]{1,0:T(8,128)(2,1)S(1)} %get-tuple-element.19.side_ref, f32[128,2048]{1,0:T(8,128)S(1)} %relax_kernel.1.part_ref, f32[128,1024]{1,0:T(8,128)S(1)} %get-tuple-element.29.plane_ref, f32[128,128]{1,0:T(8,128)S(1)} %get-tuple-element.30.open_ref, ...), custom_call_target="tpu_custom_call" | custom-call | flops 4000000000 | bytes 2031616 | tf_op jit(solution)/shard_map/last_kernel_0/pallas_call | solution.py:681
  28.1 0.4 %collective-permute-done.7.refs_1_ = f32[128,512]{1,0:T(8,128)S(1)} collective-permute-done((f32[128,512]{1,0:T(8,128)S(1)}, f32[128,512]{1,0:T(8,128)S(1)}, u32[]{:S(2)}, u32[]{:S(2)}) %collective-permute-start.7) | collective-permute-done | bytes 262176 | tf_op jit(solution)/shard_map/ppermute | solution.py:713
  28.5 1.0 %last_kernel_1.1 = f32[128,2048]{1,0:T(8,128)} custom-call(bf16[256,128]{1,0:T(8,128)(2,1)S(1)} %get-tuple-element.19.side_ref, f32[128,2048]{1,0:T(8,128)S(1)} %relax_kernel.1.part_ref, f32[128,1024]{1,0:T(8,128)S(1)} %get-tuple-element.29.plane_ref, f32[128,128]{1,0:T(8,128)S(1)} %get-tuple-element.30.open_ref, ...), custom_call_target="tpu_custom_call", output_to_operand_aliasing={{}: (4, {})} | custom-call | bytes 3080192 | tf_op jit(solution)/shard_map/last_kernel_1/pallas_call | solution.py:681
  (5 shorter events, 0.0 us)
Async XLA Ops:
  1.4 20.7 %collective-permute-start.4 = (f32[128,1024]{1,0:T(8,128)S(1)}, f32[128,1024]{1,0:T(8,128)S(1)}, u32[]{:S(2)}, u32[]{:S(2)}) collective-permute-start(f32[128,1024]{1,0:T(8,128)S(1)} %get-tuple-element.23), channel_id=1, source_target_pairs={{0,16},{16,0},{1,17},{17,1},{2,18},{18,2},{3,19},{19,3},{4,20},{20... | collective-permute-start | bytes 1572872 | tf_op jit(solution)/shard_map/ppermute | solution.py:713
  5.3 2.9 %copy-start.2 = (s32[1,2,64]{2,1,0:T(2,128)S(1)}, s32[1,2,64]{2,1,0:T(2,128)}, u32[]{:S(2)}) copy-start(s32[1,2,64]{2,1,0:T(2,128)} %rows_ref.1) | copy-start | bytes 1540
  5.3 1.3 %collective-permute-start = (f32[88,128]{1,0:T(8,128)S(1)}, f32[88,128]{1,0:T(8,128)S(1)}, u32[]{:S(2)}, u32[]{:S(2)}) collective-permute-start(f32[88,128]{1,0:T(8,128)S(1)} %sums_kernel.1), channel_id=1, source_target_pairs={{0,1},{1,0},{2,3},{3,2},{4,5},{5,4},{6,7},{7,6},{8,9},{9,8},{10,11... | collective-permute-start | bytes 135176 | tf_op jit(solution)/shard_map/ppermute | solution.py:703
  6.6 4.1 %collective-permute-start.1 = (f32[88,128]{1,0:T(8,128)S(1)}, f32[88,128]{1,0:T(8,128)S(1)}, u32[]{:S(2)}, u32[]{:S(2)}) collective-permute-start(f32[88,128]{1,0:T(8,128)S(1)} %add.12), channel_id=1, source_target_pairs={{0,2},{1,3},{2,0},{3,1},{4,6},{5,7},{6,4},{7,5},{8,10},{9,11},{10,... | collective-permute-start | bytes 135176 | tf_op jit(solution)/shard_map/ppermute | solution.py:703
  9.1 17.9 %collective-permute-start.6 = (f32[128,512]{1,0:T(8,128)S(1)}, f32[128,512]{1,0:T(8,128)S(1)}, u32[]{:S(2)}, u32[]{:S(2)}) collective-permute-start(f32[128,512]{1,0:T(8,128)S(1)} %get-tuple-element.31), channel_id=1, source_target_pairs={{0,16},{16,0},{1,17},{17,1},{2,18},{18,2},{3,19},{19,3},{4,20},{20... | collective-permute-start | bytes 786440 | tf_op jit(solution)/shard_map/ppermute | solution.py:713
  10.7 6.8 %copy-start = (s32[6,128]{1,0:T(8,128)S(1)}, s32[6,128]{1,0:T(8,128)}, u32[]{:S(2)}) copy-start(s32[6,128]{1,0:T(8,128)} %near_ref.7) | copy-start | bytes 9220
  10.7 6.8 %copy-start.1 = (s32[6,128]{1,0:T(8,128)S(1)}, s32[6,128]{1,0:T(8,128)}, u32[]{:S(2)}) copy-start(s32[6,128]{1,0:T(8,128)} %mask_ref.7) | copy-start | bytes 9220
  10.7 4.1 %collective-permute-start.2 = (f32[88,128]{1,0:T(8,128)S(1)}, f32[88,128]{1,0:T(8,128)S(1)}, u32[]{:S(2)}, u32[]{:S(2)}) collective-permute-start(f32[88,128]{1,0:T(8,128)S(1)} %add.13), channel_id=1, source_target_pairs={{0,4},{1,5},{2,6},{3,7},{4,0},{5,1},{6,2},{7,3},{8,12},{9,13},{10,... | collective-permute-start | bytes 135176 | tf_op jit(solution)/shard_map/ppermute | solution.py:703
  14.8 5.0 %collective-permute-start.3 = (f32[88,128]{1,0:T(8,128)S(1)}, f32[88,128]{1,0:T(8,128)S(1)}, u32[]{:S(2)}, u32[]{:S(2)}) collective-permute-start(f32[88,128]{1,0:T(8,128)S(1)} %add.14), channel_id=1, source_target_pairs={{0,8},{1,9},{2,10},{3,11},{4,12},{5,13},{6,14},{7,15},{8,0},{9,1},... | collective-permute-start | bytes 135176 | tf_op jit(solution)/shard_map/ppermute | solution.py:703
  18.3 0.7 %copy-start.3 = (f32[128]{0:T(128)S(1)}, f32[128]{0:T(128)}, u32[]{:S(2)}) copy-start(f32[128]{0:T(128)} %param.6) | copy-start | bytes 1540
  20.0 4.9 %collective-permute-start.5 = (f32[80,64]{1,0:T(8,128)S(1)}, f32[80,64]{1,0:T(8,128)S(1)}, u32[]{:S(2)}, u32[]{:S(2)}) collective-permute-start(f32[80,64]{1,0:T(8,128)S(1)} %share_kernel.1.after_ref), channel_id=1, source_target_pairs={{0,16},{16,0},{1,17},{17,1},{2,18},{18,2},{3,19},{19,3},{4,20},{20... | collective-permute-start | bytes 61448 | tf_op jit(solution)/shard_map/ppermute | solution.py:713
  20.6 7.9 %collective-permute-start.7 = (f32[128,512]{1,0:T(8,128)S(1)}, f32[128,512]{1,0:T(8,128)S(1)}, u32[]{:S(2)}, u32[]{:S(2)}) collective-permute-start(f32[128,512]{1,0:T(8,128)S(1)} %pass_kernel.1), channel_id=1, source_target_pairs={{0,16},{16,0},{1,17},{17,1},{2,18},{18,2},{3,19},{19,3},{4,20},{20... | collective-permute-start | bytes 786440 | tf_op jit(solution)/shard_map/ppermute | solution.py:713
